TPU v7x, 32 devices: a whole 2x2x4 slice. The times are simulated.
32 devices in a mesh: dp: 8 (over z, x), mp: 4 (over y, core).
Axes of the slice: x: 2, y: 2, z: 4, core: 2. Of those that a mesh axis runs over, the one named last changes fastest.
Arguments:
- tokens: bfloat16 [8192, 8192], P('dp', 'mp'), may hold values from -6 to 6
- value_weight: bfloat16 [8192, 1024], P('mp'), may hold values from -0.0625 to 0.0625
- adapter_down_panels: bfloat16 [24, 64, 8192], P('dp', None, 'mp'), may hold values from -0.0625 to 0.0625
- adapter_up_panels: bfloat16 [24, 64, 1024], P('dp', None, 'mp'), may hold values from -0.75 to 0.75
- cotangent: bfloat16 [8192, 1024], P('dp', 'mp'), may hold values from -6 to 6
- block_list_entry: int32 [256], P('dp'), may hold values from 0 to 7, as said below
- device_tenant_list: int32 [64], P('dp'), may hold values from 0 to 23, as said below
- tenant_location_map: int32 [24], replicated, may hold values from 0 to 23, as said below
Outputs:
- values: bfloat16 [8192, 1024], P('dp', 'mp')
- token_gradient: bfloat16 [8192, 8192], P('dp', 'mp')
- grad_a: bfloat16 [24, 64, 8192], P('dp', None, 'mp')
- grad_b: bfloat16 [24, 64, 1024], P('dp', None, 'mp')
Inputs may be any that keep to these rules, and one draw needn't show every extreme that they name: `device_tenant_list`: each entry names a tenant; no tenant stands twice in one list. Of one device's 8 entries, at most 2 name tenants whose storage location tenant_location_map[t] lies on one dp index (tenant_location_map[t] // 3), and every device's list has 2 entries on some one dp index. A permutation: tenant t's panels are row tenant_location_map[t] of adapter_down_panels and adapter_up_panels. `block_list_entry`: every entry of a device's tenant list is named by at least one of that device's row blocks.
All inputs are finite; a program needn't handle non-finite values.
Results may differ from a plain program's by a relative error of at most 0.0057.
Values may be sent and summed in bfloat16 or wider, within the bound.
No kernel may reach another device: no remote copies, remote signals or barrier semaphores. Data moves between devices by JAX's collectives and lax.ppermute only.
A program may use at most 128 MiB of HBM per device.

v0:
```python
import jax
import jax.numpy as jnp
from jax import lax
from jax.sharding import PartitionSpec as P

MOST = 2


def compare_table(left, right):
    return left[:, None] == right[None, :]


def shards(
    tokens,
    value_weight,
    adapter_down_panels,
    adapter_up_panels,
    cotangent,
    block_list_entry,
    device_tenant_list,
    tenant_location_map,
):
    rows, width_loc = tokens.shape
    stored_panels, adapter_rank_size, ignored_result = adapter_down_panels.shape
    output_location = adapter_up_panels.shape[2]
    blocks = block_list_entry.shape[0]
    block_rows = rows // blocks
    listed = device_tenant_list.shape[0]
    tenants = tenant_location_map.shape[0]
    capacity = lax.axis_size("dp") * MOST
    slot_ids = jnp.arange(listed, dtype=jnp.int32)
    tenant_ids = jnp.arange(tenants, dtype=jnp.int32)
    storage_location = jnp.sum(
        jnp.where(compare_table(device_tenant_list, tenant_ids), tenant_location_map[None, :], 0),
        axis=1,
    )
    holder = storage_location // stored_panels
    local_row = storage_location % stored_panels
    earlier = slot_ids[:, None] > slot_ids[None, :]
    rank_at = jnp.sum(jnp.where(compare_table(holder, holder) & earlier, 1, 0), axis=1).astype(
        jnp.int32
    )
    position = holder * MOST + rank_at
    canonical = jnp.min(
        jnp.where(compare_table(device_tenant_list, device_tenant_list), slot_ids[None, :], listed),
        axis=1,
    )
    block_canon = jnp.sum(
        jnp.where(compare_table(block_list_entry, slot_ids), canonical[None, :], 0), axis=1
    )
    requests = jnp.zeros((capacity,), jnp.int32).at[position].set(local_row + 1)
    incoming = lax.all_to_all(requests, "dp", split_axis=0, concat_axis=0, tiled=True)
    serve_adapters = compare_table(
        incoming, jnp.arange(1, stored_panels + 1, dtype=jnp.int32)
    ).astype(jnp.bfloat16)
    returned_down_panel = jnp.einsum(
        "vj,jiz->viz", serve_adapters, adapter_down_panels, preferred_element_type=jnp.float32
    ).astype(jnp.bfloat16)
    returned_up_panel = jnp.einsum(
        "wu,une->wne", serve_adapters, adapter_up_panels, preferred_element_type=jnp.float32
    ).astype(jnp.bfloat16)
    got_a, got_b = (
        lax.all_to_all(returned_down_panel, "dp", split_axis=0, concat_axis=0, tiled=True),
        lax.all_to_all(returned_up_panel, "dp", split_axis=0, concat_axis=0, tiled=True),
    )
    slot_a = got_a[position]
    slot_b = got_b[position]
    w_cols = value_weight
    base_flipped_weight = lax.psum_scatter(
        lax.dot_general(
            w_cols, tokens, (((0,), (1,)), ((), ())), preferred_element_type=jnp.float32
        ),
        "mp",
        scatter_dimension=0,
        tiled=True,
    )
    token_blocks = tokens.reshape(blocks, block_rows, width_loc)
    cot_blocks = cotangent.reshape(blocks, block_rows, output_location)
    block_down_panel = slot_a[block_list_entry]
    block_up_panel = slot_b[block_list_entry]
    down_part = jnp.einsum(
        "bnd,brd->bnr", token_blocks, block_down_panel, preferred_element_type=jnp.float32
    )
    down_low = lax.psum(down_part, "mp").astype(jnp.bfloat16)
    adapter_output = jnp.einsum(
        "afq,aqy->afy", down_low, block_up_panel, preferred_element_type=jnp.float32
    ).reshape(rows, output_location)
    values = (base_flipped_weight.T + adapter_output).astype(jnp.bfloat16)
    up_part = jnp.einsum(
        "bnc,brc->bnr", cot_blocks, block_up_panel, preferred_element_type=jnp.float32
    )
    up_grad = lax.psum(up_part, "mp").astype(jnp.bfloat16)
    w_cols = value_weight
    base_backward_pass = lax.dot_general(
        lax.all_gather(cotangent, "mp", axis=1, tiled=True),
        w_cols,
        (((1,), (1,)), ((), ())),
        preferred_element_type=jnp.float32,
    )
    adapter_backward_pass = jnp.einsum(
        "swq,sqj->swj", up_grad, block_down_panel, preferred_element_type=jnp.float32
    ).reshape(rows, width_loc)
    token_gradient = (base_backward_pass + adapter_backward_pass).astype(jnp.bfloat16)
    block_grad_a = jnp.einsum(
        "bnr,bnd->brd", up_grad, token_blocks, preferred_element_type=jnp.float32
    )
    block_grad_b = jnp.einsum(
        "bnr,bnc->brc", down_low, cot_blocks, preferred_element_type=jnp.float32
    )
    gather_slots = compare_table(block_canon, slot_ids).astype(jnp.float32)
    share_a = jnp.einsum(
        "bs,brd->srd", gather_slots, block_grad_a, precision=lax.Precision.HIGHEST
    ).astype(jnp.bfloat16)
    share_b = jnp.einsum(
        "bs,brc->src", gather_slots, block_grad_b, precision=lax.Precision.HIGHEST
    ).astype(jnp.bfloat16)
    send_a = (
        jnp.zeros((capacity, adapter_rank_size, width_loc), jnp.bfloat16).at[position].set(share_a)
    )
    send_b = (
        jnp.zeros((capacity, adapter_rank_size, output_location), jnp.bfloat16)
        .at[position]
        .set(share_b)
    )
    back_a, back_b = (
        lax.all_to_all(send_a, "dp", split_axis=0, concat_axis=0, tiled=True),
        lax.all_to_all(send_b, "dp", split_axis=0, concat_axis=0, tiled=True),
    )
    grad_a = jnp.einsum(
        "qk,qrd->krd", serve_adapters, back_a, preferred_element_type=jnp.float32
    ).astype(jnp.bfloat16)
    grad_b = jnp.einsum(
        "qk,qrc->krc", serve_adapters, back_b, preferred_element_type=jnp.float32
    ).astype(jnp.bfloat16)
    return (values, token_gradient, grad_a, grad_b)


def solution(mesh):
    in_specs = (
        P("dp", "mp"),
        P("mp", None),
        P("dp", None, "mp"),
        P("dp", None, "mp"),
        P("dp", "mp"),
        P("dp"),
        P("dp"),
        P(),
    )
    out_specs = (P("dp", "mp"), P("dp", "mp"), P("dp", None, "mp"), P("dp", None, "mp"))
    return jax.shard_map(shards, mesh=mesh, in_specs=in_specs, out_specs=out_specs, check_vma=False)
```

profile of v0, /device:TPU:0, one launch (start us, length us, event | category | flops | bytes accessed | tf_op | source)
XLA Modules:
  0.0 331.4 jit_solution(15694684499845150932)
XLA Ops:
  9.6 7.3 %all-to-all-start = ((s32[8,2,1]{1,2,0:T(1,128)}), s32[8,2,1]{1,2,0:T(1,128)S(1)}, u32[]{:S(2)}, u32[]{:S(2)}) async-start(s32[8,2,1]{1,2,0:T(1,128)} %bitcast.5), calls=%async_computation.1 | async-start | bytes 8192 | tf_op jit(solution)/shard_map/all_to_all | solution.py:52
  16.9 6.4 %all-to-all-done = s32[8,2,1]{1,2,0:T(1,128)S(1)} async-done(((s32[8,2,1]{1,2,0:T(1,128)}), s32[8,2,1]{1,2,0:T(1,128)S(1)}, u32[]{:S(2)}, u32[]{:S(2)}) %all-to-all-start) | async-done | bytes 96 | tf_op jit(solution)/shard_map/all_to_all | solution.py:52
  26.8 3.5 %all-to-all-start.2 = ((bf16[16,64,256]{2,1,0:T(8,128)(2,1)}), bf16[16,64,256]{2,1,0:T(8,128)(2,1)S(1)}, u32[]{:S(2)}, u32[]{:S(2)}) async-start(bf16[16,64,256]{2,1,0:T(8,128)(2,1)} %copy.51), calls=%async_computation.3 | async-start | bytes 1048576 | tf_op jit(solution)/shard_map/all_to_all | solution.py:64
  32.1 4.3 %copy.49 = bf16[16,64,2048]{2,1,0:T(8,128)(2,1)} copy(bf16[16,64,2048]{2,0,1:T(8,128)(2,1)S(1)} %convolution_convert_fusion) | data formatting | bytes 8388608 | tf_op jit(solution)/shard_map/convert_element_type | solution.py:58
  36.4 7.2 %all-to-all-done.2 = bf16[16,64,256]{2,1,0:T(8,128)(2,1)S(1)} async-done(((bf16[16,64,256]{2,1,0:T(8,128)(2,1)}), bf16[16,64,256]{2,1,0:T(8,128)(2,1)S(1)}, u32[]{:S(2)}, u32[]{:S(2)}) %all-to-all-start.2) | async-done | bytes 524320 | tf_op jit(solution)/shard_map/all_to_all | solution.py:64
  43.6 4.5 %all-to-all-start.1 = ((bf16[16,64,2048]{2,1,0:T(8,128)(2,1)}), bf16[16,64,2048]{2,1,0:T(8,128)(2,1)}, u32[]{:S(2)}, u32[]{:S(2)}) async-start(bf16[16,64,2048]{2,1,0:T(8,128)(2,1)} %copy.49), calls=%async_computation.2 | async-start | bytes 8388608 | tf_op jit(solution)/shard_map/all_to_all | solution.py:63
  49.1 9.9 %fusion.56 = f32[1024,1024]{1,0:T(8,128)} fusion(bf16[2048,1024]{1,0:T(8,128)(2,1)} %param.9, bf16[1024,2048]{1,0:T(8,128)(2,1)} %param.8), kind=kOutput, calls=%fused_computation.80 | convolution fusion | flops 4294967296 | bytes 12582912 | tf_op jit(solution)/shard_map/dot_general | solution.py:70
  62.2 77.6 %all-to-all-done.1 = bf16[16,64,2048]{2,1,0:T(8,128)(2,1)} async-done(((bf16[16,64,2048]{2,1,0:T(8,128)(2,1)}), bf16[16,64,2048]{2,1,0:T(8,128)(2,1)}, u32[]{:S(2)}, u32[]{:S(2)}) %all-to-all-start.1) | async-done | bytes 4194336 | tf_op jit(solution)/shard_map/all_to_all | solution.py:63
  139.8 2.9 gather_fusion
  142.7 5.0 %gather_fusion.1 = bf16[32,64,2048]{2,1,0:T(8,128)(2,1)} fusion(bf16[8,64,2048]{2,1,0:T(8,128)(2,1)S(1)} %gather_fusion, s32[1024]{0:T(1024)S(1)} %pad_clamp_fusion), kind=kCustom, calls=%fused_computation.1 | custom fusion | bytes 16777344 | tf_op jit(solution)/shard_map/gather | solution.py:79
  147.7 6.9 %convolution_bitcast_fusion.1 = f32[32,32,64]{2,1,0:T(8,128)S(1)} fusion(bf16[32,64,2048]{2,1,0:T(8,128)(2,1)} %gather_fusion.1, bf16[32,32,2048]{2,1,0:T(8,128)(2,1)} %bitcast.67), kind=kOutput, calls=%fused_computation.20 | convolution fusion | flops 268435456 | bytes 12845056 | tf_op jit(solution)/shard_map/bnd,brd->bnr/dot_general | solution.py:81
  154.5 25.3 %all-reduce.2 = (bf16[32,32,64]{2,1,0:T(8,128)(2,1)S(1)}, bf16[32,32,64]{2,1,0:T(8,128)(2,1)S(1)}) all-reduce(f32[32,32,64]{2,1,0:T(8,128)S(1)} %convolution_bitcast_fusion.1, f32[32,32,64]{2,1,0:T(8,128)S(1)} %convolution_bitcast_fusion), channel_id=1, replica_groups=mesh['dp'=8,'mp'=4] {'mp'}, use_global_device_ids=true, to_apply=%region_4.5 | all-reduce | flops 131072 | bytes 786432 | tf_op jit(solution)/shard_map/psum | solution.py:84
  180.3 2.0 fusion.13
  183.2 2.2 scatter_fusion.1
  185.4 5.3 %all-to-all-start.4 = ((bf16[16,64,256]{2,1,0:T(8,128)(2,1)}), bf16[16,64,256]{2,1,0:T(8,128)(2,1)S(1)}, u32[]{:S(2)}, u32[]{:S(2)}) async-start(bf16[16,64,256]{2,1,0:T(8,128)(2,1)} %scatter_fusion.1), calls=%async_computation.5 | async-start | bytes 1048576 | tf_op jit(solution)/shard_map/all_to_all | solution.py:127
  190.7 4.6 %fusion.57 = f32[32,64,2048]{2,1,0:T(8,128)S(1)} fusion(bf16[32,32,64]{2,1,0:T(8,128)(2,1)S(1)} %get-tuple-element.21, bf16[32,32,2048]{2,1,0:T(8,128)(2,1)} %bitcast.68), kind=kOutput, calls=%fused_computation.81 | convolution fusion | flops 268435456 | bytes 21102592 | tf_op jit(solution)/shard_map/bnr,bnd->brd/dot_general | solution.py:104
  195.2 12.2 %fusion.5 = bf16[8,64,2048]{2,0,1:T(8,128)(2,1)S(1)} fusion(f32[32,64,2048]{2,1,0:T(8,128)S(1)} %fusion.57, s32[32]{0:T(128)S(1)} %select_reduce_fusion), kind=kOutput, calls=%fused_computation.14 | convolution fusion | flops 403702016 | bytes 18874496 | tf_op jit(solution)/shard_map/bs,brd->srd/dot_general | solution.py:111
  208.6 2.5 broadcast_in_dim.53
  211.1 5.1 %scatter_fusion = bf16[16,64,2048]{2,1,0:T(8,128)(2,1)} fusion(bf16[16,64,2048]{2,1,0:T(8,128)(2,1)} %broadcast_in_dim.53, s32[8]{0:T(128)S(1)} %fusion.53, bf16[8,64,2048]{2,1,0:T(8,128)(2,1)S(1)} %copy.54), kind=kCustom, calls=%fused_computation.5 | custom fusion | bytes 6291488 | tf_op jit(solution)/shard_map/scatter | solution.py:118
  216.2 6.4 %all-to-all-start.3 = ((bf16[16,64,2048]{2,1,0:T(8,128)(2,1)}), bf16[16,64,2048]{2,1,0:T(8,128)(2,1)}, u32[]{:S(2)}, u32[]{:S(2)}) async-start(bf16[16,64,2048]{2,1,0:T(8,128)(2,1)} %scatter_fusion), calls=%async_computation.4 | async-start | bytes 8388608 | tf_op jit(solution)/shard_map/all_to_all | solution.py:126
  223.2 7.8 %fusion.58 = f32[32,32,2048]{2,1,0:T(8,128)} fusion(bf16[32,32,64]{2,1,0:T(8,128)(2,1)S(1)} %get-tuple-element.21, bf16[32,64,2048]{2,1,0:T(8,128)(2,1)} %gather_fusion.1), kind=kOutput, calls=%fused_computation.82 | convolution fusion | flops 268435456 | bytes 16908288 | tf_op jit(solution)/shard_map/swq,sqj->swj/dot_general | solution.py:100
  231.1 11.8 %fusion.2 = bf16[1024,2048]{1,0:T(8,128)(2,1)} fusion(f32[32,32,2048]{2,1,0:T(8,128)} %fusion.58, bf16[1024,1024]{1,0:T(8,128)(2,1)} %all-gather.2.cloned.1.call-done, bf16[2048,1024]{1,0:T(8,128)(2,1)} %param.9), kind=kOutput, calls=%fused_computation.10 | convolution fusion | flops 4299161600 | bytes 18874368 | tf_op jit(solution)/shard_map/dot_general | solution.py:94
  246.4 69.4 %all-to-all-done.3 = bf16[16,64,2048]{2,1,0:T(8,128)(2,1)} async-done(((bf16[16,64,2048]{2,1,0:T(8,128)(2,1)}), bf16[16,64,2048]{2,1,0:T(8,128)(2,1)}, u32[]{:S(2)}, u32[]{:S(2)}) %all-to-all-start.3) | async-done | bytes 4194336 | tf_op jit(solution)/shard_map/all_to_all | solution.py:126
  315.8 6.8 %fusion.8 = bf16[3,64,2048]{2,0,1:T(4,128)(2,1)S(1)} fusion(bf16[16,64,2048]{2,1,0:T(8,128)(2,1)} %all-to-all-done.3, s32[16]{0:T(128)S(1)} %eq.88, s32[3]{0:T(128)S(1)} %iota_add_fusion), kind=kOutput, calls=%fused_computation.15 | convolution fusion | flops 12976176 | bytes 4980812 | tf_op jit(solution)/shard_map/qk,qrd->krd/dot_general | solution.py:129
  (57 shorter events, 20.0 us)
Async XLA Ops:
  7.2 23.2 %copy-start = (bf16[3,64,2048]{2,1,0:T(8,128)(2,1)S(1)}, bf16[3,64,2048]{2,1,0:T(8,128)(2,1)}, u32[]{:S(2)}) copy-start(bf16[3,64,2048]{2,1,0:T(8,128)(2,1)} %param.10) | copy-start | bytes 2359300
  9.6 13.6 %all-to-all-start = ((s32[8,2,1]{1,2,0:T(1,128)}), s32[8,2,1]{1,2,0:T(1,128)S(1)}, u32[]{:S(2)}, u32[]{:S(2)}) async-start(s32[8,2,1]{1,2,0:T(1,128)} %bitcast.5), calls=%async_computation.1 | async-start | bytes 8192 | tf_op jit(solution)/shard_map/all_to_all | solution.py:52
  26.8 16.8 %all-to-all-start.2 = ((bf16[16,64,256]{2,1,0:T(8,128)(2,1)}), bf16[16,64,256]{2,1,0:T(8,128)(2,1)S(1)}, u32[]{:S(2)}, u32[]{:S(2)}) async-start(bf16[16,64,256]{2,1,0:T(8,128)(2,1)} %copy.51), calls=%async_computation.3 | async-start | bytes 1048576 | tf_op jit(solution)/shard_map/all_to_all | solution.py:64
  43.6 96.3 %all-to-all-start.1 = ((bf16[16,64,2048]{2,1,0:T(8,128)(2,1)}), bf16[16,64,2048]{2,1,0:T(8,128)(2,1)}, u32[]{:S(2)}, u32[]{:S(2)}) async-start(bf16[16,64,2048]{2,1,0:T(8,128)(2,1)} %copy.49), calls=%async_computation.2 | async-start | bytes 8388608 | tf_op jit(solution)/shard_map/all_to_all | solution.py:63
  48.1 183.0 %all-gather.2.cloned.1.call-start = ((), (), s32[]{:S(2)}) async-start(), calls=%async_computation.7 | async-start | bytes 2621440 | tf_op jit(solution)/shard_map/all_gather | solution.py:95
  48.9 195.1 %reduce-scatter.2.cloned.1.call-start = ((), (), s32[]{:S(2)}) async-start(), calls=%async_computation.6 | async-start | bytes 5242880 | tf_op jit(solution)/shard_map/reduce_scatter | solution.py:69
  59.0 0.7 copy-start.8
  59.0 0.7 copy-start.7
  59.0 2.2 copy-start.4
  61.2 1.1 copy-start.2
  179.8 15.4 %copy-start.5 = (bf16[32,32,64]{2,1,0:T(8,128)(2,1)}, bf16[32,32,64]{2,1,0:T(8,128)(2,1)S(1)}, u32[]{:S(2)}) copy-start(bf16[32,32,64]{2,1,0:T(8,128)(2,1)S(1)} %get-tuple-element.20) | copy-start | bytes 393220
  185.4 30.8 %all-to-all-start.4 = ((bf16[16,64,256]{2,1,0:T(8,128)(2,1)}), bf16[16,64,256]{2,1,0:T(8,128)(2,1)S(1)}, u32[]{:S(2)}, u32[]{:S(2)}) async-start(bf16[16,64,256]{2,1,0:T(8,128)(2,1)} %scatter_fusion.1), calls=%async_computation.5 | async-start | bytes 1048576 | tf_op jit(solution)/shard_map/all_to_all | solution.py:127
  216.2 6.4 %copy-start.3 = (bf16[32,64,256]{2,1,0:T(8,128)(2,1)S(1)}, bf16[32,64,256]{2,1,0:T(8,128)(2,1)}, u32[]{:S(2)}) copy-start(bf16[32,64,256]{2,1,0:T(8,128)(2,1)} %copy-done.2) | copy-start | bytes 3145732
  216.2 6.4 %copy-start.6 = (bf16[32,32,64]{2,1,0:T(8,128)(2,1)S(1)}, bf16[32,32,64]{2,1,0:T(8,128)(2,1)}, u32[]{:S(2)}) copy-start(bf16[32,32,64]{2,1,0:T(8,128)(2,1)} %copy-done.5) | copy-start | bytes 393220
  216.2 99.6 %all-to-all-start.3 = ((bf16[16,64,2048]{2,1,0:T(8,128)(2,1)}), bf16[16,64,2048]{2,1,0:T(8,128)(2,1)}, u32[]{:S(2)}, u32[]{:S(2)}) async-start(bf16[16,64,2048]{2,1,0:T(8,128)(2,1)} %scatter_fusion), calls=%async_computation.4 | async-start | bytes 8388608 | tf_op jit(solution)/shard_map/all_to_all | solution.py:126
  244.0 80.1 %copy-start.1 = (bf16[3,64,2048]{2,1,0:T(8,128)(2,1)S(1)}, bf16[3,64,2048]{2,1,0:T(8,128)(2,1)}, u32[]{:S(2)}) copy-start(bf16[3,64,2048]{2,1,0:T(8,128)(2,1)} %param.10) | copy-start | bytes 2359300
Sparse Core Ops, SparseCore 0:
  50.5 24.1 all-gather.1
  77.2 44.4 reduce-scatter.1
where the time goes:
time: 336 us; the launch traced here: 331 us
  waiting for transfers between devices  161 us (48%)
  matrix products  66.7 us (20%)
  local copies, waits for them, and re-layouts  32.7 us (10%)
  starting transfers between devices  27.2 us (8%)
  blocking collectives  25.3 us (8%)
  between operations  14.7 us (4%)
  other arithmetic  3.52 us (1%)
    all_to_all x1, waiting for transfers between devices, shards(): lax.all_to_all(returned_down_panel, 'dp', split_axis=0, concat_axis=0, ti...  77.6 us
    all_to_all x1, waiting for transfers between devices, shards(): lax.all_to_all(send_a, 'dp', split_axis=0, concat_axis=0, tiled=True)  69.4 us
    psum x1, blocking collectives, shards(): down_low = lax.psum(down_part, 'mp').astype(jnp.bfloat16)  25.3 us
    dot_general x1, matrix products, shards(): jnp.einsum('bs,brd->srd', gather_slots, block_grad_a, precision=lax.Preci...  12.2 us
    dot_general x1, matrix products, shards(): lax.dot_general(lax.all_gather(cotangent, 'mp', axis=1, tiled=True), w_co...  11.8 us
    dot_general x1, matrix products, shards(): lax.dot_general(w_cols, tokens, (((0,), (1,)), ((), ())), preferred_eleme...  9.94 us
    dot_general x1, matrix products, shards(): jnp.einsum('swq,sqj->swj', up_grad, block_down_panel, preferred_element_t...  7.83 us
    all_to_all x1, starting transfers between devices, shards(): lax.all_to_all(requests, 'dp', split_axis=0, concat_axis=0, tiled=True)  7.25 us
  transfers between devices with their start and end apart: 7, of which 4 were waited for; matrix products, arithmetic and copies ran while one was open for 26% of the time, Pallas kernels for 0%

commit v1 on v0

v1 whole, which is shorter than its diff:
```python
import jax
import jax.numpy as jnp
from jax import lax
from jax.sharding import PartitionSpec as P

F32 = jnp.float32
BF16 = jnp.bfloat16


def ring_order(n):
    cols = 1
    while 2 * (2 * cols) ** 2 <= n:
        cols *= 2
    rows = n // cols
    if cols < 2 or rows % 2 or rows * cols != n:
        return list(range(n))
    walk = [z * cols for z in range(rows)]
    for step, z in enumerate(reversed(range(rows))):
        across = range(1, cols) if step % 2 == 0 else reversed(range(1, cols))
        walk += [z * cols + x for x in across]
    return walk


def mp_sum(part, size):
    if size & (size - 1):
        return lax.psum(part, "mp")
    bit = 1
    while bit < size:
        part = part + lax.ppermute(part, "mp", [(i, i ^ bit) for i in range(size)])
        bit *= 2
    return part


def make_shards(n_dp, n_mp):
    order = ring_order(n_dp)
    place = [order.index(e) for e in range(n_dp)]
    forward = [(order[i], order[(i + 1) % n_dp]) for i in range(n_dp)]
    backward = [(b, a) for a, b in forward]
    half_way = n_dp // 2

    def shards(
        tokens,
        value_weight,
        adapter_down_panels,
        adapter_up_panels,
        cotangent,
        block_list_entry,
        device_tenant_list,
        tenant_location_map,
    ):
        rows, width = tokens.shape
        stored, rank, _ = adapter_down_panels.shape
        out_width = adapter_up_panels.shape[2]
        blocks = block_list_entry.shape[0]
        block_rows = rows // blocks
        listed = device_tenant_list.shape[0]
        tenants = tenant_location_map.shape[0]
        half = width // 2

        me = jnp.asarray(place, jnp.int32)[lax.axis_index("dp")]
        dp_at = jnp.asarray(order, jnp.int32)

        list_location = tenant_location_map[device_tenant_list]
        block_location = list_location[block_list_entry]
        row_location = jnp.repeat(block_location, block_rows)[:, None]
        row_slot = jnp.repeat(block_list_entry, block_rows)[:, None]

        up_all = lax.all_to_all(
            jnp.broadcast_to(adapter_up_panels[None], (n_dp,) + adapter_up_panels.shape),
            "dp", split_axis=0, concat_axis=0, tiled=True,
        ).reshape(tenants, rank, out_width)
        block_up = up_all[block_location]
        cot_blocks = cotangent.reshape(blocks, block_rows, out_width)
        up_part = jnp.einsum("bnc,brc->bnr", cot_blocks, block_up, preferred_element_type=F32)
        up_grad = mp_sum(up_part.reshape(rows, rank), n_mp).astype(BF16)

        from_behind, from_ahead = [adapter_down_panels], [adapter_down_panels]
        for _ in range(1, half_way):
            from_behind.append(lax.ppermute(from_behind[-1], "dp", forward))
            from_ahead.append(lax.ppermute(from_ahead[-1], "dp", backward))
        opposite = jnp.concatenate(
            [
                lax.ppermute(from_behind[-1][:, :, :half], "dp", forward),
                lax.ppermute(from_ahead[-1][:, :, half:], "dp", backward),
            ],
            axis=2,
        )
        held = jnp.concatenate(
            from_ahead + [opposite] + from_behind[:0:-1], axis=0
        )

        base_flipped = lax.psum_scatter(
            lax.dot_general(value_weight, tokens, (((0,), (1,)), ((), ())), preferred_element_type=F32),
            "mp", scatter_dimension=0, tiled=True,
        )
        cot_all = lax.all_gather(cotangent, "mp", axis=1, tiled=True)

        def spread(low, keep, count):
            eye = jnp.tile(jnp.eye(rank, dtype=BF16), (1, count))
            wide = jnp.dot(low, eye, preferred_element_type=F32)
            group = lax.broadcasted_iota(jnp.int32, (1, count * rank), 1) // rank
            return jnp.where(group == keep, wide, 0.0).astype(BF16)

        def own_share(ahead):
            dest = dp_at[(me + ahead) % n_dp]
            mine = spread(up_grad, row_location - dest * stored, stored)
            return lax.dot_general(mine, tokens, (((0,), (0,)), ((), ())), preferred_element_type=F32)

        far = own_share(half_way)
        going_ahead = far[:, :half].astype(BF16)
        going_back = far[:, half:].astype(BF16)
        ahead_sum = lax.ppermute(going_ahead, "dp", forward)
        back_sum = lax.ppermute(going_back, "dp", backward)
        zeros = jnp.zeros((stored * rank, half), F32)
        for k in range(half_way - 1, 0, -1):
            share_ahead, share_back = own_share(k), own_share(-k)
            if k == half_way - 1:
                got_ahead = jnp.concatenate([ahead_sum.astype(F32), zeros], axis=1)
                got_back = jnp.concatenate([zeros, back_sum.astype(F32)], axis=1)
            else:
                got_ahead, got_back = ahead_sum.astype(F32), back_sum.astype(F32)
            ahead_sum = lax.ppermute((share_ahead + got_ahead).astype(BF16), "dp", forward)
            back_sum = lax.ppermute((share_back + got_back).astype(BF16), "dp", backward)
        grad_a = (own_share(0) + ahead_sum.astype(F32) + back_sum.astype(F32)).astype(BF16)
        grad_a = grad_a.reshape(stored, rank, width)

        owner = list_location // stored
        ring_at = jnp.asarray(place, jnp.int32)[owner]
        held_row = ((ring_at - me) % n_dp) * stored + list_location % stored
        slot_down = held[held_row].reshape(listed * rank, width)

        down_wide = lax.dot_general(tokens, slot_down, (((1,), (1,)), ((), ())), preferred_element_type=F32)
        down_part = jnp.zeros((rows, rank), F32)
        for s in range(listed):
            down_part = down_part + jnp.where(row_slot == s, down_wide[:, s * rank:(s + 1) * rank], 0.0)
        down_low = mp_sum(down_part, n_mp).astype(BF16)
        adapter_output = jnp.einsum(
            "afq,aqy->afy", down_low.reshape(blocks, block_rows, rank), block_up, preferred_element_type=F32
        ).reshape(rows, out_width)
        values = (base_flipped.T + adapter_output).astype(BF16)

        up_wide = spread(up_grad, row_slot, listed)
        token_gradient = (
            lax.dot_general(cot_all, value_weight, (((1,), (1,)), ((), ())), preferred_element_type=F32)
            + jnp.dot(up_wide, slot_down, preferred_element_type=F32)
        ).astype(BF16)

        down_spread = spread(down_low, row_location, tenants)
        share_b = lax.dot_general(
            down_spread, cotangent, (((0,), (0,)), ((), ())), preferred_element_type=F32
        ).astype(BF16)
        back_b = lax.all_to_all(
            share_b.reshape(tenants, rank, out_width), "dp", split_axis=0, concat_axis=0, tiled=True
        ).reshape(n_dp, stored, rank, out_width)
        grad_b = jnp.sum(back_b.astype(F32), axis=0).astype(BF16)
        return (values, token_gradient, grad_a, grad_b)

    return shards


def solution(mesh):
    in_specs = (
        P("dp", "mp"),
        P("mp", None),
        P("dp", None, "mp"),
        P("dp", None, "mp"),
        P("dp", "mp"),
        P("dp"),
        P("dp"),
        P(),
    )
    out_specs = (P("dp", "mp"), P("dp", "mp"), P("dp", None, "mp"), P("dp", None, "mp"))
    shards = make_shards(mesh.shape["dp"], mesh.shape["mp"])
    return jax.shard_map(shards, mesh=mesh, in_specs=in_specs, out_specs=out_specs, check_vma=False)
```

time: 336 us -> 220 us (0.65)
  waiting for transfers between devices: 161 us -> 51.9 us
  blocking collectives: 25.3 us -> 0 us
  other arithmetic: 3.52 us -> 17.6 us
  matrix products: 66.7 us -> 55.3 us
  between operations: 14.7 us -> 26 us
  starting transfers between devices: 27.2 us -> 35.2 us
    all_to_all x5 -> x2, waiting for transfers between devices: 161 us -> 1.59 us  [the longest x1 1.59 us: shards(): lax.all_to_all(share_b.reshape(tenants, rank, out_width), 'dp', split_axi...]
    ppermute x0 -> x20, waiting for transfers between devices: none -> 49.7 us  [the longest x1 19.3 us: shards(): lax.ppermute(from_ahead[-1][:, :, half:], 'dp', backward)]
    psum x1 -> x0, blocking collectives: 25.3 us -> none  [shards(): down_low = lax.psum(down_part, 'mp').astype(jnp.bfloat16)]
    ppermute x0 -> x20, starting transfers between devices: none -> 23.3 us  [the longest x3 6.69 us: shards(): from_ahead.append(lax.ppermute(from_ahead[-1], 'dp', backward))]
    all_to_all x5 -> x2, starting transfers between devices: 26.9 us -> 11.8 us  [the longest x1 6.19 us: shards(): lax.all_to_all(jnp.broadcast_to(adapter_up_panels[None], (n_dp,) + adapte...]
    convert_element_type x1 -> x9, other arithmetic: 1.42 us -> 14.1 us  [the longest x2 4.55 us: shards(): (share_back + got_back).astype(BF16)]
    dot_general x14 -> x16, matrix products: 66.7 us -> 55.3 us  [the longest x8 13.7 us: own_share(): lax.dot_general(mine, tokens, (((0,), (0,)), ((), ())), preferred_element...]
    unnamed x21 -> x35, local copies, waits for them, and re-layouts: 4.43 us -> 12.4 us
  transfers between devices with their start and end apart: 7 -> 24, of which waited for: 4 -> 7; matrix products, arithmetic and copies ran while one was open for 26% -> 46% of each run, Pallas kernels for 0% -> 0%
where the time goes in v1:
time: 220 us; the launch traced here: 216 us
  matrix products  55.3 us (25%)
  waiting for transfers between devices  51.9 us (24%)
  starting transfers between devices  35.2 us (16%)
  local copies, waits for them, and re-layouts  29.6 us (13%)
  between operations  26 us (12%)
  other arithmetic  17.6 us (8%)
    ppermute x1, waiting for transfers between devices, shards(): lax.ppermute(from_ahead[-1][:, :, half:], 'dp', backward)  19.3 us
    dot_general x8, matrix products, own_share(): lax.dot_general(mine, tokens, (((0,), (0,)), ((), ())), preferred_element...  13.7 us
    unnamed x35, local copies, waits for them, and re-layouts  12.4 us
    dot_general x1, matrix products, shards(): lax.dot_general(cot_all, value_weight, (((1,), (1,)), ((), ())), preferre...  10.6 us
    dot_general x1, matrix products, shards(): lax.dot_general(value_weight, tokens, (((0,), (1,)), ((), ())), preferred...  10.4 us
    ppermute x4, waiting for transfers between devices, mp_sum(): part = part + lax.ppermute(part, 'mp', [(i, i ^ bit) for i in range(size)])  9.81 us
    ppermute x3, waiting for transfers between devices, shards(): lax.ppermute((share_back + got_back).astype(BF16), 'dp', backward)  9.07 us
    dot_general x1, matrix products, shards(): jnp.dot(up_wide, slot_down, preferred_element_type=F32)  8.75 us
  transfers between devices with their start and end apart: 24, of which 7 were waited for; matrix products, arithmetic and copies ran while one was open for 46% of the time, Pallas kernels for 0%

profile of v1, /device:TPU:0, one launch (start us, length us, event | category | flops | bytes accessed | tf_op | source)
XLA Modules:
  0.0 215.7 jit_solution(1441703671719374801)
XLA Ops:
  7.9 3.0 %collective-permute-start = (bf16[3,64,2048]{2,1,0:T(8,128)(2,1)}, bf16[3,64,2048]{2,1,0:T(8,128)(2,1)}, u32[]{:S(2)}, u32[]{:S(2)}) collective-permute-start(bf16[3,64,2048]{2,1,0:T(8,128)(2,1)} %param.13), channel_id=1, source_target_pairs={{8,0},{16,8},{24,16},{28,24},{20,28},{12,20},{4,12},{0,4},{9,1},{1... | collective-permute-start | bytes 2359304 | tf_op jit(solution)/shard_map/ppermute | solution.py:80
  12.9 6.2 %all-to-all-start = ((bf16[8,3,64,256]{3,2,1,0:T(8,128)(2,1)}), bf16[8,3,64,256]{3,2,1,0:T(8,128)(2,1)S(1)}, u32[]{:S(2)}, u32[]{:S(2)}) async-start(bf16[8,3,64,256]{3,2,1,0:T(8,128)(2,1)} %broadcast_in_dim.106), calls=%async_computation.1 | async-start | bytes 1572864 | tf_op jit(solution)/shard_map/all_to_all | solution.py:68
  19.1 10.4 %fusion.68 = f32[1024,1024]{1,0:T(8,128)} fusion(bf16[2048,1024]{1,0:T(8,128)(2,1)} %param.12, bf16[1024,2048]{1,0:T(8,128)(2,1)} %param.11), kind=kOutput, calls=%fused_computation.158 | convolution fusion | flops 4294967296 | bytes 12582912 | tf_op jit(solution)/shard_map/dot_general | solution.py:93
  51.9 2.3 %constant_dynamic-update-slice_fusion.6 = bf16[24,64,2048]{2,1,0:T(8,128)(2,1)} fusion(bf16[3,64,2048]{2,1,0:T(8,128)(2,1)} %param.13), kind=kLoop, calls=%fused_computation.88 | loop fusion | bytes 1572864
  55.8 2.3 %constant_dynamic-update-slice_fusion.5 = bf16[24,64,2048]{2,1,0:T(8,128)(2,1)} fusion(bf16[24,64,2048]{2,1,0:T(8,128)(2,1)} %constant_dynamic-update-slice_fusion.6, bf16[3,64,2048]{2,1,0:T(8,128)(2,1)} %collective-permute-done), kind=kLoop, calls=%fused_computation.87 | loop fusion | bytes 1572864
  58.1 7.6 %collective-permute-done.1 = bf16[3,64,2048]{2,1,0:T(8,128)(2,1)} collective-permute-done((bf16[3,64,2048]{2,1,0:T(8,128)(2,1)}, bf16[3,64,2048]{2,1,0:T(8,128)(2,1)}, u32[]{:S(2)}, u32[]{:S(2)}) %collective-permute-start.1) | collective-permute-done | bytes 786464 | tf_op jit(solution)/shard_map/ppermute | solution.py:80
  69.9 9.4 %collective-permute-done.11 = f32[1024,64]{1,0:T(8,128)S(1)} collective-permute-done((f32[1024,64]{1,0:T(8,128)S(1)}, f32[1024,64]{1,0:T(8,128)S(1)}, u32[]{:S(2)}, u32[]{:S(2)}) %collective-permute-start.11) | collective-permute-done | bytes 262176 | tf_op jit(solution)/shard_map/ppermute | solution.py:29
  84.0 2.6 %collective-permute-start.16 = (bf16[192,1024]{1,0:T(8,128)(2,1)S(1)}, bf16[192,1024]{1,0:T(8,128)(2,1)S(1)}, u32[]{:S(2)}, u32[]{:S(2)}) collective-permute-start(bf16[192,1024]{1,0:T(8,128)(2,1)S(1)} %get-tuple-element.13), channel_id=1, source_target_pairs={{8,0},{16,8},{24,16},{28,24},{20,28},{12,20},{4,12},{0,4},{9,1},{1... | collective-permute-start | bytes 1179656 | tf_op jit(solution)/shard_map/ppermute | solution.py:113
  86.6 2.2 %fusion.4 = f32[192,2048]{1,0:T(8,128)} fusion(bf16[1024,2048]{1,0:T(8,128)(2,1)S(1)} %copy-done.3, bf16[1024,192]{0,1:T(8,128)(2,1)S(1)} %fusion.72, s32[1024]{0:T(1024)S(1)} %get-tuple-element.21, s32[192]{0:T(256)S(1)} %and_select_fusion), kind=kOutput, calls=%fused_computation.33 | convolution fusion | flops 805699584 | bytes 6165248 | tf_op jit(solution)/shard_map/dot_general | solution.py:107
  88.8 2.2 %fusion.5 = f32[192,2048]{1,0:T(8,128)} fusion(bf16[1024,2048]{1,0:T(8,128)(2,1)S(1)} %copy-done.3, bf16[1024,192]{0,1:T(8,128)(2,1)S(1)} %fusion.72, s32[1024]{0:T(1024)S(1)} %get-tuple-element.20, s32[192]{0:T(256)S(1)} %and_select_fusion), kind=kOutput, calls=%fused_computation.34 | convolution fusion | flops 805699584 | bytes 6165248 | tf_op jit(solution)/shard_map/dot_general | solution.py:107
  91.0 3.8 %collective-permute-done.16 = bf16[192,1024]{1,0:T(8,128)(2,1)S(1)} collective-permute-done((bf16[192,1024]{1,0:T(8,128)(2,1)S(1)}, bf16[192,1024]{1,0:T(8,128)(2,1)S(1)}, u32[]{:S(2)}, u32[]{:S(2)}) %collective-permute-start.16) | collective-permute-done | bytes 393248 | tf_op jit(solution)/shard_map/ppermute | solution.py:113
  103.9 19.3 %collective-permute-done.7 = bf16[3,64,1024]{2,1,0:T(8,128)(2,1)S(1)} collective-permute-done((bf16[3,64,1024]{2,1,0:T(8,128)(2,1)S(1)}, bf16[3,64,1024]{2,1,0:T(8,128)(2,1)S(1)}, u32[]{:S(2)}, u32[]{:S(2)}) %collective-permute-start.7) | collective-permute-done | bytes 393248 | tf_op jit(solution)/shard_map/ppermute | solution.py:84
  129.3 4.8 %gather_fusion.2 = bf16[8,64,2048]{2,1,0:T(8,128)(2,1)} fusion(bf16[24,64,2048]{2,1,0:T(8,128)(2,1)} %constant_dynamic-update-slice_fusion, s32[1024]{0:T(1024)S(1)} %pad_clamp_fusion.2), kind=kCustom, calls=%fused_computation.2 | custom fusion | bytes 4194336 | tf_op jit(solution)/shard_map/gather | solution.py:130
  134.1 5.3 %convolution_bitcast_fusion = f32[1024,512]{0,1:T(8,128)S(1)} fusion(bf16[512,2048]{1,0:T(8,128)(2,1)} %bitcast.86, bf16[1024,2048]{1,0:T(8,128)(2,1)} %param.11), kind=kOutput, calls=%fused_computation.10 | convolution fusion | flops 2147483648 | bytes 8388608 | tf_op jit(solution)/shard_map/dot_general | solution.py:132
  141.5 3.5 %collective-permute-start.9 = (f32[1024,64]{0,1:T(8,128)S(1)}, f32[1024,64]{0,1:T(8,128)}, u32[]{:S(2)}, u32[]{:S(2)}) collective-permute-start(f32[1024,64]{0,1:T(8,128)S(1)} %fusion.99), channel_id=1, source_target_pairs={{0,2},{1,3},{2,0},{3,1},{4,6},{5,7},{6,4},{7,5},{8,10},{9,11},{10,... | collective-permute-start | bytes 786440 | tf_op jit(solution)/shard_map/ppermute | solution.py:29
  151.4 10.6 %fusion.70 = f32[1024,2048]{1,0:T(8,128)} fusion(bf16[1024,1024]{1,0:T(8,128)(2,1)} %all-gather.2.cloned.1.call-done, bf16[2048,1024]{1,0:T(8,128)(2,1)} %param.12), kind=kOutput, calls=%fused_computation.160 | convolution fusion | flops 4294967296 | bytes 14680064 | tf_op jit(solution)/shard_map/dot_general | solution.py:144
  163.1 3.7 %convolution_convert_fusion = bf16[1536,256]{1,0:T(8,128)(2,1)} fusion(bf16[1024,256]{1,0:T(8,128)(2,1)S(1)} %copy-done.9, bf16[1024,64]{0,1:T(8,128)(2,1)S(1)} %add_convert_fusion.9, bf16[64,1536]{1,0:T(8,128)(2,1)} %tile.17, s32[1536]{0:T(1024)} %add_select_fusion, s32[1024]{0:T(1024)S(1)} %broadcast_in_dim_reshape.7), kind=kOutput, calls=%fused_computation.7 | convolution fusion | flops 1011744768 | bytes 1648640 | tf_op jit(solution)/shard_map/dot_general | solution.py:149
  166.8 5.7 %all-to-all-start.1 = ((bf16[24,64,256]{2,1,0:T(8,128)(2,1)}), bf16[24,64,256]{2,1,0:T(8,128)(2,1)S(1)}, u32[]{:S(2)}, u32[]{:S(2)}) async-start(bf16[24,64,256]{2,1,0:T(8,128)(2,1)} %bitcast.91), calls=%async_computation.2 | async-start | bytes 1572864 | tf_op jit(solution)/shard_map/all_to_all | solution.py:152
  172.5 2.4 %add_convert_fusion.2 = bf16[192,2048]{1,0:T(8,128)(2,1)} fusion(f32[192,2048]{1,0:T(8,128)S(1)} %fusion.8, bf16[192,2048]{1,0:T(8,128)(2,1)} %collective-permute-done.18), kind=kLoop, calls=%fused_computation.12 | loop fusion | flops 1179648 | bytes 3145728 | tf_op jit(solution)/shard_map/convert_element_type | solution.py:123
  176.8 2.2 %add_convert_fusion.5 = bf16[192,2048]{1,0:T(8,128)(2,1)} fusion(f32[192,2048]{1,0:T(8,128)S(1)} %copy-done.5, bf16[192,2048]{1,0:T(8,128)(2,1)} %collective-permute-done.14), kind=kLoop, calls=%fused_computation.15 | loop fusion | flops 1179648 | bytes 3145728 | tf_op jit(solution)/shard_map/convert_element_type | solution.py:122
  179.0 8.8 %add_convert_fusion = bf16[1024,2048]{1,0:T(8,128)(2,1)} fusion(f32[1024,2048]{1,0:T(8,128)} %fusion.70, bf16[512,2048]{1,0:T(8,128)(2,1)} %bitcast.87, bf16[1024,64]{1,0:T(8,128)(2,1)} %copy-done.10, bf16[64,512]{1,0:T(8,128)(2,1)} %tile.13, s32[512]{0:T(512)S(1)} %add_select_fusion.1, s32[1024]{0:T(1024)S(1)} %broadcast_in_dim_reshape.6), kind=kOutput, calls=%fused_computation.5 | convolution fusion | flops 2220359680 | bytes 14882816 | tf_op jit(solution)/shard_map/dot_general | solution.py:145
  188.6 2.2 %fusion.69 = f32[32,32,256]{2,1,0:T(8,128)} fusion(bf16[32,32,64]{2,1,0:T(8,128)(2,1)} %bitcast.90, bf16[32,64,256]{2,1,0:T(8,128)(2,1)S(1)} %gather_fusion.4), kind=kOutput, calls=%fused_computation.159 | convolution fusion | flops 33554432 | bytes 2228224 | tf_op jit(solution)/shard_map/afq,aqy->afy/dot_general | solution.py:137
  194.8 9.1 %collective-permute-done.19 = bf16[192,2048]{1,0:T(8,128)(2,1)} collective-permute-done((bf16[192,2048]{1,0:T(8,128)(2,1)}, bf16[192,2048]{1,0:T(8,128)(2,1)}, u32[]{:S(2)}, u32[]{:S(2)}) %collective-permute-start.19) | collective-permute-done | bytes 786464 | tf_op jit(solution)/shard_map/ppermute | solution.py:123
  203.9 2.6 %add_convert_fusion.1 = bf16[192,2048]{1,0:T(8,128)(2,1)} fusion(bf16[192,2048]{1,0:T(8,128)(2,1)} %collective-permute-done.19, f32[192,2048]{1,0:T(8,128)S(1)} %copy-done.7, bf16[192,2048]{1,0:T(8,128)(2,1)} %collective-permute-done.15), kind=kLoop, calls=%fused_computation.11 | loop fusion | flops 1966080 | bytes 3932160 | tf_op jit(solution)/shard_map/convert_element_type | solution.py:124
  (129 shorter events, 57.6 us)
Async XLA Ops:
  7.2 144.3 %all-gather.2.cloned.1.call-start = ((), (), s32[]{:S(2)}) async-start(), calls=%async_computation.4 | async-start | bytes 2621440 | tf_op jit(solution)/shard_map/all_gather | solution.py:96
  7.9 38.9 %collective-permute-start = (bf16[3,64,2048]{2,1,0:T(8,128)(2,1)}, bf16[3,64,2048]{2,1,0:T(8,128)(2,1)}, u32[]{:S(2)}, u32[]{:S(2)}) collective-permute-start(bf16[3,64,2048]{2,1,0:T(8,128)(2,1)} %param.13), channel_id=1, source_target_pairs={{8,0},{16,8},{24,16},{28,24},{20,28},{12,20},{4,12},{0,4},{9,1},{1... | collective-permute-start | bytes 2359304 | tf_op jit(solution)/shard_map/ppermute | solution.py:80
  10.9 37.9 %collective-permute-start.3 = (bf16[3,64,2048]{2,1,0:T(8,128)(2,1)}, bf16[3,64,2048]{2,1,0:T(8,128)(2,1)}, u32[]{:S(2)}, u32[]{:S(2)}) collective-permute-start(bf16[3,64,2048]{2,1,0:T(8,128)(2,1)} %param.13), channel_id=1, source_target_pairs={{0,8},{8,16},{16,24},{24,28},{28,20},{20,12},{12,4},{4,0},{1,9},{9... | collective-permute-start | bytes 2359304 | tf_op jit(solution)/shard_map/ppermute | solution.py:79
  12.9 36.0 %all-to-all-start = ((bf16[8,3,64,256]{3,2,1,0:T(8,128)(2,1)}), bf16[8,3,64,256]{3,2,1,0:T(8,128)(2,1)S(1)}, u32[]{:S(2)}, u32[]{:S(2)}) async-start(bf16[8,3,64,256]{3,2,1,0:T(8,128)(2,1)} %broadcast_in_dim.106), calls=%async_computation.1 | async-start | bytes 1572864 | tf_op jit(solution)/shard_map/all_to_all | solution.py:68
  19.1 187.4 %reduce-scatter.2.cloned.1.call-start = ((), (), s32[]{:S(2)}) async-start(), calls=%async_computation.3 | async-start | bytes 5242880 | tf_op jit(solution)/shard_map/reduce_scatter | solution.py:92
  46.8 18.9 %collective-permute-start.1 = (bf16[3,64,2048]{2,1,0:T(8,128)(2,1)}, bf16[3,64,2048]{2,1,0:T(8,128)(2,1)}, u32[]{:S(2)}, u32[]{:S(2)}) collective-permute-start(bf16[3,64,2048]{2,1,0:T(8,128)(2,1)} %collective-permute-done), channel_id=1, source_target_pairs={{8,0},{16,8},{24,16},{28,24},{20,28},{12,20},{4,12},{0,4},{9,1},{1... | collective-permute-start | bytes 2359304 | tf_op jit(solution)/shard_map/ppermute | solution.py:80
  48.8 18.6 %collective-permute-start.4 = (bf16[3,64,2048]{2,1,0:T(8,128)(2,1)}, bf16[3,64,2048]{2,1,0:T(8,128)(2,1)}, u32[]{:S(2)}, u32[]{:S(2)}) collective-permute-start(bf16[3,64,2048]{2,1,0:T(8,128)(2,1)} %collective-permute-done.3), channel_id=1, source_target_pairs={{0,8},{8,16},{16,24},{24,28},{28,20},{20,12},{12,4},{4,0},{1,9},{9... | collective-permute-start | bytes 2359304 | tf_op jit(solution)/shard_map/ppermute | solution.py:79
  49.9 4.2 %collective-permute-start.10 = (f32[1024,64]{1,0:T(8,128)S(1)}, f32[1024,64]{1,0:T(8,128)S(1)}, u32[]{:S(2)}, u32[]{:S(2)}) collective-permute-start(f32[1024,64]{1,0:T(8,128)S(1)} %bitcast.88), channel_id=1, source_target_pairs={{0,1},{1,0},{2,3},{3,2},{4,5},{5,4},{6,7},{7,6},{8,9},{9,8},{10,11... | collective-permute-start | bytes 786440 | tf_op jit(solution)/shard_map/ppermute | solution.py:29
  54.2 25.1 %collective-permute-start.11 = (f32[1024,64]{1,0:T(8,128)S(1)}, f32[1024,64]{1,0:T(8,128)S(1)}, u32[]{:S(2)}, u32[]{:S(2)}) collective-permute-start(f32[1024,64]{1,0:T(8,128)S(1)} %bitcast_add_fusion.1), channel_id=1, source_target_pairs={{0,2},{1,3},{2,0},{3,1},{4,6},{5,7},{6,4},{7,5},{8,10},{9,11},{10,... | collective-permute-start | bytes 786440 | tf_op jit(solution)/shard_map/ppermute | solution.py:29
  65.7 32.8 %collective-permute-start.2 = (bf16[3,64,2048]{2,1,0:T(8,128)(2,1)}, bf16[3,64,2048]{2,1,0:T(8,128)(2,1)S(1)}, u32[]{:S(2)}, u32[]{:S(2)}) collective-permute-start(bf16[3,64,2048]{2,1,0:T(8,128)(2,1)} %collective-permute-done.1), channel_id=1, source_target_pairs={{8,0},{16,8},{24,16},{28,24},{20,28},{12,20},{4,12},{0,4},{9,1},{1... | collective-permute-start | bytes 2359304 | tf_op jit(solution)/shard_map/ppermute | solution.py:80
  67.4 32.6 %collective-permute-start.5 = (bf16[3,64,2048]{2,1,0:T(8,128)(2,1)}, bf16[3,64,2048]{2,1,0:T(8,128)(2,1)S(1)}, u32[]{:S(2)}, u32[]{:S(2)}) collective-permute-start(bf16[3,64,2048]{2,1,0:T(8,128)(2,1)} %collective-permute-done.4), channel_id=1, source_target_pairs={{0,8},{8,16},{16,24},{24,28},{28,20},{20,12},{12,4},{4,0},{1,9},{9... | collective-permute-start | bytes 2359304 | tf_op jit(solution)/shard_map/ppermute | solution.py:79
  84.0 10.8 %collective-permute-start.16 = (bf16[192,1024]{1,0:T(8,128)(2,1)S(1)}, bf16[192,1024]{1,0:T(8,128)(2,1)S(1)}, u32[]{:S(2)}, u32[]{:S(2)}) collective-permute-start(bf16[192,1024]{1,0:T(8,128)(2,1)S(1)} %get-tuple-element.13), channel_id=1, source_target_pairs={{8,0},{16,8},{24,16},{28,24},{20,28},{12,20},{4,12},{0,4},{9,1},{1... | collective-permute-start | bytes 1179656 | tf_op jit(solution)/shard_map/ppermute | solution.py:113
  88.8 11.9 %collective-permute-start.12 = (bf16[192,1024]{1,0:T(8,128)(2,1)S(1)}, bf16[192,1024]{1,0:T(8,128)(2,1)S(1)}, u32[]{:S(2)}, u32[]{:S(2)}) collective-permute-start(bf16[192,1024]{1,0:T(8,128)(2,1)S(1)} %get-tuple-element.12), channel_id=1, source_target_pairs={{0,8},{8,16},{16,24},{24,28},{28,20},{20,12},{12,4},{4,0},{1,9},{9... | collective-permute-start | bytes 1179656 | tf_op jit(solution)/shard_map/ppermute | solution.py:112
  96.8 48.2 %collective-permute-start.17 = (bf16[192,2048]{1,0:T(8,128)(2,1)}, bf16[192,2048]{1,0:T(8,128)(2,1)}, u32[]{:S(2)}, u32[]{:S(2)}) collective-permute-start(bf16[192,2048]{1,0:T(8,128)(2,1)} %add_convert_fusion.4), channel_id=1, source_target_pairs={{8,0},{16,8},{24,16},{28,24},{20,28},{12,20},{4,12},{0,4},{9,1},{1... | collective-permute-start | bytes 2359304 | tf_op jit(solution)/shard_map/ppermute | solution.py:123
  98.6 24.6 %collective-permute-start.7 = (bf16[3,64,1024]{2,1,0:T(8,128)(2,1)S(1)}, bf16[3,64,1024]{2,1,0:T(8,128)(2,1)S(1)}, u32[]{:S(2)}, u32[]{:S(2)}) collective-permute-start(bf16[3,64,1024]{2,1,0:T(8,128)(2,1)S(1)} %slice.61), channel_id=1, source_target_pairs={{8,0},{16,8},{24,16},{28,24},{20,28},{12,20},{4,12},{0,4},{9,1},{1... | collective-permute-start | bytes 1179656 | tf_op jit(solution)/shard_map/ppermute | solution.py:84
  100.1 23.1 %collective-permute-start.6 = (bf16[3,64,1024]{2,1,0:T(8,128)(2,1)S(1)}, bf16[3,64,1024]{2,1,0:T(8,128)(2,1)S(1)}, u32[]{:S(2)}, u32[]{:S(2)}) collective-permute-start(bf16[3,64,1024]{2,1,0:T(8,128)(2,1)S(1)} %slice.60), channel_id=1, source_target_pairs={{0,8},{8,16},{16,24},{24,28},{28,20},{20,12},{12,4},{4,0},{1,9},{9... | collective-permute-start | bytes 1179656 | tf_op jit(solution)/shard_map/ppermute | solution.py:83
  102.7 46.0 %collective-permute-start.13 = (bf16[192,2048]{1,0:T(8,128)(2,1)}, bf16[192,2048]{1,0:T(8,128)(2,1)}, u32[]{:S(2)}, u32[]{:S(2)}) collective-permute-start(bf16[192,2048]{1,0:T(8,128)(2,1)} %add_convert_fusion.7), channel_id=1, source_target_pairs={{0,8},{8,16},{16,24},{24,28},{28,20},{20,12},{12,4},{4,0},{1,9},{9... | collective-permute-start | bytes 2359304 | tf_op jit(solution)/shard_map/ppermute | solution.py:122
  139.6 1.6 collective-permute-start.8
  141.5 20.6 %collective-permute-start.9 = (f32[1024,64]{0,1:T(8,128)S(1)}, f32[1024,64]{0,1:T(8,128)}, u32[]{:S(2)}, u32[]{:S(2)}) collective-permute-start(f32[1024,64]{0,1:T(8,128)S(1)} %fusion.99), channel_id=1, source_target_pairs={{0,2},{1,3},{2,0},{3,1},{4,6},{5,7},{6,4},{7,5},{8,10},{9,11},{10,... | collective-permute-start | bytes 786440 | tf_op jit(solution)/shard_map/ppermute | solution.py:29
  147.2 25.2 %collective-permute-start.18 = (bf16[192,2048]{1,0:T(8,128)(2,1)}, bf16[192,2048]{1,0:T(8,128)(2,1)}, u32[]{:S(2)}, u32[]{:S(2)}) collective-permute-start(bf16[192,2048]{1,0:T(8,128)(2,1)} %add_convert_fusion.3), channel_id=1, source_target_pairs={{8,0},{16,8},{24,16},{28,24},{20,28},{12,20},{4,12},{0,4},{9,1},{1... | collective-permute-start | bytes 2359304 | tf_op jit(solution)/shard_map/ppermute | solution.py:123
  150.9 26.0 %collective-permute-start.14 = (bf16[192,2048]{1,0:T(8,128)(2,1)}, bf16[192,2048]{1,0:T(8,128)(2,1)}, u32[]{:S(2)}, u32[]{:S(2)}) collective-permute-start(bf16[192,2048]{1,0:T(8,128)(2,1)} %add_convert_fusion.6), channel_id=1, source_target_pairs={{0,8},{8,16},{16,24},{24,28},{28,20},{20,12},{12,4},{4,0},{1,9},{9... | collective-permute-start | bytes 2359304 | tf_op jit(solution)/shard_map/ppermute | solution.py:122
  166.8 27.2 %all-to-all-start.1 = ((bf16[24,64,256]{2,1,0:T(8,128)(2,1)}), bf16[24,64,256]{2,1,0:T(8,128)(2,1)S(1)}, u32[]{:S(2)}, u32[]{:S(2)}) async-start(bf16[24,64,256]{2,1,0:T(8,128)(2,1)} %bitcast.91), calls=%async_computation.2 | async-start | bytes 1572864 | tf_op jit(solution)/shard_map/all_to_all | solution.py:152
  174.8 29.0 %collective-permute-start.19 = (bf16[192,2048]{1,0:T(8,128)(2,1)}, bf16[192,2048]{1,0:T(8,128)(2,1)}, u32[]{:S(2)}, u32[]{:S(2)}) collective-permute-start(bf16[192,2048]{1,0:T(8,128)(2,1)} %add_convert_fusion.2), channel_id=1, source_target_pairs={{8,0},{16,8},{24,16},{28,24},{20,28},{12,20},{4,12},{0,4},{9,1},{1... | collective-permute-start | bytes 2359304 | tf_op jit(solution)/shard_map/ppermute | solution.py:123
  179.0 24.8 %collective-permute-start.15 = (bf16[192,2048]{1,0:T(8,128)(2,1)}, bf16[192,2048]{1,0:T(8,128)(2,1)}, u32[]{:S(2)}, u32[]{:S(2)}) collective-permute-start(bf16[192,2048]{1,0:T(8,128)(2,1)} %add_convert_fusion.5), channel_id=1, source_target_pairs={{0,8},{8,16},{16,24},{24,28},{28,20},{20,12},{12,4},{4,0},{1,9},{9... | collective-permute-start | bytes 2359304 | tf_op jit(solution)/shard_map/ppermute | solution.py:122
  (14 other events, 166.6 us)
Sparse Core Ops, SparseCore 0:
  9.6 25.5 all-gather.1
  37.7 54.7 reduce-scatter.1

commit v2 on v1

v2 whole, which is shorter than its diff:
```python
import jax
import jax.numpy as jnp
from jax import lax
from jax.experimental import pallas as pl
from jax.experimental.pallas import tpu as pltpu
from jax.sharding import PartitionSpec as P

F32 = jnp.float32
BF16 = jnp.bfloat16
MOST = 2


def grid_of(n):
    cols = 1
    while 2 * (2 * cols) ** 2 <= n:
        cols *= 2
    return (n // cols, cols) if n % cols == 0 else (n, 1)


def rows_by_need(Z):
    result = []
    for z in range(Z):
        up = {z + 1 + i: Z - 1 - i for i in range(Z - 1 - z)}
        down = {Z - z + i: i for i in range(z)}
        first, second = (up, down) if z < Z // 2 else (down, up)
        places = [None] * (Z - 1)
        for step, dest in first.items():
            places[step - 1] = dest
        rest = [dest for _, dest in sorted(second.items())]
        result.append([rest.pop(0) if p is None else p for p in places] + [z])
    return result


def lasting(us):
    return pl.CostEstimate(flops=int(us * 1.1e9), bytes_accessed=int(us * 3.4e6), transcendentals=0)


def matmul(a, b, dims=((1,), (0,))):
    return lax.dot_general(a, b, (dims, ((), ())), preferred_element_type=F32)


def after(values, others):
    count = len(values)
    return list(lax.optimization_barrier(tuple(values) + tuple(others))[:count])


def pick_panels(sources, where, which):
    slots = which.shape[0]
    _, rank, width = sources[0].shape
    n = len(sources)

    def kernel(where_ref, which_ref, *refs):
        srcs, dst, sem = refs[:n], refs[n], refs[n + 1]

        @pl.loop(0, slots)
        def _(s):
            source, panel = where_ref[s], which_ref[s]
            for b in range(n):

                @pl.when(source == b)
                def _(b=b):
                    pltpu.make_async_copy(srcs[b].at[panel], dst.at[s], sem).start()

        pltpu.make_async_copy(dst, dst, sem).wait()

    smem = pl.BlockSpec(memory_space=pltpu.SMEM)
    return pl.pallas_call(
        kernel,
        in_specs=[smem, smem] + [pl.BlockSpec(memory_space=pltpu.HBM)] * n,
        out_specs=pl.BlockSpec(memory_space=pltpu.VMEM),
        out_shape=jax.ShapeDtypeStruct((slots, rank, width), BF16),
        scratch_shapes=[pltpu.SemaphoreType.DMA],
        compiler_params=pltpu.CompilerParams(vmem_limit_bytes=32 * 1024 * 1024),
        cost_estimate=lasting(2.5),
        name="pick_panels",
    )(where, which, *sources)


def by_slot(wide, slots, rank):
    low = jnp.zeros((wide.shape[0], rank), F32)
    for s in range(wide.shape[1] // rank):
        low += jnp.where(slots == s, wide[:, s * rank:(s + 1) * rank], 0.0)
    return low


def up_products(locations, up_all, cotangent, row_slot, rank):
    rows, out_width = cotangent.shape
    listed = locations.shape[0]

    def kernel(at_ref, up_ref, cot_ref, slot_ref, part_ref, own_ref):
        for s in range(listed):
            own_ref[s * rank:(s + 1) * rank, :] = up_ref[at_ref[s]]
        low = by_slot(matmul(cot_ref[...], own_ref[...], ((1,), (1,))), slot_ref[...], rank)
        part_ref[...] = jnp.concatenate([low[:rows // 2], low[rows // 2:]], axis=1)

    vmem = pl.BlockSpec(memory_space=pltpu.VMEM)
    return pl.pallas_call(
        kernel,
        in_specs=[pl.BlockSpec(memory_space=pltpu.SMEM), vmem, vmem, vmem],
        out_specs=[vmem, vmem],
        out_shape=[
            jax.ShapeDtypeStruct((rows // 2, 2 * rank), F32),
            jax.ShapeDtypeStruct((listed * rank, out_width), BF16),
        ],
        compiler_params=pltpu.CompilerParams(vmem_limit_bytes=48 * 1024 * 1024),
        cost_estimate=lasting(2.5),
        name="up_products",
    )(locations, up_all, cotangent, row_slot)


def down_products(tokens, slot_down, row_slot, rank):
    rows, width = tokens.shape
    tile = min(256, rows // 2)
    steps = rows // 2 // tile

    def kernel(first_ref, second_ref, down_ref, slot_a_ref, slot_b_ref, part_ref):
        halves = [
            by_slot(matmul(tok[...], down_ref[...], ((1,), (1,))), slot[...], rank)
            for tok, slot in ((first_ref, slot_a_ref), (second_ref, slot_b_ref))
        ]
        part_ref[...] = jnp.concatenate(halves, axis=1)

    upper, lower = lambda i: (i, 0), lambda i: (i + steps, 0)
    return pl.pallas_call(
        kernel,
        grid=(steps,),
        in_specs=[
            pl.BlockSpec((tile, width), upper),
            pl.BlockSpec((tile, width), lower),
            pl.BlockSpec(slot_down.shape, lambda i: (0, 0)),
            pl.BlockSpec((tile, 1), upper),
            pl.BlockSpec((tile, 1), lower),
        ],
        out_specs=pl.BlockSpec((tile, 2 * rank), upper),
        out_shape=jax.ShapeDtypeStruct((rows // 2, 2 * rank), F32),
        compiler_params=pltpu.CompilerParams(vmem_limit_bytes=48 * 1024 * 1024),
        cost_estimate=lasting(4.6),
        name="down_products",
    )(tokens, tokens, slot_down, row_slot, row_slot)


def share_panels(positions, parts, row_slot, other, sizes):
    half_rows, pair = parts[0].shape
    rank, rows = pair // 2, 2 * half_rows
    listed, width = positions.shape[0], other.shape[1]
    tile = min(512, width)
    panels = sum(sizes)

    def kernel(at_ref, a_ref, b_ref, slot_ref, other_ref, wide_ref, *refs):
        out_refs, turned_ref, all_ref = refs[:-2], refs[-2], refs[-1]

        @pl.when(pl.program_id(0) == 0)
        def _():
            both = a_ref[...] + b_ref[...]
            low = jnp.concatenate([both[:, :rank], both[:, rank:]], axis=0).astype(BF16)
            column = lax.broadcasted_iota(jnp.int32, (rank, listed * rank), 1)
            eye = (column % rank == lax.broadcasted_iota(jnp.int32, (rank, listed * rank), 0)).astype(BF16)
            group = lax.broadcasted_iota(jnp.int32, (rows, listed * rank), 1) // rank
            wide = jnp.where(group == slot_ref[...], matmul(low, eye), 0.0)
            wide_ref[...] = wide.astype(BF16)
            turned_ref[...] = wide.T.astype(BF16)

        shares = matmul(turned_ref[...], other_ref[...]).astype(BF16)
        all_ref[...] = jnp.zeros(all_ref.shape, BF16)
        for s in range(listed):
            all_ref[pl.ds(pl.multiple_of(at_ref[s] * rank, rank), rank), :] = shares[s * rank:(s + 1) * rank]
        first = 0
        for ref, size in zip(out_refs, sizes):
            ref[...] = all_ref[first * rank:(first + size) * rank, :]
            first += size

    whole = lambda a: pl.BlockSpec(a.shape, lambda i, at: (0, 0))
    return pl.pallas_call(
        kernel,
        grid_spec=pltpu.PrefetchScalarGridSpec(
            num_scalar_prefetch=1,
            grid=(width // tile,),
            in_specs=[whole(parts[0]), whole(parts[1]), whole(row_slot), pl.BlockSpec((rows, tile), lambda i, at: (0, i))],
            out_specs=[pl.BlockSpec((rows, listed * rank), lambda i, at: (0, 0))]
            + [pl.BlockSpec((size * rank, tile), lambda i, at: (0, i)) for size in sizes],
            scratch_shapes=[pltpu.VMEM((listed * rank, rows), BF16), pltpu.VMEM((panels * rank, tile), BF16)],
        ),
        out_shape=[jax.ShapeDtypeStruct((rows, listed * rank), BF16)]
        + [jax.ShapeDtypeStruct((size * rank, width), BF16) for size in sizes],
        compiler_params=pltpu.CompilerParams(vmem_limit_bytes=48 * 1024 * 1024),
        cost_estimate=lasting(7.5),
        name="share_panels",
    )(positions, *parts, row_slot, other)


def add_arrivals(option, own, chosen, placing, others, stored, rank):
    width = own.shape[1]
    tile = min(512, width)
    places = [c for c, _ in chosen]
    arrays = [a for _, per_column in chosen for a in per_column]
    columns = len(placing)

    def kernel(option_ref, *refs):
        at_refs, own_refs, refs = refs[:columns], refs[columns:columns + len(places)], refs[columns + len(places):]
        got_refs, other_refs, out_ref = refs[:len(arrays)], refs[len(arrays):-1], refs[-1]

        def total_of(i):
            out = []
            for j in range(stored):
                here = slice(j * rank, (j + 1) * rank)
                total = own_refs[i][here, :].astype(F32)
                for ref in other_refs:
                    total += ref[here, :].astype(F32)
                for d in range(columns):
                    for r in range(MOST):
                        got = got_refs[i * columns + d][r * rank:(r + 1) * rank, :].astype(F32)
                        total += jnp.where(at_refs[d][places[i] * MOST + r] == j, got, 0.0)
                out_ref[here, :] = total.astype(BF16)

        if len(places) == 1:
            total_of(0)
        else:
            for i in range(len(places)):

                @pl.when(option_ref[0] == i)
                def _(i=i):
                    total_of(i)

    tall = stored * rank
    return pl.pallas_call(
        kernel,
        grid_spec=pltpu.PrefetchScalarGridSpec(
            num_scalar_prefetch=1 + columns,
            grid=(width // tile,),
            in_specs=[pl.BlockSpec((tall, tile), lambda i, *_, c=c: (c, i)) for c in places]
            + [pl.BlockSpec((MOST * rank, tile), lambda i, *_: (0, i))] * len(arrays)
            + [pl.BlockSpec((tall, tile), lambda i, *_: (0, i))] * len(others),
            out_specs=pl.BlockSpec((tall, tile), lambda i, *_: (0, i)),
        ),
        out_shape=jax.ShapeDtypeStruct((tall, width), BF16),
        compiler_params=pltpu.CompilerParams(vmem_limit_bytes=32 * 1024 * 1024),
        cost_estimate=lasting(2.5),
        name="add_arrivals",
    )(option, *[p.reshape(-1) for p in placing], *([own] * len(places)), *arrays, *others)


def base_products(mp_at, tokens, weight, count):
    rows, width = tokens.shape
    cols = weight.shape[1] // count
    tile = min(256, rows)

    def kernel(at_ref, tok_ref, *refs):
        for w, out in zip(refs[:count], refs[count:]):
            out[...] = matmul(tok_ref[...], w[...])

    return pl.pallas_call(
        kernel,
        grid_spec=pltpu.PrefetchScalarGridSpec(
            num_scalar_prefetch=1,
            grid=(rows // tile,),
            in_specs=[pl.BlockSpec((tile, width), lambda i, m: (i, 0))]
            + [pl.BlockSpec((width, cols), lambda i, m, p=p: (0, m[0] ^ p)) for p in range(count)],
            out_specs=[pl.BlockSpec((tile, cols), lambda i, m: (i, 0))] * count,
        ),
        out_shape=[jax.ShapeDtypeStruct((rows, cols), F32)] * count,
        compiler_params=pltpu.CompilerParams(vmem_limit_bytes=48 * 1024 * 1024),
        cost_estimate=lasting(8.5),
        name="base_products",
    )(mp_at, tokens, *([weight] * count))


def input_gradient(mp_at, cots, weight, up_wide, slot_down):
    rows = up_wide.shape[0]
    width = slot_down.shape[1]
    count = len(cots)
    cols = weight.shape[1] // count
    tile = min(256, rows)

    def kernel(at_ref, up_ref, slot_ref, *refs):
        total = matmul(up_ref[...], slot_ref[...])
        for c, w in zip(refs[:count], refs[count:2 * count]):
            total += matmul(c[...], w[...], ((1,), (1,)))
        refs[2 * count][...] = total.astype(BF16)

    by_row = lambda a: pl.BlockSpec((tile, a.shape[1]), lambda i, m: (i, 0))
    return pl.pallas_call(
        kernel,
        grid_spec=pltpu.PrefetchScalarGridSpec(
            num_scalar_prefetch=1,
            grid=(rows // tile,),
            in_specs=[by_row(up_wide), pl.BlockSpec(slot_down.shape, lambda i, m: (0, 0))]
            + [by_row(c) for c in cots]
            + [pl.BlockSpec((width, cols), lambda i, m, p=p: (0, m[0] ^ p)) for p in range(count)],
            out_specs=pl.BlockSpec((tile, width), lambda i, m: (i, 0)),
        ),
        out_shape=jax.ShapeDtypeStruct((rows, width), BF16),
        compiler_params=pltpu.CompilerParams(vmem_limit_bytes=48 * 1024 * 1024),
        cost_estimate=lasting(11.0),
        name="input_gradient",
    )(mp_at, up_wide, slot_down, *cots, *([weight] * count))


def make_shards(n_dp, n_mp):
    Z, X = grid_of(n_dp)
    leave = rows_by_need(Z)
    arrive = [rows[::-1] for rows in leave]

    def line(rows, step):
        return [(z * X + x, (z + step) * X + x) for z in rows for x in range(X)]

    def columns_on(d):
        return [(z * X + x, z * X + (x + d) % X) for z in range(Z) for x in range(X)]

    def source_at(z, row):
        return z - row if row <= z else Z - 1 + row - z

    needed = [sorted({source_at(z, arrive[z][k]) for z in range(Z)}) for k in range(Z)]

    def leaving_options(step, direction):
        there = range(step) if direction > 0 else range(Z - step, Z)
        return sorted({leave[z].index(z + direction * (Z - step)) for z in there})

    def leaving_option(z, step, direction):
        dest = z + direction * (Z - step)
        return leaving_options(step, direction).index(leave[z].index(dest)) if step and 0 <= dest < Z else 0

    def tables():
        result = []
        for z in range(Z):
            for x in range(X):
                result.append(
                    [z] * Z + [x] * Z + arrive[z]
                    + [needed[k].index(source_at(z, arrive[z][k])) for k in range(Z)]
                    + leave[z] + [arrive[z].index(r) for r in range(Z)] + [leave[z].index(r) for r in range(Z)]
                    + [leaving_option(z, s, 1) for s in range(Z)] + [leaving_option(z, s, -1) for s in range(Z)]
                )
        return result

    def mp_pairs(bit):
        return [(i, i ^ bit) for i in range(n_mp)]

    def shards(
        tokens,
        value_weight,
        adapter_down_panels,
        adapter_up_panels,
        cotangent,
        block_list_entry,
        device_tenant_list,
        tenant_location_map,
    ):
        rows, width = tokens.shape
        stored, rank, _ = adapter_down_panels.shape
        out_width = adapter_up_panels.shape[2]
        blocks = block_list_entry.shape[0]
        block_rows = rows // blocks
        listed = device_tenant_list.shape[0]
        tenants = tenant_location_map.shape[0]

        dp_at = lax.axis_index("dp")
        mp_at = lax.axis_index("mp")
        mp_ref = mp_at.reshape(1)
        table = lax.dynamic_index_in_dim(jnp.asarray(tables(), jnp.int32), dp_at, keepdims=False).reshape(9, Z)
        my_row, my_col, arriving, arriving_source, leaving, arrive_place, leave_place, up_option, down_option = [
            table[i] for i in range(9)
        ]
        my_row, my_col = my_row[:1], my_col[:1]

        def mp_parts(value):
            bit = 1
            while True:
                got = lax.ppermute(value, "mp", mp_pairs(bit))
                bit *= 2
                if bit >= n_mp:
                    return value, got
                value = value + got

        cots = [cotangent]
        bit = n_mp // 2
        while bit > 1:
            cots += [lax.ppermute(c, "mp", mp_pairs(bit)) for c in cots]
            bit //= 2

        up_all = lax.all_to_all(
            jnp.broadcast_to(adapter_up_panels[None], (n_dp,) + adapter_up_panels.shape),
            "dp", split_axis=0, concat_axis=0, tiled=True,
        ).reshape(tenants, rank, out_width)

        tenant_ids = jnp.arange(tenants, dtype=jnp.int32)
        list_location = jnp.sum(
            jnp.where(device_tenant_list[:, None] == tenant_ids[None, :], tenant_location_map[None, :], 0), axis=1
        )
        slot_ids = jnp.arange(listed, dtype=jnp.int32)
        row_slot = jnp.repeat(block_list_entry, block_rows)[:, None]

        def described(locations):
            holder = lax.div(locations, jnp.full_like(locations, stored))
            earlier = slot_ids[:, None] > slot_ids[None, :]
            turn = jnp.sum(jnp.where((holder[:, None] == holder[None, :]) & earlier, 1, 0), axis=1)
            cols = jnp.full_like(locations, X)
            return lax.div(holder, cols), lax.rem(holder, cols), locations - holder * stored, turn

        turns = jnp.arange(MOST, dtype=jnp.int32)

        def asked_panels(locations, places):
            row, col, panel, turn = described(locations)
            match = (
                (row[None, None, :] == places[:, None, None])
                & (col == my_col)[None, None, :]
                & (turn[None, None, :] == turns[None, :, None])
            )
            return jnp.sum(jnp.where(match, panel[None, None, :] + 1, 0), axis=2) - 1

        lists = [list_location] + [lax.ppermute(list_location, "dp", columns_on(X - d)) for d in range(1, X)]
        to_send = [None] + [jnp.maximum(asked_panels(lists[d], arriving), 0) for d in range(1, X)]
        to_place = [None] + [asked_panels(lists[X - d], leaving) for d in range(1, X)]
        row, col, panel, turn = described(list_location)
        in_row = lambda by_row: jnp.sum(
            jnp.where(row[:, None] == jnp.arange(Z, dtype=jnp.int32)[None, :], by_row[None, :], 0), axis=1
        )
        back, on = (my_col - col) & (X - 1), (col - my_col) & (X - 1)
        pick_where = jnp.where(
            back == 0,
            jnp.where(row <= my_row, my_row - row, Z - 1 + row - my_row),
            2 * Z - 1 + (back - 1) * Z + in_row(arrive_place),
        )
        pick_which = jnp.where(back == 0, panel, turn)
        leave_at = in_row(leave_place)
        share_at = jnp.where(
            on == 0, leave_at * stored + panel, Z * stored + ((on - 1) * Z + leave_at) * MOST + turn
        )

        products = base_products(mp_ref, tokens, value_weight, n_mp)
        from_core = [lax.ppermute(products[p], "mp", mp_pairs(1)) for p in range(1, n_mp, 2)]

        below, above = [adapter_down_panels], [adapter_down_panels]
        exchanged = []
        sent, placed = [], []
        up_sum = down_sum = None
        shares = None

        def leaving_sum(option, places, others):
            return add_arrivals(
                option, own_shares, [(c, placed[c]) for c in places], to_place[1:], others, stored, rank
            )

        for phase in range(2 * Z - 2):
            step, turn_out = phase + 1, phase - (Z - 2)
            if step < Z:
                below.append(lax.ppermute(below[-1], "dp", line(range(step - 1, Z - 1), 1)))
                above.append(lax.ppermute(above[-1], "dp", line(range(1, Z - step + 1), -1)))
            if phase < Z:
                sources = [below[0]] + below[1:phase + 1] + [None] * (Z - 1 - phase) + above[1:phase + 1]
                sources = [sources[i] for i in needed[phase]]
                at = jnp.broadcast_to(arriving_source[phase], (MOST,))
                exchanged.append(
                    [
                        lax.ppermute(pick_panels(sources, at, to_send[d][phase]), "dp", columns_on(d))
                        for d in range(1, X)
                    ]
                )
            if turn_out >= 0:
                placed.append([lax.ppermute(sent[d - 1][turn_out], "dp", columns_on(d)) for d in range(1, X)])
            if turn_out >= 1:
                arrived = [] if turn_out == 1 else [up_sum, down_sum]
                if turn_out <= Z // 2:
                    up_total = down_total = leaving_sum(up_option[:1], [turn_out - 1], arrived)
                else:
                    up_total = leaving_sum(
                        up_option[turn_out:turn_out + 1], leaving_options(turn_out, 1), arrived[:1]
                    )
                    down_total = leaving_sum(
                        down_option[turn_out:turn_out + 1], leaving_options(turn_out, -1), arrived[1:]
                    )
                up_sum = lax.ppermute(up_total, "dp", line(range(turn_out), 1))
                down_sum = lax.ppermute(down_total, "dp", line(range(Z - turn_out, Z), -1))

            results = ([below[-1], above[-1]] if step < Z else []) + ([up_sum, down_sum] if turn_out >= 1 else [])
            results += placed[-1] if turn_out >= 0 else []
            if phase == 0:
                results += [up_all]
            if phase == 1:
                results += from_core + cots + exchanged[0]
            if phase == 2:
                results += exchanged[1]
            results = after(results, [])
            if step < Z:
                below[-1], above[-1] = results[:2]
                results = results[2:]
            if turn_out >= 1:
                up_sum, down_sum = results[:2]
                results = results[2:]
            if turn_out >= 0:
                placed[-1], results = results[:X - 1], results[X - 1:]
            if phase == 0:
                up_part, own_ups = up_products(list_location, results[0], cotangent, row_slot, rank)
                up_parts = mp_parts(up_part)
                up_wide, own_shares, *flat_sent = share_panels(
                    share_at, up_parts, row_slot, tokens, [Z * stored] + [MOST] * (Z * (X - 1))
                )
                sent = [flat_sent[d * Z:(d + 1) * Z] for d in range(X - 1)]
            if phase == 1:
                from_core, results = results[:n_mp // 2], results[n_mp // 2:]
                cots, exchanged[0] = results[:n_mp // 2], results[n_mp // 2:]
                base = [products[p] + from_core[p // 2] for p in range(0, n_mp, 2)]
                while len(base) > 1:
                    count = len(base) // 2
                    got = [lax.ppermute(b.astype(BF16), "mp", mp_pairs(2 * count)) for b in base[count:]]
                    base = [b + g.astype(F32) for b, g in zip(base, got)]
            if phase == 2:
                exchanged[1] = results
        grad_a = leaving_sum(up_option[:1], [Z - 1], [up_sum, down_sum]).reshape(stored, rank, width)

        slot_down = pick_panels(
            below + above[1:] + [exchanged[k][d] for d in range(X - 1) for k in range(Z)], pick_where, pick_which
        ).reshape(listed * rank, width)

        down_parts = mp_parts(down_products(tokens, slot_down, row_slot, rank))
        down_wide, share_b = share_panels(list_location, down_parts, row_slot, cotangent, [tenants])
        values = (base[0] + matmul(down_wide, own_ups)).astype(BF16)

        all_cots = []
        for c in cots:
            all_cots += [c, lax.ppermute(c, "mp", mp_pairs(1))]
        token_gradient = input_gradient(mp_ref, all_cots, value_weight, up_wide, slot_down)

        back_b = lax.all_to_all(
            share_b.reshape(tenants, rank, out_width), "dp", split_axis=0, concat_axis=0, tiled=True
        ).reshape(n_dp, stored, rank, out_width)
        grad_b = jnp.sum(back_b.astype(F32), axis=0).astype(BF16)
        return (values, token_gradient, grad_a, grad_b)

    return shards


def solution(mesh):
    in_specs = (
        P("dp", "mp"),
        P("mp", None),
        P("dp", None, "mp"),
        P("dp", None, "mp"),
        P("dp", "mp"),
        P("dp"),
        P("dp"),
        P(),
    )
    out_specs = (P("dp", "mp"), P("dp", "mp"), P("dp", None, "mp"), P("dp", None, "mp"))
    shards = make_shards(mesh.shape["dp"], mesh.shape["mp"])
    return jax.shard_map(shards, mesh=mesh, in_specs=in_specs, out_specs=out_specs, check_vma=False)
```

time: 220 us -> 202 us (0.918); the launches traced: 216 us -> 201 us
  Pallas kernels: 0 us -> 62.1 us
  matrix products: 55.3 us -> 2.62 us
  between operations: 26 us -> 1.27 us
  starting transfers between devices: 35.2 us -> 59.1 us
  local copies, waits for them, and re-layouts: 29.6 us -> 16.2 us
  other arithmetic: 17.6 us -> 6.77 us
    pallas_call x0 -> x16, Pallas kernels: none -> 62.1 us  [the longest x5 16.3 us: add_arrivals(): pl.pallas_call(kernel, grid_spec=pltpu.PrefetchScalarGridSpec(num_scalar_...]
    dot_general x16 -> x1, matrix products: 55.3 us -> 2.62 us  [matmul(): return lax.dot_general(a, b, (dims, ((), ())), preferred_element_type=F32)]
    ppermute x20 -> x31, starting transfers between devices: 23.3 us -> 48 us  [the longest x3 14.5 us: shards(): up_sum = lax.ppermute(up_total, 'dp', line(range(turn_out), 1))]
    convert_element_type x9 -> x1, other arithmetic: 14.1 us -> 2.11 us  [shards(): b.astype(BF16)]
    all_to_all x1, waiting for transfers between devices: 0.01 us -> 11.9 us  [shards(): lax.all_to_all(jnp.broadcast_to(adapter_up_panels[None], (n_dp,) + adapte...]
    ppermute x20 -> x31, waiting for transfers between devices: 49.7 us -> 40.6 us  [the longest x4 16.5 us: shards(): lax.ppermute(pick_panels(sources, at, to_send[d][phase]), 'dp', columns_o...]
    gather x5 -> x0, local copies, waits for them, and re-layouts: 7.37 us -> none  [the longest x1 4.76 us: shards(): slot_down = held[held_row].reshape(listed * rank, width)]
    unnamed x35 -> x66, local copies, waits for them, and re-layouts: 12.4 us -> 9.33 us
  transfers between devices with their start and end apart: 24 -> 33, of which waited for: 7 -> 8; matrix products, arithmetic and copies ran while one was open for 46% -> 7% of each run, Pallas kernels for 0% -> 31%
where the time goes in v2:
time: 202 us; the launch traced here: 201 us
  Pallas kernels  62.1 us (31%)
  starting transfers between devices  59.1 us (29%)
  waiting for transfers between devices  52.5 us (26%)
  local copies, waits for them, and re-layouts  16.2 us (8%)
  other arithmetic  6.77 us (3%)
  matrix products  2.62 us (1%)
    ppermute x4, waiting for transfers between devices, shards(): lax.ppermute(pick_panels(sources, at, to_send[d][phase]), 'dp', columns_o...  16.5 us
    pallas_call x5, Pallas kernels, add_arrivals(): pl.pallas_call(kernel, grid_spec=pltpu.PrefetchScalarGridSpec(num_scalar_...  16.3 us
    ppermute x3, starting transfers between devices, shards(): up_sum = lax.ppermute(up_total, 'dp', line(range(turn_out), 1))  14.5 us
    all_to_all x1, waiting for transfers between devices, shards(): lax.all_to_all(jnp.broadcast_to(adapter_up_panels[None], (n_dp,) + adapte...  11.9 us
    ppermute x4, waiting for transfers between devices, shards(): lax.ppermute(sent[d - 1][turn_out], 'dp', columns_on(d))  11.2 us
    pallas_call x2, Pallas kernels, share_panels(): pl.pallas_call(kernel, grid_spec=pltpu.PrefetchScalarGridSpec(num_scalar_...  11.1 us
    pallas_call x1, Pallas kernels, input_gradient(): pl.pallas_call(kernel, grid_spec=pltpu.PrefetchScalarGridSpec(num_scalar_...  11 us
    unnamed x66, local copies, waits for them, and re-layouts  9.33 us
  transfers between devices with their start and end apart: 33, of which 8 were waited for; matrix products, arithmetic and copies ran while one was open for 7% of the time, Pallas kernels for 31%

profile of v2, /device:TPU:0, one launch (start us, length us, event | category | flops | bytes accessed | tf_op | source)
XLA Modules:
  0.0 200.6 jit_solution(7553746691298530860)
XLA Ops:
  0.6 5.8 %collective-permute-start = (bf16[3,64,2048]{2,1,0:T(8,128)(2,1)}, bf16[3,64,2048]{2,1,0:T(8,128)(2,1)}, u32[]{:S(2)}, u32[]{:S(2)}) collective-permute-start(bf16[3,64,2048]{2,1,0:T(8,128)(2,1)} %refs_0_.5), channel_id=1, source_target_pairs={{0,8},{4,12},{8,16},{12,20},{16,24},{20,28},{1,9},{5,13},{9,17},{1... | collective-permute-start | bytes 2359304 | tf_op jit(solution)/shard_map/ppermute | solution.py:445
  9.6 7.0 %all-to-all-start = ((bf16[8,3,64,256]{3,2,1,0:T(8,128)(2,1)}), bf16[8,3,64,256]{3,2,1,0:T(8,128)(2,1)S(1)}, u32[]{:S(2)}, u32[]{:S(2)}) async-start(bf16[8,3,64,256]{3,2,1,0:T(8,128)(2,1)} %broadcast_in_dim.112), calls=%async_computation | async-start | bytes 1572864 | tf_op jit(solution)/shard_map/all_to_all | solution.py:379
  16.6 8.4 %base_products.1 = (f32[1024,256]{1,0:T(8,128)S(1)}, f32[1024,256]{1,0:T(8,128)}, f32[1024,256]{1,0:T(8,128)S(1)}, f32[1024,256]{1,0:T(8,128)}) custom-call(s32[1]{0:T(128)} %bitcast.at_ref, bf16[1024,2048]{1,0:T(8,128)(2,1)} %second_ref.1, bf16[2048,1024]{1,0:T(8,128)(2,1)} %refs_7_.1, bf16[2048,1024]{1,0:T(8,128)(2,1)} %refs_7_.1, ...), custom_call_target="tpu_custom_call" | custom-call | flops 9349999616 | bytes 28900000 | tf_op jit(solution)/shard_map/base_products/pallas_call | solution.py:251
  32.7 11.9 %all-to-all-done = bf16[8,3,64,256]{3,2,1,0:T(8,128)(2,1)S(1)} async-done(((bf16[8,3,64,256]{3,2,1,0:T(8,128)(2,1)}), bf16[8,3,64,256]{3,2,1,0:T(8,128)(2,1)S(1)}, u32[]{:S(2)}, u32[]{:S(2)}) %all-to-all-start) | async-done | bytes 786464 | tf_op jit(solution)/shard_map/all_to_all | solution.py:379
  44.5 3.0 %up_products.1 = (f32[512,128]{1,0:T(8,128)S(1)}, bf16[512,256]{1,0:T(8,128)(2,1)S(1)}) custom-call(s32[8]{0:T(128)S(1)} %select_reduce_fusion.4.at_ref, bf16[24,64,256]{2,1,0:T(8,128)(2,1)S(1)} %bitcast.25, bf16[1024,256]{1,0:T(8,128)(2,1)} %refs_0_.6, s32[1024,1]{1,0:T(8,128)S(1)} %broadcast_in_dim_reshape.4.slot_ref.slot_a_ref.slot_b_ref), custom_call_target="tpu_custom_call" | custom-call | flops 2750000128 | bytes 8500000 | tf_op jit(solution)/shard_map/up_products/pallas_call | solution.py:97
  52.8 10.5 %collective-permute-done.8.refs_7_ = bf16[2,64,2048]{2,1,0:T(8,128)(2,1)S(1)} collective-permute-done((bf16[2,64,2048]{2,1,0:T(8,128)(2,1)S(1)}, bf16[2,64,2048]{2,1,0:T(8,128)(2,1)S(1)}, u32[]{:S(2)}, u32[]{:S(2)}) %collective-permute-start.8) | collective-permute-done | bytes 524320 | tf_op jit(solution)/shard_map/ppermute | solution.py:453
  70.6 2.3 %collective-permute-done.3.refs_1_.refs_5_ = bf16[3,64,2048]{2,1,0:T(8,128)(2,1)S(1)} collective-permute-done((bf16[3,64,2048]{2,1,0:T(8,128)(2,1)}, bf16[3,64,2048]{2,1,0:T(8,128)(2,1)S(1)}, u32[]{:S(2)}, u32[]{:S(2)}) %collective-permute-start.3) | collective-permute-done | bytes 786464 | tf_op jit(solution)/shard_map/ppermute | solution.py:446
  75.0 7.4 %share_panels.2 = (bf16[1024,512]{1,0:T(8,128)(2,1)S(1)}, bf16[768,2048]{1,0:T(8,128)(2,1)}, bf16[128,2048]{1,0:T(8,128)(2,1)S(1)}, bf16[128,2048]{1,0:T(8,128)(...) custom-call(s32[8]{0:T(128)S(1)} %get-tuple-element.90.at_ref, f32[512,128]{1,0:T(8,128)S(1)} %add.66.a_ref, ...), custom_call_target="tpu_custom_call" | custom-call | flops 8249999872 | bytes 25500000 | tf_op jit(solution)/shard_map/share_panels/pallas_call | solution.py:173
  88.3 9.9 %collective-permute-done.14.refs_2_.refs_3_ = bf16[128,2048]{1,0:T(8,128)(2,1)S(1)} collective-permute-done((bf16[128,2048]{1,0:T(8,128)(2,1)S(1)}, bf16[128,2048]{1,0:T(8,128)(2,1)S(1)}, u32[]{:S(2)}, u32[]{:S(2)}) %collective-permute-start.14) | collective-permute-done | bytes 524320 | tf_op jit(solution)/shard_map/ppermute | solution.py:458
  106.9 5.6 %collective-permute-start.22 = (bf16[192,2048]{1,0:T(8,128)(2,1)S(1)}, bf16[192,2048]{1,0:T(8,128)(2,1)S(1)}, u32[]{:S(2)}, u32[]{:S(2)}) collective-permute-start(bf16[192,2048]{1,0:T(8,128)(2,1)S(1)} %add_arrivals.5), channel_id=1, source_target_pairs={{0,8},{4,12},{1,9},{5,13},{2,10},{6,14},{3,11},{7,15}} | collective-permute-start | bytes 2359304 | tf_op jit(solution)/shard_map/ppermute | solution.py:470
  114.8 6.0 %collective-permute-done.17.refs_10_ = bf16[2,64,2048]{2,1,0:T(8,128)(2,1)} collective-permute-done((bf16[2,64,2048]{2,1,0:T(8,128)(2,1)}, bf16[2,64,2048]{2,1,0:T(8,128)(2,1)}, u32[]{:S(2)}, u32[]{:S(2)}) %collective-permute-start.17) | collective-permute-done | bytes 524320 | tf_op jit(solution)/shard_map/ppermute | solution.py:453
  122.8 5.4 %down_products.1 = f32[512,128]{1,0:T(8,128)S(1)} custom-call(bf16[1024,2048]{1,0:T(8,128)(2,1)} %second_ref.1, bf16[1024,2048]{1,0:T(8,128)(2,1)} %second_ref.1, bf16[512,2048]{1,0:T(8,128)(2,1)S(1)} %bitcast.26, s32[1024,1]{1,0:T(8,128)S(1)} %broadcast_in_dim_reshape.4.slot_ref.slot_a_ref.slot_b_ref, ...), custom_call_target="tpu_custom_call" | custom-call | flops 5059999744 | bytes 15639999 | tf_op jit(solution)/shard_map/down_products/pallas_call | solution.py:124
  130.3 3.2 %add_arrivals.6 = bf16[192,2048]{1,0:T(8,128)(2,1)} custom-call(s32[1]{0:T(128)} %bitcast.12.option_ref, s32[8]{0:T(128)S(1)} %sub.55.refs_0_, bf16[768,2048]{1,0:T(8,128)(2,1)S(1)} %copy-done.24, bf16[128,2048]{1,0:T(8,128)(2,1)S(1)} %collective-permute-done.24.refs_2_, bf16[192,2048]{1,0:T(8,128)(2,1)S(1)} %collective-permute-done.22.refs_3_, ...), custom_call_target="tpu_custom_call" | custom-call | flops 2750000128 | bytes 8500000 | tf_op jit(solution)/shard_map/add_arrivals/pallas_call | solution.py:225
  133.4 5.3 %collective-permute-start.25 = (bf16[192,2048]{1,0:T(8,128)(2,1)}, bf16[192,2048]{1,0:T(8,128)(2,1)}, u32[]{:S(2)}, u32[]{:S(2)}) collective-permute-start(bf16[192,2048]{1,0:T(8,128)(2,1)} %add_arrivals.6), channel_id=1, source_target_pairs={{0,8},{4,12},{8,16},{12,20},{1,9},{5,13},{9,17},{13,21},{2,10},{6,... | collective-permute-start | bytes 2359304 | tf_op jit(solution)/shard_map/ppermute | solution.py:470
  144.1 4.8 %collective-permute-done.19.b_ref = f32[512,128]{1,0:T(8,128)S(1)} collective-permute-done((f32[512,128]{1,0:T(8,128)S(1)}, f32[512,128]{1,0:T(8,128)S(1)}, u32[]{:S(2)}, u32[]{:S(2)}) %collective-permute-start.19) | collective-permute-done | bytes 262176 | tf_op jit(solution)/shard_map/ppermute | solution.py:367
  148.9 3.7 %share_panels.3 = (bf16[1024,512]{1,0:T(8,128)(2,1)S(1)}, bf16[1536,256]{1,0:T(8,128)(2,1)}) custom-call(s32[8]{0:T(128)S(1)} %select_reduce_fusion.4.at_ref, f32[512,128]{1,0:T(8,128)S(1)} %add.67.a_ref, f32[512,128]{1,0:T(8,128)S(1)} %collective-permute-done.19.b_ref, s32[1024,1]{1,0:T(8,128)S(1)} %broadcast_in_dim_reshape.4.slot_ref.slot_a_ref.slot_b_ref, ...), custom_call_target="tpu_custom_call" | custom-call | flops 8249999872 | bytes 25500000 | tf_op jit(solution)/shard_map/share_panels/pallas_call | solution.py:173
  152.6 4.2 %all-to-all-start.1 = ((bf16[24,64,256]{2,1,0:T(8,128)(2,1)}), bf16[24,64,256]{2,1,0:T(8,128)(2,1)}, u32[]{:S(2)}, u32[]{:S(2)}) async-start(bf16[24,64,256]{2,1,0:T(8,128)(2,1)} %bitcast.17), calls=%async_computation.1 | async-start | bytes 1572864 | tf_op jit(solution)/shard_map/all_to_all | solution.py:522
  163.1 4.0 %add_arrivals.7 = bf16[192,2048]{1,0:T(8,128)(2,1)S(1)} custom-call(s32[1]{0:T(128)} %bitcast.14.option_ref, s32[8]{0:T(128)S(1)} %sub.55.refs_0_, bf16[768,2048]{1,0:T(8,128)(2,1)S(1)} %copy-done.25, bf16[768,2048]{1,0:T(8,128)(2,1)S(1)} %copy-done.25, bf16[128,2048]{1,0:T(8,128)(2,1)S(1)} %copy-done.14, bf16[128,2048]{1,0:T(8,128)(2,1)} %collective-permute-done.27.refs_4_, ...), custom_call_target="tpu_custom_call" | custom-call | flops 2750000128 | bytes 8500000 | tf_op jit(solution)/shard_map/add_arrivals/pallas_call | solution.py:225
  167.1 3.6 %collective-permute-start.28 = (bf16[192,2048]{1,0:T(8,128)(2,1)S(1)}, bf16[192,2048]{1,0:T(8,128)(2,1)S(1)}, u32[]{:S(2)}, u32[]{:S(2)}) collective-permute-start(bf16[192,2048]{1,0:T(8,128)(2,1)S(1)} %add_arrivals.7), channel_id=1, source_target_pairs={{0,8},{4,12},{8,16},{12,20},{16,24},{20,28},{1,9},{5,13},{9,17},{1... | collective-permute-start | bytes 2359304 | tf_op jit(solution)/shard_map/ppermute | solution.py:470
  170.8 4.0 %add_arrivals.8 = bf16[192,2048]{1,0:T(8,128)(2,1)S(1)} custom-call(s32[1]{0:T(128)} %bitcast.15.option_ref, s32[8]{0:T(128)S(1)} %sub.55.refs_0_, bf16[768,2048]{1,0:T(8,128)(2,1)S(1)} %copy-done.26, bf16[768,2048]{1,0:T(8,128)(2,1)S(1)} %copy-done.26, bf16[128,2048]{1,0:T(8,128)(2,1)S(1)} %copy-done.14, bf16[128,2048]{1,0:T(8,128)(2,1)} %collective-permute-done.27.refs_4_, ...), custom_call_target="tpu_custom_call" | custom-call | flops 2750000128 | bytes 8500000 | tf_op jit(solution)/shard_map/add_arrivals/pallas_call | solution.py:225
  176.2 11.0 %input_gradient.1 = bf16[1024,2048]{1,0:T(8,128)(2,1)} custom-call(s32[1]{0:T(128)} %bitcast.at_ref, bf16[1024,512]{1,0:T(8,128)(2,1)S(1)} %copy-done.29, bf16[512,2048]{1,0:T(8,128)(2,1)S(1)} %bitcast.27, bf16[1024,256]{1,0:T(8,128)(2,1)} %refs_0_.6, bf16[1024,256]{1,0:T(8,128)(2,1)} %collective-permute-done.20.refs_1_, ...), custom_call_target="tpu_custom_call" | custom-call | flops 12099999744 | bytes 37400000 | tf_op jit(solution)/shard_map/input_gradient/pallas_call | solution.py:281
  187.2 2.6 %add_convert_fusion = bf16[1024,256]{1,0:T(8,128)(2,1)} fusion(bf16[1024,256]{1,0:T(8,128)(2,1)S(1)} %collective-permute-done.9, f32[1024,256]{1,0:T(8,128)S(1)} %get-tuple-element.41, f32[1024,256]{1,0:T(8,128)} %collective-permute-done.4, bf16[1024,512]{1,0:T(8,128)(2,1)S(1)} %get-tuple-element.58, bf16[512,256]{1,0:T(8,128)(2,1)S(1)} %copy-done.1), kind=kOutput, calls=%fused_computation | convolution fusion | flops 269746176 | bytes 4456448 | tf_op jit(solution)/shard_map/dot_general | solution.py:39
  189.8 5.7 %collective-permute-done.29.refs_4_ = bf16[192,2048]{1,0:T(8,128)(2,1)S(1)} collective-permute-done((bf16[192,2048]{1,0:T(8,128)(2,1)S(1)}, bf16[192,2048]{1,0:T(8,128)(2,1)S(1)}, u32[]{:S(2)}, u32[]{:S(2)}) %collective-permute-start.29) | collective-permute-done | bytes 786464 | tf_op jit(solution)/shard_map/ppermute | solution.py:471
  195.5 3.2 %add_arrivals.9 = bf16[192,2048]{1,0:T(8,128)(2,1)} custom-call(s32[1]{0:T(128)} %bitcast.12.option_ref, s32[8]{0:T(128)S(1)} %sub.55.refs_0_, bf16[768,2048]{1,0:T(8,128)(2,1)S(1)} %copy-done.27, bf16[128,2048]{1,0:T(8,128)(2,1)S(1)} %collective-permute-done.30.refs_2_, bf16[192,2048]{1,0:T(8,128)(2,1)S(1)} %collective-permute-done.28.refs_3_, ...), custom_call_target="tpu_custom_call" | custom-call | flops 2750000128 | bytes 8500000 | tf_op jit(solution)/shard_map/add_arrivals/pallas_call | solution.py:225
  (154 shorter events, 61.0 us)
Async XLA Ops:
  0.6 32.0 %collective-permute-start = (bf16[3,64,2048]{2,1,0:T(8,128)(2,1)}, bf16[3,64,2048]{2,1,0:T(8,128)(2,1)}, u32[]{:S(2)}, u32[]{:S(2)}) collective-permute-start(bf16[3,64,2048]{2,1,0:T(8,128)(2,1)} %refs_0_.5), channel_id=1, source_target_pairs={{0,8},{4,12},{8,16},{12,20},{16,24},{20,28},{1,9},{5,13},{9,17},{1... | collective-permute-start | bytes 2359304 | tf_op jit(solution)/shard_map/ppermute | solution.py:445
  6.4 26.2 %collective-permute-start.1 = (bf16[3,64,2048]{2,1,0:T(8,128)(2,1)}, bf16[3,64,2048]{2,1,0:T(8,128)(2,1)}, u32[]{:S(2)}, u32[]{:S(2)}) collective-permute-start(bf16[3,64,2048]{2,1,0:T(8,128)(2,1)} %refs_0_.5), channel_id=1, source_target_pairs={{8,0},{12,4},{16,8},{20,12},{24,16},{28,20},{9,1},{13,5},{17,9},{2... | collective-permute-start | bytes 2359304 | tf_op jit(solution)/shard_map/ppermute | solution.py:446
  9.6 35.0 %all-to-all-start = ((bf16[8,3,64,256]{3,2,1,0:T(8,128)(2,1)}), bf16[8,3,64,256]{3,2,1,0:T(8,128)(2,1)S(1)}, u32[]{:S(2)}, u32[]{:S(2)}) async-start(bf16[8,3,64,256]{3,2,1,0:T(8,128)(2,1)} %broadcast_in_dim.112), calls=%async_computation | async-start | bytes 1572864 | tf_op jit(solution)/shard_map/all_to_all | solution.py:379
  25.0 44.1 %collective-permute-start.4 = (f32[1024,256]{1,0:T(8,128)}, f32[1024,256]{1,0:T(8,128)}, u32[]{:S(2)}, u32[]{:S(2)}) collective-permute-start(f32[1024,256]{1,0:T(8,128)} %get-tuple-element.44), channel_id=1, source_target_pairs={{0,1},{1,0},{2,3},{3,2},{4,5},{5,4},{6,7},{7,6},{8,9},{9,8},{10,11... | collective-permute-start | bytes 3145736 | tf_op jit(solution)/shard_map/ppermute | solution.py:429
  25.0 45.6 %collective-permute-start.5 = (f32[1024,256]{1,0:T(8,128)}, f32[1024,256]{1,0:T(8,128)}, u32[]{:S(2)}, u32[]{:S(2)}) collective-permute-start(f32[1024,256]{1,0:T(8,128)} %get-tuple-element.45), channel_id=1, source_target_pairs={{0,1},{1,0},{2,3},{3,2},{4,5},{5,4},{6,7},{7,6},{8,9},{9,8},{10,11... | collective-permute-start | bytes 3145736 | tf_op jit(solution)/shard_map/ppermute | solution.py:429
  29.8 20.7 %collective-permute-start.6 = (bf16[1024,256]{1,0:T(8,128)(2,1)}, bf16[1024,256]{1,0:T(8,128)(2,1)}, u32[]{:S(2)}, u32[]{:S(2)}) collective-permute-start(bf16[1024,256]{1,0:T(8,128)(2,1)} %refs_0_.6), channel_id=1, source_target_pairs={{0,2},{1,3},{2,0},{3,1},{4,6},{5,7},{6,4},{7,5},{8,10},{9,11},{10,... | collective-permute-start | bytes 1572872 | tf_op jit(solution)/shard_map/ppermute | solution.py:376
  50.5 20.1 %collective-permute-start.2 = (bf16[3,64,2048]{2,1,0:T(8,128)(2,1)}, bf16[3,64,2048]{2,1,0:T(8,128)(2,1)S(1)}, u32[]{:S(2)}, u32[]{:S(2)}) collective-permute-start(bf16[3,64,2048]{2,1,0:T(8,128)(2,1)} %collective-permute-done.refs_0_.refs_1_), channel_id=1, source_target_pairs={{8,16},{12,20},{16,24},{20,28},{9,17},{13,21},{17,25},{21,29},{10,... | collective-permute-start | bytes 2359304 | tf_op jit(solution)/shard_map/ppermute | solution.py:445
  51.2 21.7 %collective-permute-start.3 = (bf16[3,64,2048]{2,1,0:T(8,128)(2,1)}, bf16[3,64,2048]{2,1,0:T(8,128)(2,1)S(1)}, u32[]{:S(2)}, u32[]{:S(2)}) collective-permute-start(bf16[3,64,2048]{2,1,0:T(8,128)(2,1)} %collective-permute-done.1.refs_1_.refs_2_.refs_4_), channel_id=1, source_target_pairs={{8,0},{12,4},{16,8},{20,12},{9,1},{13,5},{17,9},{21,13},{10,2},{14... | collective-permute-start | bytes 2359304 | tf_op jit(solution)/shard_map/ppermute | solution.py:446
  69.1 18.5 %collective-permute-start.15 = (bf16[2,64,2048]{2,1,0:T(8,128)(2,1)S(1)}, bf16[2,64,2048]{2,1,0:T(8,128)(2,1)S(1)}, u32[]{:S(2)}, u32[]{:S(2)}) collective-permute-start(bf16[2,64,2048]{2,1,0:T(8,128)(2,1)S(1)} %pick_panels.6), channel_id=1, source_target_pairs={{0,4},{4,0},{8,12},{12,8},{16,20},{20,16},{24,28},{28,24},{1,5},{5... | collective-permute-start | bytes 1572872 | tf_op jit(solution)/shard_map/ppermute | solution.py:453
  73.0 26.0 %collective-permute-start.10 = (bf16[3,64,2048]{2,1,0:T(8,128)(2,1)S(1)}, bf16[3,64,2048]{2,1,0:T(8,128)(2,1)S(1)}, u32[]{:S(2)}, u32[]{:S(2)}) collective-permute-start(bf16[3,64,2048]{2,1,0:T(8,128)(2,1)S(1)} %collective-permute-done.2.refs_0_.refs_2_), channel_id=1, source_target_pairs={{16,24},{20,28},{17,25},{21,29},{18,26},{22,30},{19,27},{23,31}} | collective-permute-start | bytes 2359304 | tf_op jit(solution)/shard_map/ppermute | solution.py:445
  73.7 25.3 %collective-permute-start.11 = (bf16[3,64,2048]{2,1,0:T(8,128)(2,1)S(1)}, bf16[3,64,2048]{2,1,0:T(8,128)(2,1)S(1)}, u32[]{:S(2)}, u32[]{:S(2)}) collective-permute-start(bf16[3,64,2048]{2,1,0:T(8,128)(2,1)S(1)} %collective-permute-done.3.refs_1_.refs_5_), channel_id=1, source_target_pairs={{8,0},{12,4},{9,1},{13,5},{10,2},{14,6},{11,3},{15,7}} | collective-permute-start | bytes 2359304 | tf_op jit(solution)/shard_map/ppermute | solution.py:446
  86.0 28.8 %collective-permute-start.16 = (bf16[2,64,2048]{2,1,0:T(8,128)(2,1)}, bf16[2,64,2048]{2,1,0:T(8,128)(2,1)}, u32[]{:S(2)}, u32[]{:S(2)}) collective-permute-start(bf16[2,64,2048]{2,1,0:T(8,128)(2,1)} %pick_panels.7), channel_id=1, source_target_pairs={{0,4},{4,0},{8,12},{12,8},{16,20},{20,16},{24,28},{28,24},{1,5},{5... | collective-permute-start | bytes 1572872 | tf_op jit(solution)/shard_map/ppermute | solution.py:453
  101.2 19.6 %collective-permute-start.17 = (bf16[2,64,2048]{2,1,0:T(8,128)(2,1)}, bf16[2,64,2048]{2,1,0:T(8,128)(2,1)}, u32[]{:S(2)}, u32[]{:S(2)}) collective-permute-start(bf16[2,64,2048]{2,1,0:T(8,128)(2,1)} %pick_panels.8), channel_id=1, source_target_pairs={{0,4},{4,0},{8,12},{12,8},{16,20},{20,16},{24,28},{28,24},{1,5},{5... | collective-permute-start | bytes 1572872 | tf_op jit(solution)/shard_map/ppermute | solution.py:453
  106.9 23.4 %collective-permute-start.22 = (bf16[192,2048]{1,0:T(8,128)(2,1)S(1)}, bf16[192,2048]{1,0:T(8,128)(2,1)S(1)}, u32[]{:S(2)}, u32[]{:S(2)}) collective-permute-start(bf16[192,2048]{1,0:T(8,128)(2,1)S(1)} %add_arrivals.5), channel_id=1, source_target_pairs={{0,8},{4,12},{1,9},{5,13},{2,10},{6,14},{3,11},{7,15}} | collective-permute-start | bytes 2359304 | tf_op jit(solution)/shard_map/ppermute | solution.py:470
  128.3 28.5 %collective-permute-start.27 = (bf16[128,2048]{1,0:T(8,128)(2,1)}, bf16[128,2048]{1,0:T(8,128)(2,1)}, u32[]{:S(2)}, u32[]{:S(2)}) collective-permute-start(bf16[128,2048]{1,0:T(8,128)(2,1)} %get-tuple-element.69), channel_id=1, source_target_pairs={{0,4},{4,0},{8,12},{12,8},{16,20},{20,16},{24,28},{28,24},{1,5},{5... | collective-permute-start | bytes 1572872 | tf_op jit(solution)/shard_map/ppermute | solution.py:458
  130.2 44.6 %collective-permute-start.20 = (bf16[1024,256]{1,0:T(8,128)(2,1)}, bf16[1024,256]{1,0:T(8,128)(2,1)}, u32[]{:S(2)}, u32[]{:S(2)}) collective-permute-start(bf16[1024,256]{1,0:T(8,128)(2,1)} %refs_0_.6), channel_id=1, source_target_pairs={{0,1},{1,0},{2,3},{3,2},{4,5},{5,4},{6,7},{7,6},{8,9},{9,8},{10,11... | collective-permute-start | bytes 1572872 | tf_op jit(solution)/shard_map/ppermute | solution.py:519
  133.4 25.2 %collective-permute-start.25 = (bf16[192,2048]{1,0:T(8,128)(2,1)}, bf16[192,2048]{1,0:T(8,128)(2,1)}, u32[]{:S(2)}, u32[]{:S(2)}) collective-permute-start(bf16[192,2048]{1,0:T(8,128)(2,1)} %add_arrivals.6), channel_id=1, source_target_pairs={{0,8},{4,12},{8,16},{12,20},{1,9},{5,13},{9,17},{13,21},{2,10},{6,... | collective-permute-start | bytes 2359304 | tf_op jit(solution)/shard_map/ppermute | solution.py:470
  138.7 21.5 %collective-permute-start.26 = (bf16[192,2048]{1,0:T(8,128)(2,1)}, bf16[192,2048]{1,0:T(8,128)(2,1)}, u32[]{:S(2)}, u32[]{:S(2)}) collective-permute-start(bf16[192,2048]{1,0:T(8,128)(2,1)} %add_arrivals.6), channel_id=1, source_target_pairs={{16,8},{20,12},{24,16},{28,20},{17,9},{21,13},{25,17},{29,21},{18,... | collective-permute-start | bytes 2359304 | tf_op jit(solution)/shard_map/ppermute | solution.py:471
  148.9 27.3 %collective-permute-start.21 = (bf16[1024,256]{1,0:T(8,128)(2,1)}, bf16[1024,256]{1,0:T(8,128)(2,1)}, u32[]{:S(2)}, u32[]{:S(2)}) collective-permute-start(bf16[1024,256]{1,0:T(8,128)(2,1)} %collective-permute-done.6.refs_2_), channel_id=1, source_target_pairs={{0,1},{1,0},{2,3},{3,2},{4,5},{5,4},{6,7},{7,6},{8,9},{9,8},{10,11... | collective-permute-start | bytes 1572872 | tf_op jit(solution)/shard_map/ppermute | solution.py:519
  152.6 46.2 %all-to-all-start.1 = ((bf16[24,64,256]{2,1,0:T(8,128)(2,1)}), bf16[24,64,256]{2,1,0:T(8,128)(2,1)}, u32[]{:S(2)}, u32[]{:S(2)}) async-start(bf16[24,64,256]{2,1,0:T(8,128)(2,1)} %bitcast.17), calls=%async_computation.1 | async-start | bytes 1572864 | tf_op jit(solution)/shard_map/all_to_all | solution.py:522
  156.8 33.0 %collective-permute-start.30 = (bf16[128,2048]{1,0:T(8,128)(2,1)S(1)}, bf16[128,2048]{1,0:T(8,128)(2,1)S(1)}, u32[]{:S(2)}, u32[]{:S(2)}) collective-permute-start(bf16[128,2048]{1,0:T(8,128)(2,1)S(1)} %get-tuple-element.73), channel_id=1, source_target_pairs={{0,4},{4,0},{8,12},{12,8},{16,20},{20,16},{24,28},{28,24},{1,5},{5... | collective-permute-start | bytes 1572872 | tf_op jit(solution)/shard_map/ppermute | solution.py:458
  158.7 28.5 %collective-permute-start.9 = (bf16[1024,256]{1,0:T(8,128)(2,1)}, bf16[1024,256]{1,0:T(8,128)(2,1)S(1)}, u32[]{:S(2)}, u32[]{:S(2)}) collective-permute-start(bf16[1024,256]{1,0:T(8,128)(2,1)} %add_convert_fusion.1), channel_id=1, source_target_pairs={{0,2},{1,3},{2,0},{3,1},{4,6},{5,7},{6,4},{7,5},{8,10},{9,11},{10,... | collective-permute-start | bytes 1572872 | tf_op jit(solution)/shard_map/ppermute | solution.py:503
  167.1 22.7 %collective-permute-start.28 = (bf16[192,2048]{1,0:T(8,128)(2,1)S(1)}, bf16[192,2048]{1,0:T(8,128)(2,1)S(1)}, u32[]{:S(2)}, u32[]{:S(2)}) collective-permute-start(bf16[192,2048]{1,0:T(8,128)(2,1)S(1)} %add_arrivals.7), channel_id=1, source_target_pairs={{0,8},{4,12},{8,16},{12,20},{16,24},{20,28},{1,9},{5,13},{9,17},{1... | collective-permute-start | bytes 2359304 | tf_op jit(solution)/shard_map/ppermute | solution.py:470
  174.8 20.7 %collective-permute-start.29 = (bf16[192,2048]{1,0:T(8,128)(2,1)S(1)}, bf16[192,2048]{1,0:T(8,128)(2,1)S(1)}, u32[]{:S(2)}, u32[]{:S(2)}) collective-permute-start(bf16[192,2048]{1,0:T(8,128)(2,1)S(1)} %add_arrivals.8), channel_id=1, source_target_pairs={{8,0},{12,4},{16,8},{20,12},{24,16},{28,20},{9,1},{13,5},{17,9},{2... | collective-permute-start | bytes 2359304 | tf_op jit(solution)/shard_map/ppermute | solution.py:471
  (42 other events, 350.8 us)

commit v3 on v2

v3 whole, which is shorter than its diff:
```python
import jax
import jax.numpy as jnp
from jax import lax
from jax.experimental import pallas as pl
from jax.experimental.pallas import tpu as pltpu
from jax.sharding import PartitionSpec as P

F32 = jnp.float32
BF16 = jnp.bfloat16


def ring_order(n):
    cols = 1
    while 2 * (2 * cols) ** 2 <= n:
        cols *= 2
    rows = n // cols
    if cols < 2 or rows % 2 or rows * cols != n:
        return list(range(n))
    walk = [z * cols for z in range(rows)]
    for step, z in enumerate(reversed(range(rows))):
        across = range(1, cols) if step % 2 == 0 else reversed(range(1, cols))
        walk += [z * cols + x for x in across]
    return walk


def lasting(us):
    return pl.CostEstimate(flops=int(us * 0.05 * 1.1e9), bytes_accessed=int(us * 0.05 * 3.4e6), transcendentals=0)


def matmul(a, b, dims=((1,), (0,))):
    return lax.dot_general(a, b, (dims, ((), ())), preferred_element_type=F32)


def after(values):
    return list(lax.optimization_barrier(tuple(values)))


def pick_panels(sources, halves, where, which):
    slots = where.shape[0]
    _, rank, width = sources[0].shape
    n, cut = len(sources), width // 2

    def kernel(where_ref, which_ref, *refs):
        srcs, (left, right), dst, sem = refs[:n], refs[n:n + 2], refs[n + 2], refs[n + 3]

        @pl.loop(0, slots)
        def _(s):
            source, panel = where_ref[s], which_ref[s]
            for b in range(n):

                @pl.when(source == b)
                def _(b=b):
                    pltpu.make_async_copy(srcs[b].at[panel], dst.at[s], sem).start()

            @pl.when(source == n)
            def _():
                pltpu.make_async_copy(left.at[panel], dst.at[s, :, pl.ds(0, cut)], sem).start()
                pltpu.make_async_copy(right.at[panel], dst.at[s, :, pl.ds(cut, cut)], sem).start()

        pltpu.make_async_copy(dst, dst, sem).wait()

    smem = pl.BlockSpec(memory_space=pltpu.SMEM)
    return pl.pallas_call(
        kernel,
        in_specs=[smem, smem] + [pl.BlockSpec(memory_space=pl.ANY)] * (n + 2),
        out_specs=pl.BlockSpec(memory_space=pltpu.VMEM),
        out_shape=jax.ShapeDtypeStruct((slots, rank, width), BF16),
        scratch_shapes=[pltpu.SemaphoreType.DMA],
        compiler_params=pltpu.CompilerParams(vmem_limit_bytes=32 * 1024 * 1024),
        cost_estimate=lasting(2.5),
        name="pick_panels",
    )(where, which, *sources, *halves)


def by_slot(wide, slots, rank):
    low = jnp.zeros((wide.shape[0], rank), F32)
    for s in range(wide.shape[1] // rank):
        low += jnp.where(slots == s, wide[:, s * rank:(s + 1) * rank], 0.0)
    return low


def up_products(locations, up_all, cotangent, row_slot, rank):
    rows, out_width = cotangent.shape
    listed = locations.shape[0]

    def kernel(at_ref, up_ref, cot_ref, slot_ref, part_ref, own_ref):
        for s in range(listed):
            own_ref[s * rank:(s + 1) * rank, :] = up_ref[at_ref[s]]
        low = by_slot(matmul(cot_ref[...], own_ref[...], ((1,), (1,))), slot_ref[...], rank)
        part_ref[...] = jnp.concatenate([low[:rows // 2], low[rows // 2:]], axis=1)

    vmem = pl.BlockSpec(memory_space=pltpu.VMEM)
    return pl.pallas_call(
        kernel,
        in_specs=[pl.BlockSpec(memory_space=pltpu.SMEM), vmem, vmem, vmem],
        out_specs=[vmem, vmem],
        out_shape=[
            jax.ShapeDtypeStruct((rows // 2, 2 * rank), F32),
            jax.ShapeDtypeStruct((listed * rank, out_width), BF16),
        ],
        compiler_params=pltpu.CompilerParams(vmem_limit_bytes=48 * 1024 * 1024),
        cost_estimate=lasting(2.5),
        name="up_products",
    )(locations, up_all, cotangent, row_slot)


def down_products(tokens, slot_down, row_slot, rank):
    rows, width = tokens.shape
    tile = min(256, rows // 2)
    steps = rows // 2 // tile

    def kernel(first_ref, second_ref, down_ref, slot_a_ref, slot_b_ref, part_ref):
        halves = [
            by_slot(matmul(tok[...], down_ref[...], ((1,), (1,))), slot[...], rank)
            for tok, slot in ((first_ref, slot_a_ref), (second_ref, slot_b_ref))
        ]
        part_ref[...] = jnp.concatenate(halves, axis=1)

    upper, lower = lambda i: (i, 0), lambda i: (i + steps, 0)
    return pl.pallas_call(
        kernel,
        grid=(steps,),
        in_specs=[
            pl.BlockSpec((tile, width), upper),
            pl.BlockSpec((tile, width), lower),
            pl.BlockSpec(slot_down.shape, lambda i: (0, 0)),
            pl.BlockSpec((tile, 1), upper),
            pl.BlockSpec((tile, 1), lower),
        ],
        out_specs=pl.BlockSpec((tile, 2 * rank), upper),
        out_shape=jax.ShapeDtypeStruct((rows // 2, 2 * rank), F32),
        compiler_params=pltpu.CompilerParams(vmem_limit_bytes=48 * 1024 * 1024),
        cost_estimate=lasting(4.6),
        name="down_products",
    )(tokens, tokens, slot_down, row_slot, row_slot)


def share_panels(positions, parts, row_slot, other, panels, far=None):
    half_rows, pair = parts[0].shape
    rank, rows = pair // 2, 2 * half_rows
    listed, width = positions.shape[0], other.shape[1]
    tile = min(512, width // 2 if far else width)
    steps = width // tile

    def kernel(at_ref, a_ref, b_ref, slot_ref, other_ref, dense_ref, wide_ref, *refs):
        turned_ref = refs[-1]
        step = pl.program_id(0)

        @pl.when(step == 0)
        def _():
            both = a_ref[...] + b_ref[...]
            low = jnp.concatenate([both[:, :rank], both[:, rank:]], axis=0).astype(BF16)
            column = lax.broadcasted_iota(jnp.int32, (rank, listed * rank), 1)
            eye = (column % rank == lax.broadcasted_iota(jnp.int32, (rank, listed * rank), 0)).astype(BF16)
            group = lax.broadcasted_iota(jnp.int32, (rows, listed * rank), 1) // rank
            wide = jnp.where(group == slot_ref[...], matmul(low, eye), 0.0)
            wide_ref[...] = wide.astype(BF16)
            turned_ref[...] = wide.T.astype(BF16)

        shares = matmul(turned_ref[...], other_ref[...]).astype(BF16)
        dense_ref[...] = jnp.zeros(dense_ref.shape, BF16)
        for s in range(listed):
            dense_ref[pl.ds(pl.multiple_of(at_ref[s] * rank, rank), rank), :] = shares[s * rank:(s + 1) * rank]
        if far:
            left_ref, right_ref = refs[:2]

            @pl.when(step < steps // 2)
            def _():
                left_ref[...] = dense_ref[far[0] * rank:far[1] * rank, :]

            @pl.when(step >= steps // 2)
            def _():
                right_ref[...] = dense_ref[far[0] * rank:far[1] * rank, :]

    whole = lambda a: pl.BlockSpec(a.shape, lambda i, at: (0, 0))
    out_specs = [
        pl.BlockSpec((panels * rank, tile), lambda i, at: (0, i)),
        pl.BlockSpec((rows, listed * rank), lambda i, at: (0, 0)),
    ]
    out_shape = [
        jax.ShapeDtypeStruct((panels * rank, width), BF16),
        jax.ShapeDtypeStruct((rows, listed * rank), BF16),
    ]
    if far:
        tall = (far[1] - far[0]) * rank
        out_specs += [
            pl.BlockSpec((tall, tile), lambda i, at: (0, jnp.minimum(i, steps // 2 - 1))),
            pl.BlockSpec((tall, tile), lambda i, at: (0, jnp.maximum(i - steps // 2, 0))),
        ]
        out_shape += [jax.ShapeDtypeStruct((tall, width // 2), BF16)] * 2
    return pl.pallas_call(
        kernel,
        grid_spec=pltpu.PrefetchScalarGridSpec(
            num_scalar_prefetch=1,
            grid=(steps,),
            in_specs=[whole(parts[0]), whole(parts[1]), whole(row_slot), pl.BlockSpec((rows, tile), lambda i, at: (0, i))],
            out_specs=out_specs,
            scratch_shapes=[pltpu.VMEM((listed * rank, rows), BF16)],
        ),
        out_shape=out_shape,
        compiler_params=pltpu.CompilerParams(vmem_limit_bytes=48 * 1024 * 1024),
        cost_estimate=lasting(7.5),
        name="share_panels",
    )(positions, *parts, row_slot, other)


def add_panels(first, *others):
    rows, width = others[0].shape
    tile = min(512, width)

    def kernel(*refs):
        total = refs[0][...].astype(F32)
        for ref in refs[1:-1]:
            total += ref[...].astype(F32)
        refs[-1][...] = total.astype(BF16)

    spec = pl.BlockSpec((rows, tile), lambda i: (0, i))
    return pl.pallas_call(
        kernel,
        grid=(width // tile,),
        in_specs=[spec] * (1 + len(others)),
        out_specs=spec,
        out_shape=jax.ShapeDtypeStruct((rows, width), BF16),
        cost_estimate=lasting(260.0),
        name="add_panels",
    )(first, *others)


def base_products(mp_at, tokens, weight, count):
    rows, width = tokens.shape
    cols = weight.shape[1] // count
    tile = min(256, rows)

    def kernel(at_ref, tok_ref, *refs):
        weights, outs = refs[:count], refs[count:]
        for p in range(1, count, 2):
            outs[-1][:, p // 2 * cols:(p // 2 + 1) * cols] = matmul(tok_ref[...], weights[p][...])
        for p in range(0, count, 2):
            outs[p // 2][...] = matmul(tok_ref[...], weights[p][...])

    return pl.pallas_call(
        kernel,
        grid_spec=pltpu.PrefetchScalarGridSpec(
            num_scalar_prefetch=1,
            grid=(rows // tile,),
            in_specs=[pl.BlockSpec((tile, width), lambda i, m: (i, 0))]
            + [pl.BlockSpec((width, cols), lambda i, m, p=p: (0, m[0] ^ p)) for p in range(count)],
            out_specs=[pl.BlockSpec((tile, cols), lambda i, m: (i, 0))] * (count // 2)
            + [pl.BlockSpec((tile, count // 2 * cols), lambda i, m: (i, 0))],
        ),
        out_shape=[jax.ShapeDtypeStruct((rows, cols), F32)] * (count // 2)
        + [jax.ShapeDtypeStruct((rows, count // 2 * cols), F32)],
        compiler_params=pltpu.CompilerParams(vmem_limit_bytes=48 * 1024 * 1024),
        cost_estimate=lasting(170.0),
        name="base_products",
    )(mp_at, tokens, *([weight] * count))


def input_gradient(mp_at, cots, weight, up_wide, slot_down):
    rows = up_wide.shape[0]
    width = slot_down.shape[1]
    count = len(cots)
    cols = weight.shape[1] // count
    tile = min(256, rows)

    def kernel(at_ref, up_ref, slot_ref, *refs):
        total = matmul(up_ref[...], slot_ref[...])
        for c, w in zip(refs[:count], refs[count:2 * count]):
            total += matmul(c[...], w[...], ((1,), (1,)))
        refs[2 * count][...] = total.astype(BF16)

    by_row = lambda a: pl.BlockSpec((tile, a.shape[1]), lambda i, m: (i, 0))
    return pl.pallas_call(
        kernel,
        grid_spec=pltpu.PrefetchScalarGridSpec(
            num_scalar_prefetch=1,
            grid=(rows // tile,),
            in_specs=[by_row(up_wide), pl.BlockSpec(slot_down.shape, lambda i, m: (0, 0))]
            + [by_row(c) for c in cots]
            + [pl.BlockSpec((width, cols), lambda i, m, p=p: (0, m[0] ^ p)) for p in range(count)],
            out_specs=pl.BlockSpec((tile, width), lambda i, m: (i, 0)),
        ),
        out_shape=jax.ShapeDtypeStruct((rows, width), BF16),
        compiler_params=pltpu.CompilerParams(vmem_limit_bytes=48 * 1024 * 1024),
        cost_estimate=lasting(11.0),
        name="input_gradient",
    )(mp_at, up_wide, slot_down, *cots, *([weight] * count))


def make_shards(n_dp, n_mp):
    order = ring_order(n_dp)
    place = [order.index(e) for e in range(n_dp)]
    forward = [(order[i], order[(i + 1) % n_dp]) for i in range(n_dp)]
    backward = [(b, a) for a, b in forward]
    half_way = n_dp // 2

    def tables(stored):
        rows = []
        for e in range(n_dp):
            arrives, ring = [], []
            for owner in range(n_dp):
                ahead = (place[owner] - place[e]) % n_dp
                arrives += [n_dp - 1 if ahead == half_way else ahead - (ahead > half_way)] * stored
                ring += [ahead * stored + j for j in range(stored)]
            rows.append([arrives, ring])
        return rows

    def mp_pairs(bit):
        return [(i, i ^ bit) for i in range(n_mp)]

    def shards(
        tokens,
        value_weight,
        adapter_down_panels,
        adapter_up_panels,
        cotangent,
        block_list_entry,
        device_tenant_list,
        tenant_location_map,
    ):
        rows, width = tokens.shape
        stored, rank, _ = adapter_down_panels.shape
        out_width = adapter_up_panels.shape[2]
        blocks = block_list_entry.shape[0]
        block_rows = rows // blocks
        listed = device_tenant_list.shape[0]
        tenants = tenant_location_map.shape[0]
        half = width // 2

        dp_at = lax.axis_index("dp")
        mp_at = lax.axis_index("mp")
        mp_ref = mp_at.reshape(1)
        at_tables = jnp.asarray(tables(stored), jnp.int32)
        mine = lax.dynamic_index_in_dim(at_tables, dp_at, keepdims=False)
        arrives_at, ring_at = mine[0], mine[1]

        def mp_parts(value):
            bit = 1
            while True:
                got = lax.ppermute(value, "mp", mp_pairs(bit))
                bit *= 2
                if bit >= n_mp:
                    return value, got
                value = value + got

        up_all = lax.all_to_all(
            jnp.broadcast_to(adapter_up_panels[None], (n_dp,) + adapter_up_panels.shape),
            "dp", split_axis=0, concat_axis=0, tiled=True,
        ).reshape(tenants, rank, out_width)

        tenant_ids = jnp.arange(tenants, dtype=jnp.int32)
        list_location = jnp.sum(
            jnp.where(device_tenant_list[:, None] == tenant_ids[None, :], tenant_location_map[None, :], 0), axis=1
        )
        slot_ids = jnp.arange(listed, dtype=jnp.int32)
        row_slot = jnp.repeat(block_list_entry, block_rows)[:, None]
        at_list = lambda table: jnp.sum(
            jnp.where(list_location[:, None] == tenant_ids[None, :], table[None, :], 0), axis=1
        )

        where = at_list(arrives_at)
        which = at_list(jnp.asarray([j % stored for j in range(tenants)], jnp.int32))

        def both_ways(ahead, back):
            return [lax.ppermute(ahead, "dp", forward), lax.ppermute(back, "dp", backward)]

        def message(k, ahead, back):
            got_ahead, got_back = ahead.astype(F32), back.astype(F32)
            if ahead.shape[1] < width:
                got_ahead = jnp.pad(got_ahead, ((0, 0), (0, width - half)))
                got_back = jnp.pad(got_back, ((0, 0), (half, 0)))
            return [
                (dense[k].astype(F32) + got_ahead).astype(BF16),
                (dense[n_dp - k].astype(F32) + got_back).astype(BF16),
            ]

        held = [[adapter_down_panels, adapter_down_panels]]
        opposite, sums, cots = None, None, None
        last_in, last_out = half_way - 1, half_way + 1
        for phase in range(last_out + 1):
            now = {}
            if phase < last_in:
                now["held"] = both_ways(*held[-1])
            elif phase == last_in:
                now["opposite"] = both_ways(held[-1][0][:, :, :half], held[-1][1][:, :, half:])
            if phase == 2:
                now["sums"] = both_ways(*far_halves)
            elif phase > 2:
                now["sums"] = both_ways(*message(half_way + 2 - phase, *sums))
            if phase == 0:
                now["ups"] = [up_all]
                ready, *now["held"] = after([tokens] + now["held"])
                *products, others = base_products(mp_ref, ready, value_weight, n_mp)
                now["base"] = products + [others]
            elif phase == 1:
                up_part, own_ups = up_products(list_location, up_all, cotangent, row_slot, rank)
                far = (half_way * stored, half_way * stored + stored)
                now["shares"] = share_panels(
                    at_list(ring_at), mp_parts(up_part), row_slot, tokens, tenants, far
                )
                *products, others = base
                now["base"] = products + [lax.ppermute(others, "mp", mp_pairs(1))]
            elif phase == 2:
                *products, from_core = base
                base = [b + from_core[:, i * out_width:(i + 1) * out_width] for i, b in enumerate(products)]
                while len(base) > 1:
                    count = len(base) // 2
                    got = [lax.ppermute(b.astype(BF16), "mp", mp_pairs(2 * count)) for b in base[count:]]
                    base = [b + g.astype(F32) for b, g in zip(base, got)]
                now["base"] = base
            elif phase == 3:
                cots = [cotangent]
                bit = n_mp // 2
                while bit > 1:
                    cots += [lax.ppermute(c, "mp", mp_pairs(bit)) for c in cots]
                    bit //= 2
                now["cots"] = cots
            if phase == last_in + 1:
                slot_down = pick_panels(
                    [h[1] for h in held] + [h[0] for h in held[:0:-1]], opposite, where, which
                ).reshape(listed * rank, width)
                now["down"] = [slot_down] + list(mp_parts(down_products(tokens, slot_down, row_slot, rank)))

            keys = list(now)
            tied = after([v for k in keys for v in now[k]])
            for k in keys:
                now[k], tied = tied[:len(now[k])], tied[len(now[k]):]
            if "held" in now:
                held.append(now["held"])
            opposite, sums = now.get("opposite", opposite), now.get("sums", sums)
            base, cots = now.get("base", base if phase else None), now.get("cots", cots)
            if "ups" in now:
                (up_all,) = now["ups"]
            if "shares" in now:
                dense, up_wide, *far_halves = now["shares"]
                dense = dense.reshape(n_dp, stored * rank, width)
            if "down" in now:
                slot_down, *down_parts = now["down"]
        grad_a = add_panels(dense.reshape(-1, width), *sums).reshape(stored, rank, width)

        share_b, down_wide = share_panels(list_location, down_parts, row_slot, cotangent, tenants)
        values = (base[0] + matmul(down_wide, own_ups)).astype(BF16)

        all_cots = []
        for c in cots:
            all_cots += [c, lax.ppermute(c, "mp", mp_pairs(1))]
        token_gradient = input_gradient(mp_ref, all_cots, value_weight, up_wide, slot_down)

        back_b = lax.all_to_all(
            share_b.reshape(tenants, rank, out_width), "dp", split_axis=0, concat_axis=0, tiled=True
        ).reshape(n_dp, stored, rank, out_width)
        grad_b = jnp.sum(back_b.astype(F32), axis=0).astype(BF16)
        return (values, token_gradient, grad_a, grad_b)

    return shards


def solution(mesh):
    in_specs = (
        P("dp", "mp"),
        P("mp", None),
        P("dp", None, "mp"),
        P("dp", None, "mp"),
        P("dp", "mp"),
        P("dp"),
        P("dp"),
        P(),
    )
    out_specs = (P("dp", "mp"), P("dp", "mp"), P("dp", None, "mp"), P("dp", None, "mp"))
    shards = make_shards(mesh.shape["dp"], mesh.shape["mp"])
    return jax.shard_map(shards, mesh=mesh, in_specs=in_specs, out_specs=out_specs, check_vma=False)
```

time: 202 us -> 182 us (0.901)
  waiting for transfers between devices: 52.5 us -> 86 us
  starting transfers between devices: 59.1 us -> 32.8 us
  Pallas kernels: 62.1 us -> 40.8 us
  local copies, waits for them, and re-layouts: 16.2 us -> 8.88 us
  other arithmetic: 6.77 us -> 9.95 us
    ppermute x23 -> x17, starting transfers between devices: 41.6 us -> 17.4 us  [the longest x8 10.3 us: both_ways(): lax.ppermute(back, 'dp', backward)]
    pallas_call x5 -> x1, Pallas kernels: 16.3 us -> 3.72 us  [add_panels(): pl.pallas_call(kernel, grid=(width // tile,), in_specs=[spec] * (1 + len(...]
    ppermute x4, waiting for transfers between devices: 4.81 us -> 16.8 us  [mp_parts(): got = lax.ppermute(value, 'mp', mp_pairs(bit))]
    ppermute x1, waiting for transfers between devices: 0.01 us -> 8.9 us  [shards(): cots += [lax.ppermute(c, 'mp', mp_pairs(bit)) for c in cots]]
    all_to_all x1, waiting for transfers between devices: 0.01 us -> 7.87 us  [shards(): lax.all_to_all(share_b.reshape(tenants, rank, out_width), 'dp', split_axi...]
    ppermute x1, waiting for transfers between devices: 0.01 us -> 7.67 us  [shards(): lax.ppermute(b.astype(BF16), 'mp', mp_pairs(2 * count))]
    all_to_all x1, waiting for transfers between devices: 11.9 us -> 5.43 us  [shards(): lax.all_to_all(jnp.broadcast_to(adapter_up_panels[None], (n_dp,) + adapte...]
    pallas_call x5 -> x1, Pallas kernels: 7 us -> 1.89 us  [pick_panels(): pl.pallas_call(kernel, in_specs=[smem, smem] + [pl.BlockSpec(memory_space...]
  transfers between devices with their start and end apart: 33 -> 27, of which waited for: 8 -> 13; matrix products, arithmetic and copies ran while one was open for 7% -> 5% of each run, Pallas kernels for 31% -> 23%
where the time goes in v3:
time: 182 us; the launch traced here: 181 us
  waiting for transfers between devices  86 us (47%)
  Pallas kernels  40.8 us (22%)
  starting transfers between devices  32.8 us (18%)
  other arithmetic  9.95 us (5%)
  local copies, waits for them, and re-layouts  8.88 us (5%)
    ppermute x8, waiting for transfers between devices, both_ways(): lax.ppermute(ahead, 'dp', forward)  24.6 us
    ppermute x4, waiting for transfers between devices, mp_parts(): got = lax.ppermute(value, 'mp', mp_pairs(bit))  16.8 us
    ppermute x8, waiting for transfers between devices, both_ways(): lax.ppermute(back, 'dp', backward)  14.7 us
    pallas_call x1, Pallas kernels, input_gradient(): pl.pallas_call(kernel, grid_spec=pltpu.PrefetchScalarGridSpec(num_scalar_...  10.9 us
    ppermute x8, starting transfers between devices, both_ways(): lax.ppermute(back, 'dp', backward)  10.3 us
    pallas_call x2, Pallas kernels, share_panels(): pl.pallas_call(kernel, grid_spec=pltpu.PrefetchScalarGridSpec(num_scalar_...  9.67 us
    ppermute x1, waiting for transfers between devices, shards(): cots += [lax.ppermute(c, 'mp', mp_pairs(bit)) for c in cots]  8.9 us
    all_to_all x1, waiting for transfers between devices, shards(): lax.all_to_all(share_b.reshape(tenants, rank, out_width), 'dp', split_axi...  7.87 us
  transfers between devices with their start and end apart: 27, of which 13 were waited for; matrix products, arithmetic and copies ran while one was open for 5% of the time, Pallas kernels for 23%

profile of v3, /device:TPU:0, one launch (start us, length us, event | category | flops | bytes accessed | tf_op | source)
XLA Modules:
  0.0 181.0 jit_solution(14712069789798611098)
XLA Ops:
  0.6 3.1 %collective-permute-start = (bf16[3,64,2048]{2,1,0:T(8,128)(2,1)}, bf16[3,64,2048]{2,1,0:T(8,128)(2,1)S(1)}, u32[]{:S(2)}, u32[]{:S(2)}) collective-permute-start(bf16[3,64,2048]{2,1,0:T(8,128)(2,1)} %refs_0_.3), channel_id=1, source_target_pairs={{0,8},{8,16},{16,24},{24,28},{28,20},{20,12},{12,4},{4,0},{1,9},{9... | collective-permute-start | bytes 2359304 | tf_op jit(solution)/shard_map/ppermute | solution.py:365
  3.7 2.0 %broadcast_in_dim.53 = bf16[8,3,64,256]{3,2,1,0:T(8,128)(2,1)} broadcast(bf16[3,64,256]{2,1,0:T(8,128)(2,1)} %param.13), dimensions={1,2,3} | broadcast | bytes 884736 | tf_op jit(solution)/shard_map/broadcast_in_dim | solution.py:347
  5.7 6.3 %all-to-all-start = ((bf16[8,3,64,256]{3,2,1,0:T(8,128)(2,1)}), bf16[8,3,64,256]{3,2,1,0:T(8,128)(2,1)S(1)}, u32[]{:S(2)}, u32[]{:S(2)}) async-start(bf16[8,3,64,256]{3,2,1,0:T(8,128)(2,1)} %broadcast_in_dim.53), calls=%async_computation | async-start | bytes 1572864 | tf_op jit(solution)/shard_map/all_to_all | solution.py:346
  11.9 10.3 %collective-permute-done.refs_6_ = bf16[3,64,2048]{2,1,0:T(8,128)(2,1)S(1)} collective-permute-done((bf16[3,64,2048]{2,1,0:T(8,128)(2,1)}, bf16[3,64,2048]{2,1,0:T(8,128)(2,1)S(1)}, u32[]{:S(2)}, u32[]{:S(2)}) %collective-permute-start) | collective-permute-done | bytes 786464 | tf_op jit(solution)/shard_map/ppermute | solution.py:365
  22.2 2.2 %collective-permute-done.1.refs_1_ = bf16[3,64,2048]{2,1,0:T(8,128)(2,1)S(1)} collective-permute-done((bf16[3,64,2048]{2,1,0:T(8,128)(2,1)}, bf16[3,64,2048]{2,1,0:T(8,128)(2,1)S(1)}, u32[]{:S(2)}, u32[]{:S(2)}) %collective-permute-start.1) | collective-permute-done | bytes 786464 | tf_op jit(solution)/shard_map/ppermute | solution.py:365
  25.3 7.8 %base_products.1 = (f32[1024,256]{1,0:T(8,128)S(1)}, f32[1024,256]{1,0:T(8,128)S(1)}, f32[1024,512]{1,0:T(8,128)S(1)}) custom-call(s32[1]{0:T(128)} %bitcast.1.at_ref, bf16[1024,2048]{1,0:T(8,128)(2,1)} %second_ref.1, bf16[2048,1024]{1,0:T(8,128)(2,1)} %refs_7_.1, bf16[2048,1024]{1,0:T(8,128)(2,1)} %refs_7_.1, bf16[2048,1024]{1,0:T(8,128)(2,1)} %refs_7_.1, ...), custom_call_target="tpu_custom_call" | custom-call | flops 9349999616 | bytes 28900000 | tf_op jit(solution)/shard_map/base_products/pallas_call | solution.py:241
  35.4 5.4 %all-to-all-done = bf16[8,3,64,256]{3,2,1,0:T(8,128)(2,1)S(1)} async-done(((bf16[8,3,64,256]{3,2,1,0:T(8,128)(2,1)}), bf16[8,3,64,256]{3,2,1,0:T(8,128)(2,1)S(1)}, u32[]{:S(2)}, u32[]{:S(2)}) %all-to-all-start) | async-done | bytes 786464 | tf_op jit(solution)/shard_map/all_to_all | solution.py:346
  40.8 2.0 %collective-permute-start.3 = (bf16[3,64,2048]{2,1,0:T(8,128)(2,1)}, bf16[3,64,2048]{2,1,0:T(8,128)(2,1)}, u32[]{:S(2)}, u32[]{:S(2)}) collective-permute-start(bf16[3,64,2048]{2,1,0:T(8,128)(2,1)} %copy-done.9), channel_id=1, source_target_pairs={{8,0},{16,8},{24,16},{28,24},{20,28},{12,20},{4,12},{0,4},{9,1},{1... | collective-permute-start | bytes 2359304 | tf_op jit(solution)/shard_map/ppermute | solution.py:365
  43.6 2.3 %up_products.1 = (f32[512,128]{1,0:T(8,128)S(1)}, bf16[512,256]{1,0:T(8,128)(2,1)S(1)}) custom-call(s32[8]{0:T(128)S(1)} %select_reduce_fusion.3.at_ref, bf16[24,64,256]{2,1,0:T(8,128)(2,1)S(1)} %bitcast.14, bf16[1024,256]{1,0:T(8,128)(2,1)S(1)} %copy-done, s32[1024,1]{1,0:T(8,128)S(1)} %broadcast_in_dim_reshape.4.slot_ref.slot_a_ref.slot_b_ref), custom_call_target="tpu_custom_call" | custom-call | flops 137500000 | bytes 425000 | tf_op jit(solution)/shard_map/up_products/pallas_call | solution.py:93
  49.4 6.6 %collective-permute-done.5.b_ref = f32[512,128]{1,0:T(8,128)S(1)} collective-permute-done((f32[512,128]{1,0:T(8,128)S(1)}, f32[512,128]{1,0:T(8,128)S(1)}, u32[]{:S(2)}, u32[]{:S(2)}) %collective-permute-start.5) | collective-permute-done | bytes 262176 | tf_op jit(solution)/shard_map/ppermute | solution.py:340
  56.0 7.9 %share_panels.2 = (bf16[1536,2048]{1,0:T(8,128)(2,1)}, bf16[1024,512]{1,0:T(8,128)(2,1)S(1)}, bf16[192,1024]{1,0:T(8,128)(2,1)S(1)}, bf16[192,1024]{1,0:T(8,128)(2,1)S(1)}) custom-call(s32[8]{0:T(128)S(1)} %get-tuple-element.100.at_ref, f32[512,128]{1,0:T(8,128)S(1)} %add.45.a_ref, f32[512,128]{1,0:T(8,128)S(1)} %collective-permute-done.5.b_ref, ...), custom_call_target="tpu_custom_call" | custom-call | flops 412500000 | bytes 1275000 | tf_op jit(solution)/shard_map/share_panels/pallas_call | solution.py:191
  67.4 1.9 %collective-permute-start.8 = (bf16[3,64,2048]{2,1,0:T(8,128)(2,1)}, bf16[3,64,2048]{2,1,0:T(8,128)(2,1)S(1)}, u32[]{:S(2)}, u32[]{:S(2)}) collective-permute-start(bf16[3,64,2048]{2,1,0:T(8,128)(2,1)} %collective-permute-done.3.refs_2_), channel_id=1, source_target_pairs={{8,0},{16,8},{24,16},{28,24},{20,28},{12,20},{4,12},{0,4},{9,1},{1... | collective-permute-start | bytes 2359304 | tf_op jit(solution)/shard_map/ppermute | solution.py:365
  69.4 1.9 %collective-permute-start.10 = (bf16[192,1024]{1,0:T(8,128)(2,1)S(1)}, bf16[192,1024]{1,0:T(8,128)(2,1)S(1)}, u32[]{:S(2)}, u32[]{:S(2)}) collective-permute-start(bf16[192,1024]{1,0:T(8,128)(2,1)S(1)} %get-tuple-element.71), channel_id=1, source_target_pairs={{8,0},{16,8},{24,16},{28,24},{20,28},{12,20},{4,12},{0,4},{9,1},{1... | collective-permute-start | bytes 1179656 | tf_op jit(solution)/shard_map/ppermute | solution.py:365
  71.3 7.7 %collective-permute-done.11 = bf16[1024,256]{1,0:T(8,128)(2,1)S(1)} collective-permute-done((bf16[1024,256]{1,0:T(8,128)(2,1)S(1)}, bf16[1024,256]{1,0:T(8,128)(2,1)S(1)}, u32[]{:S(2)}, u32[]{:S(2)}) %collective-permute-start.11) | collective-permute-done | bytes 524320 | tf_op jit(solution)/shard_map/ppermute | solution.py:408
  79.0 2.4 %convert_add_fusion = f32[1024,256]{1,0:T(8,128)} fusion(bf16[1024,256]{1,0:T(8,128)(2,1)S(1)} %collective-permute-done.11, f32[1024,256]{1,0:T(8,128)S(1)} %get-tuple-element.72, f32[1024,512]{1,0:T(8,128)} %collective-permute-done.6), kind=kLoop, calls=%fused_computation.7 | loop fusion | flops 786432 | bytes 3670016 | tf_op jit(solution)/shard_map/add | solution.py:409
  81.4 13.1 %collective-permute-done.9 = bf16[192,1024]{1,0:T(8,128)(2,1)S(1)} collective-permute-done((bf16[192,1024]{1,0:T(8,128)(2,1)S(1)}, bf16[192,1024]{1,0:T(8,128)(2,1)S(1)}, u32[]{:S(2)}, u32[]{:S(2)}) %collective-permute-start.9) | collective-permute-done | bytes 393248 | tf_op jit(solution)/shard_map/ppermute | solution.py:365
  99.6 8.9 %collective-permute-done.16.refs_2_ = bf16[1024,256]{1,0:T(8,128)(2,1)} collective-permute-done((bf16[1024,256]{1,0:T(8,128)(2,1)S(1)}, bf16[1024,256]{1,0:T(8,128)(2,1)}, u32[]{:S(2)}, u32[]{:S(2)}) %collective-permute-start.16) | collective-permute-done | bytes 524320 | tf_op jit(solution)/shard_map/ppermute | solution.py:415
  108.5 12.5 %collective-permute-done.13.refs_8_ = bf16[3,64,1024]{2,1,0:T(8,128)(2,1)S(1)} collective-permute-done((bf16[3,64,1024]{2,1,0:T(8,128)(2,1)S(1)}, bf16[3,64,1024]{2,1,0:T(8,128)(2,1)S(1)}, u32[]{:S(2)}, u32[]{:S(2)}) %collective-permute-start.13) | collective-permute-done | bytes 393248 | tf_op jit(solution)/shard_map/ppermute | solution.py:365
  126.7 4.6 %down_products.1 = f32[512,128]{1,0:T(8,128)S(1)} custom-call(bf16[1024,2048]{1,0:T(8,128)(2,1)} %second_ref.1, bf16[1024,2048]{1,0:T(8,128)(2,1)} %second_ref.1, bf16[512,2048]{1,0:T(8,128)(2,1)S(1)} %bitcast.12, s32[1024,1]{1,0:T(8,128)S(1)} %broadcast_in_dim_reshape.4.slot_ref.slot_a_ref.slot_b_ref, ...), custom_call_target="tpu_custom_call" | custom-call | flops 253000000 | bytes 781999 | tf_op jit(solution)/shard_map/down_products/pallas_call | solution.py:120
  133.5 7.8 %collective-permute-done.20.b_ref = f32[512,128]{1,0:T(8,128)S(1)} collective-permute-done((f32[512,128]{1,0:T(8,128)S(1)}, f32[512,128]{1,0:T(8,128)S(1)}, u32[]{:S(2)}, u32[]{:S(2)}) %collective-permute-start.20) | collective-permute-done | bytes 262176 | tf_op jit(solution)/shard_map/ppermute | solution.py:340
  149.2 4.2 %all-to-all-start.1 = ((bf16[24,64,256]{2,1,0:T(8,128)(2,1)}), bf16[24,64,256]{2,1,0:T(8,128)(2,1)}, u32[]{:S(2)}, u32[]{:S(2)}) async-start(bf16[24,64,256]{2,1,0:T(8,128)(2,1)} %bitcast.15), calls=%async_computation.1 | async-start | bytes 1572864 | tf_op jit(solution)/shard_map/all_to_all | solution.py:449
  156.6 10.9 %input_gradient.1 = bf16[1024,2048]{1,0:T(8,128)(2,1)} custom-call(s32[1]{0:T(128)} %bitcast.1.at_ref, bf16[1024,512]{1,0:T(8,128)(2,1)S(1)} %copy-done.2, bf16[512,2048]{1,0:T(8,128)(2,1)S(1)} %bitcast.13, bf16[1024,256]{1,0:T(8,128)(2,1)S(1)} %copy-done, bf16[1024,256]{1,0:T(8,128)(2,1)} %collective-permute-done.21.refs_1_, ...), custom_call_target="tpu_custom_call" | custom-call | flops 605000000 | bytes 1870000 | tf_op jit(solution)/shard_map/input_gradient/pallas_call | solution.py:273
  167.5 3.7 %add_panels.1 = bf16[192,2048]{1,0:T(8,128)(2,1)} custom-call(bf16[1536,2048]{1,0:T(8,128)(2,1)} %get-tuple-element.76.refs_0_, bf16[192,2048]{1,0:T(8,128)(2,1)} %collective-permute-done.23.refs_1_, bf16[192,2048]{1,0:T(8,128)(2,1)} %collective-permute-done.24.refs_2_), custom_call_target="tpu_custom_call" | custom-call | flops 14300000256 | bytes 44200000 | tf_op jit(solution)/shard_map/add_panels/pallas_call | solution.py:218
  171.2 7.9 %all-to-all-done.1 = bf16[24,64,256]{2,1,0:T(8,128)(2,1)} async-done(((bf16[24,64,256]{2,1,0:T(8,128)(2,1)}), bf16[24,64,256]{2,1,0:T(8,128)(2,1)}, u32[]{:S(2)}, u32[]{:S(2)}) %all-to-all-start.1) | async-done | bytes 786464 | tf_op jit(solution)/shard_map/all_to_all | solution.py:449
  (95 shorter events, 36.8 us)
Async XLA Ops:
  0.6 21.6 %collective-permute-start = (bf16[3,64,2048]{2,1,0:T(8,128)(2,1)}, bf16[3,64,2048]{2,1,0:T(8,128)(2,1)S(1)}, u32[]{:S(2)}, u32[]{:S(2)}) collective-permute-start(bf16[3,64,2048]{2,1,0:T(8,128)(2,1)} %refs_0_.3), channel_id=1, source_target_pairs={{0,8},{8,16},{16,24},{24,28},{28,20},{20,12},{12,4},{4,0},{1,9},{9... | collective-permute-start | bytes 2359304 | tf_op jit(solution)/shard_map/ppermute | solution.py:365
  3.7 20.7 %collective-permute-start.1 = (bf16[3,64,2048]{2,1,0:T(8,128)(2,1)}, bf16[3,64,2048]{2,1,0:T(8,128)(2,1)S(1)}, u32[]{:S(2)}, u32[]{:S(2)}) collective-permute-start(bf16[3,64,2048]{2,1,0:T(8,128)(2,1)} %refs_0_.3), channel_id=1, source_target_pairs={{8,0},{16,8},{24,16},{28,24},{20,28},{12,20},{4,12},{0,4},{9,1},{1... | collective-permute-start | bytes 2359304 | tf_op jit(solution)/shard_map/ppermute | solution.py:365
  5.7 35.1 %all-to-all-start = ((bf16[8,3,64,256]{3,2,1,0:T(8,128)(2,1)}), bf16[8,3,64,256]{3,2,1,0:T(8,128)(2,1)S(1)}, u32[]{:S(2)}, u32[]{:S(2)}) async-start(bf16[8,3,64,256]{3,2,1,0:T(8,128)(2,1)} %broadcast_in_dim.53), calls=%async_computation | async-start | bytes 1572864 | tf_op jit(solution)/shard_map/all_to_all | solution.py:346
  40.8 23.2 %collective-permute-start.6 = (f32[1024,512]{1,0:T(8,128)}, f32[1024,512]{1,0:T(8,128)}, u32[]{:S(2)}, u32[]{:S(2)}) collective-permute-start(f32[1024,512]{1,0:T(8,128)} %copy-done.12), channel_id=1, source_target_pairs={{0,1},{1,0},{2,3},{3,2},{4,5},{5,4},{6,7},{7,6},{8,9},{9,8},{10,11... | collective-permute-start | bytes 6291464 | tf_op jit(solution)/shard_map/ppermute | solution.py:402
  40.8 23.1 %collective-permute-start.2 = (bf16[3,64,2048]{2,1,0:T(8,128)(2,1)}, bf16[3,64,2048]{2,1,0:T(8,128)(2,1)}, u32[]{:S(2)}, u32[]{:S(2)}) collective-permute-start(bf16[3,64,2048]{2,1,0:T(8,128)(2,1)} %copy-done.7), channel_id=1, source_target_pairs={{0,8},{8,16},{16,24},{24,28},{28,20},{20,12},{12,4},{4,0},{1,9},{9... | collective-permute-start | bytes 2359304 | tf_op jit(solution)/shard_map/ppermute | solution.py:365
  40.8 23.1 %collective-permute-start.3 = (bf16[3,64,2048]{2,1,0:T(8,128)(2,1)}, bf16[3,64,2048]{2,1,0:T(8,128)(2,1)}, u32[]{:S(2)}, u32[]{:S(2)}) collective-permute-start(bf16[3,64,2048]{2,1,0:T(8,128)(2,1)} %copy-done.9), channel_id=1, source_target_pairs={{8,0},{16,8},{24,16},{28,24},{20,28},{12,20},{4,12},{0,4},{9,1},{1... | collective-permute-start | bytes 2359304 | tf_op jit(solution)/shard_map/ppermute | solution.py:365
  47.6 8.4 %collective-permute-start.5 = (f32[512,128]{1,0:T(8,128)S(1)}, f32[512,128]{1,0:T(8,128)S(1)}, u32[]{:S(2)}, u32[]{:S(2)}) collective-permute-start(f32[512,128]{1,0:T(8,128)S(1)} %add.45.a_ref), channel_id=1, source_target_pairs={{0,2},{1,3},{2,0},{3,1},{4,6},{5,7},{6,4},{7,5},{8,10},{9,11},{10,... | collective-permute-start | bytes 786440 | tf_op jit(solution)/shard_map/ppermute | solution.py:340
  65.7 13.3 %collective-permute-start.11 = (bf16[1024,256]{1,0:T(8,128)(2,1)S(1)}, bf16[1024,256]{1,0:T(8,128)(2,1)S(1)}, u32[]{:S(2)}, u32[]{:S(2)}) collective-permute-start(bf16[1024,256]{1,0:T(8,128)(2,1)S(1)} %add_convert_fusion.7), channel_id=1, source_target_pairs={{0,2},{1,3},{2,0},{3,1},{4,6},{5,7},{6,4},{7,5},{8,10},{9,11},{10,... | collective-permute-start | bytes 1572872 | tf_op jit(solution)/shard_map/ppermute | solution.py:408
  67.3 27.2 %collective-permute-start.7 = (bf16[3,64,2048]{2,1,0:T(8,128)(2,1)}, bf16[3,64,2048]{2,1,0:T(8,128)(2,1)S(1)}, u32[]{:S(2)}, u32[]{:S(2)}) collective-permute-start(bf16[3,64,2048]{2,1,0:T(8,128)(2,1)} %collective-permute-done.2.refs_5_), channel_id=1, source_target_pairs={{0,8},{8,16},{16,24},{24,28},{28,20},{20,12},{12,4},{4,0},{1,9},{9... | collective-permute-start | bytes 2359304 | tf_op jit(solution)/shard_map/ppermute | solution.py:365
  67.4 27.1 %collective-permute-start.8 = (bf16[3,64,2048]{2,1,0:T(8,128)(2,1)}, bf16[3,64,2048]{2,1,0:T(8,128)(2,1)S(1)}, u32[]{:S(2)}, u32[]{:S(2)}) collective-permute-start(bf16[3,64,2048]{2,1,0:T(8,128)(2,1)} %collective-permute-done.3.refs_2_), channel_id=1, source_target_pairs={{8,0},{16,8},{24,16},{28,24},{20,28},{12,20},{4,12},{0,4},{9,1},{1... | collective-permute-start | bytes 2359304 | tf_op jit(solution)/shard_map/ppermute | solution.py:365
  69.3 25.2 %collective-permute-start.9 = (bf16[192,1024]{1,0:T(8,128)(2,1)S(1)}, bf16[192,1024]{1,0:T(8,128)(2,1)S(1)}, u32[]{:S(2)}, u32[]{:S(2)}) collective-permute-start(bf16[192,1024]{1,0:T(8,128)(2,1)S(1)} %get-tuple-element.70), channel_id=1, source_target_pairs={{0,8},{8,16},{16,24},{24,28},{28,20},{20,12},{12,4},{4,0},{1,9},{9... | collective-permute-start | bytes 1179656 | tf_op jit(solution)/shard_map/ppermute | solution.py:365
  69.4 25.1 %collective-permute-start.10 = (bf16[192,1024]{1,0:T(8,128)(2,1)S(1)}, bf16[192,1024]{1,0:T(8,128)(2,1)S(1)}, u32[]{:S(2)}, u32[]{:S(2)}) collective-permute-start(bf16[192,1024]{1,0:T(8,128)(2,1)S(1)} %get-tuple-element.71), channel_id=1, source_target_pairs={{8,0},{16,8},{24,16},{28,24},{20,28},{12,20},{4,12},{0,4},{9,1},{1... | collective-permute-start | bytes 1179656 | tf_op jit(solution)/shard_map/ppermute | solution.py:365
  94.8 27.3 %collective-permute-start.15 = (bf16[192,2048]{1,0:T(8,128)(2,1)S(1)}, bf16[192,2048]{1,0:T(8,128)(2,1)S(1)}, u32[]{:S(2)}, u32[]{:S(2)}) collective-permute-start(bf16[192,2048]{1,0:T(8,128)(2,1)S(1)} %get-tuple-element.105), channel_id=1, source_target_pairs={{8,0},{16,8},{24,16},{28,24},{20,28},{12,20},{4,12},{0,4},{9,1},{1... | collective-permute-start | bytes 2359304 | tf_op jit(solution)/shard_map/ppermute | solution.py:365
  96.6 25.5 %collective-permute-start.14 = (bf16[192,2048]{1,0:T(8,128)(2,1)S(1)}, bf16[192,2048]{1,0:T(8,128)(2,1)S(1)}, u32[]{:S(2)}, u32[]{:S(2)}) collective-permute-start(bf16[192,2048]{1,0:T(8,128)(2,1)S(1)} %get-tuple-element.106), channel_id=1, source_target_pairs={{0,8},{8,16},{16,24},{24,28},{28,20},{20,12},{12,4},{4,0},{1,9},{9... | collective-permute-start | bytes 2359304 | tf_op jit(solution)/shard_map/ppermute | solution.py:365
  96.9 11.6 %collective-permute-start.16 = (bf16[1024,256]{1,0:T(8,128)(2,1)S(1)}, bf16[1024,256]{1,0:T(8,128)(2,1)}, u32[]{:S(2)}, u32[]{:S(2)}) collective-permute-start(bf16[1024,256]{1,0:T(8,128)(2,1)S(1)} %copy-done), channel_id=1, source_target_pairs={{0,2},{1,3},{2,0},{3,1},{4,6},{5,7},{6,4},{7,5},{8,10},{9,11},{10,... | collective-permute-start | bytes 1572872 | tf_op jit(solution)/shard_map/ppermute | solution.py:415
  97.5 23.5 %collective-permute-start.13 = (bf16[3,64,1024]{2,1,0:T(8,128)(2,1)S(1)}, bf16[3,64,1024]{2,1,0:T(8,128)(2,1)S(1)}, u32[]{:S(2)}, u32[]{:S(2)}) collective-permute-start(bf16[3,64,1024]{2,1,0:T(8,128)(2,1)S(1)} %slice.49), channel_id=1, source_target_pairs={{8,0},{16,8},{24,16},{28,24},{20,28},{12,20},{4,12},{0,4},{9,1},{1... | collective-permute-start | bytes 1179656 | tf_op jit(solution)/shard_map/ppermute | solution.py:365
  99.3 22.8 %collective-permute-start.12 = (bf16[3,64,1024]{2,1,0:T(8,128)(2,1)S(1)}, bf16[3,64,1024]{2,1,0:T(8,128)(2,1)S(1)}, u32[]{:S(2)}, u32[]{:S(2)}) collective-permute-start(bf16[3,64,1024]{2,1,0:T(8,128)(2,1)S(1)} %slice.48), channel_id=1, source_target_pairs={{0,8},{8,16},{16,24},{24,28},{28,20},{20,12},{12,4},{4,0},{1,9},{9... | collective-permute-start | bytes 1179656 | tf_op jit(solution)/shard_map/ppermute | solution.py:365
  122.7 18.6 %collective-permute-start.18 = (bf16[192,2048]{1,0:T(8,128)(2,1)S(1)}, bf16[192,2048]{1,0:T(8,128)(2,1)S(1)}, u32[]{:S(2)}, u32[]{:S(2)}) collective-permute-start(bf16[192,2048]{1,0:T(8,128)(2,1)S(1)} %get-tuple-element.103), channel_id=1, source_target_pairs={{8,0},{16,8},{24,16},{28,24},{20,28},{12,20},{4,12},{0,4},{9,1},{1... | collective-permute-start | bytes 2359304 | tf_op jit(solution)/shard_map/ppermute | solution.py:365
  123.2 18.2 %collective-permute-start.17 = (bf16[192,2048]{1,0:T(8,128)(2,1)S(1)}, bf16[192,2048]{1,0:T(8,128)(2,1)S(1)}, u32[]{:S(2)}, u32[]{:S(2)}) collective-permute-start(bf16[192,2048]{1,0:T(8,128)(2,1)S(1)} %get-tuple-element.104), channel_id=1, source_target_pairs={{0,8},{8,16},{16,24},{24,28},{28,20},{20,12},{12,4},{4,0},{1,9},{9... | collective-permute-start | bytes 2359304 | tf_op jit(solution)/shard_map/ppermute | solution.py:365
  143.1 24.4 %collective-permute-start.24 = (bf16[192,2048]{1,0:T(8,128)(2,1)}, bf16[192,2048]{1,0:T(8,128)(2,1)}, u32[]{:S(2)}, u32[]{:S(2)}) collective-permute-start(bf16[192,2048]{1,0:T(8,128)(2,1)} %get-tuple-element.101), channel_id=1, source_target_pairs={{8,0},{16,8},{24,16},{28,24},{20,28},{12,20},{4,12},{0,4},{9,1},{1... | collective-permute-start | bytes 2359304 | tf_op jit(solution)/shard_map/ppermute | solution.py:365
  143.5 24.0 %collective-permute-start.23 = (bf16[192,2048]{1,0:T(8,128)(2,1)}, bf16[192,2048]{1,0:T(8,128)(2,1)}, u32[]{:S(2)}, u32[]{:S(2)}) collective-permute-start(bf16[192,2048]{1,0:T(8,128)(2,1)} %get-tuple-element.102), channel_id=1, source_target_pairs={{0,8},{8,16},{16,24},{24,28},{28,20},{20,12},{12,4},{4,0},{1,9},{9... | collective-permute-start | bytes 2359304 | tf_op jit(solution)/shard_map/ppermute | solution.py:365
  145.1 11.0 %collective-permute-start.21 = (bf16[1024,256]{1,0:T(8,128)(2,1)S(1)}, bf16[1024,256]{1,0:T(8,128)(2,1)}, u32[]{:S(2)}, u32[]{:S(2)}) collective-permute-start(bf16[1024,256]{1,0:T(8,128)(2,1)S(1)} %copy-done), channel_id=1, source_target_pairs={{0,1},{1,0},{2,3},{3,2},{4,5},{5,4},{6,7},{7,6},{8,9},{9,8},{10,11... | collective-permute-start | bytes 1572872 | tf_op jit(solution)/shard_map/ppermute | solution.py:446
  145.1 11.0 %collective-permute-start.22 = (bf16[1024,256]{1,0:T(8,128)(2,1)}, bf16[1024,256]{1,0:T(8,128)(2,1)}, u32[]{:S(2)}, u32[]{:S(2)}) collective-permute-start(bf16[1024,256]{1,0:T(8,128)(2,1)} %collective-permute-done.16.refs_2_), channel_id=1, source_target_pairs={{0,1},{1,0},{2,3},{3,2},{4,5},{5,4},{6,7},{7,6},{8,9},{9,8},{10,11... | collective-permute-start | bytes 1572872 | tf_op jit(solution)/shard_map/ppermute | solution.py:446
  149.2 29.9 %all-to-all-start.1 = ((bf16[24,64,256]{2,1,0:T(8,128)(2,1)}), bf16[24,64,256]{2,1,0:T(8,128)(2,1)}, u32[]{:S(2)}, u32[]{:S(2)}) async-start(bf16[24,64,256]{2,1,0:T(8,128)(2,1)} %bitcast.15), calls=%async_computation.1 | async-start | bytes 1572864 | tf_op jit(solution)/shard_map/all_to_all | solution.py:449
  (22 other events, 238.4 us)

commit v4 on v3

--- a/solution.py
+++ b/solution.py
@@ -135,14 +135,14 @@
     )(tokens, tokens, slot_down, row_slot, row_slot)
 
 
-def share_panels(positions, parts, row_slot, other, panels, far=None):
+def share_panels(positions, parts, row_slot, lane_slot, other, panels, far=None):
     half_rows, pair = parts[0].shape
     rank, rows = pair // 2, 2 * half_rows
     listed, width = positions.shape[0], other.shape[1]
-    tile = min(512, width // 2 if far else width)
+    tile = min(1024, width // 2 if far else width)
     steps = width // tile
 
-    def kernel(at_ref, a_ref, b_ref, slot_ref, other_ref, dense_ref, wide_ref, *refs):
+    def kernel(at_ref, a_ref, b_ref, slot_ref, lane_ref, other_ref, dense_ref, wide_ref, *refs):
         turned_ref = refs[-1]
         step = pl.program_id(0)
 
@@ -155,7 +155,9 @@
             group = lax.broadcasted_iota(jnp.int32, (rows, listed * rank), 1) // rank
             wide = jnp.where(group == slot_ref[...], matmul(low, eye), 0.0)
             wide_ref[...] = wide.astype(BF16)
-            turned_ref[...] = wide.T.astype(BF16)
+            turned = jnp.concatenate([both[:, :rank], both[:, rank:]], axis=0).T
+            for s in range(listed):
+                turned_ref[s * rank:(s + 1) * rank, :] = jnp.where(lane_ref[...] == s, turned, 0.0).astype(BF16)
 
         shares = matmul(turned_ref[...], other_ref[...]).astype(BF16)
         dense_ref[...] = jnp.zeros(dense_ref.shape, BF16)
@@ -193,7 +195,7 @@
         grid_spec=pltpu.PrefetchScalarGridSpec(
             num_scalar_prefetch=1,
             grid=(steps,),
-            in_specs=[whole(parts[0]), whole(parts[1]), whole(row_slot), pl.BlockSpec((rows, tile), lambda i, at: (0, i))],
+            in_specs=[whole(parts[0]), whole(parts[1]), whole(row_slot), whole(lane_slot), pl.BlockSpec((rows, tile), lambda i, at: (0, i))],
             out_specs=out_specs,
             scratch_shapes=[pltpu.VMEM((listed * rank, rows), BF16)],
         ),
@@ -201,7 +203,7 @@
         compiler_params=pltpu.CompilerParams(vmem_limit_bytes=48 * 1024 * 1024),
         cost_estimate=lasting(7.5),
         name="share_panels",
-    )(positions, *parts, row_slot, other)
+    )(positions, *parts, row_slot, lane_slot, other)
 
 
 def add_panels(first, *others):
@@ -354,11 +356,12 @@
         )
         slot_ids = jnp.arange(listed, dtype=jnp.int32)
         row_slot = jnp.repeat(block_list_entry, block_rows)[:, None]
+        lane_slot = row_slot.reshape(1, rows)
         at_list = lambda table: jnp.sum(
             jnp.where(list_location[:, None] == tenant_ids[None, :], table[None, :], 0), axis=1
         )
 
-        where = at_list(arrives_at)
+        where, share_place = at_list(arrives_at), at_list(ring_at)
         which = at_list(jnp.asarray([j % stored for j in range(tenants)], jnp.int32))
 
         def both_ways(ahead, back):
@@ -389,6 +392,7 @@
                 now["sums"] = both_ways(*message(half_way + 2 - phase, *sums))
             if phase == 0:
                 now["ups"] = [up_all]
+                now["index"] = [row_slot, lane_slot, list_location, share_place, where, which]
                 ready, *now["held"] = after([tokens] + now["held"])
                 *products, others = base_products(mp_ref, ready, value_weight, n_mp)
                 now["base"] = products + [others]
@@ -396,7 +400,7 @@
                 up_part, own_ups = up_products(list_location, up_all, cotangent, row_slot, rank)
                 far = (half_way * stored, half_way * stored + stored)
                 now["shares"] = share_panels(
-                    at_list(ring_at), mp_parts(up_part), row_slot, tokens, tenants, far
+                    share_place, mp_parts(up_part), row_slot, lane_slot, tokens, tenants, far
                 )
                 *products, others = base
                 now["base"] = products + [lax.ppermute(others, "mp", mp_pairs(1))]
@@ -431,6 +435,7 @@
             base, cots = now.get("base", base if phase else None), now.get("cots", cots)
             if "ups" in now:
                 (up_all,) = now["ups"]
+                row_slot, lane_slot, list_location, share_place, where, which = now["index"]
             if "shares" in now:
                 dense, up_wide, *far_halves = now["shares"]
                 dense = dense.reshape(n_dp, stored * rank, width)
@@ -438,7 +443,7 @@
                 slot_down, *down_parts = now["down"]
         grad_a = add_panels(dense.reshape(-1, width), *sums).reshape(stored, rank, width)
 
-        share_b, down_wide = share_panels(list_location, down_parts, row_slot, cotangent, tenants)
+        share_b, down_wide = share_panels(list_location, down_parts, row_slot, lane_slot, cotangent, tenants)
         values = (base[0] + matmul(down_wide, own_ups)).astype(BF16)
 
         all_cots = []

time: 182 us -> 180 us (0.989)
  transfers between devices with their start and end apart: 27 -> 27, of which waited for: 13 -> 13; matrix products, arithmetic and copies ran while one was open for 5% -> 5% of each run, Pallas kernels for 23% -> 22%
where the time goes in v4:
time: 180 us
  waiting for transfers between devices  85.9 us (48%)
  Pallas kernels  39.8 us (22%)
  starting transfers between devices  32.7 us (18%)
  other arithmetic  9.98 us (6%)
  local copies, waits for them, and re-layouts  8.73 us (5%)
    ppermute x8, waiting for transfers between devices, both_ways(): lax.ppermute(ahead, 'dp', forward)  23.3 us
    ppermute x4, waiting for transfers between devices, mp_parts(): got = lax.ppermute(value, 'mp', mp_pairs(bit))  17.7 us
    ppermute x8, waiting for transfers between devices, both_ways(): lax.ppermute(back, 'dp', backward)  14.7 us
    pallas_call x1, Pallas kernels, input_gradient(): pl.pallas_call(kernel, grid_spec=pltpu.PrefetchScalarGridSpec(num_scalar_...  10.9 us
    ppermute x8, starting transfers between devices, both_ways(): lax.ppermute(back, 'dp', backward)  10.3 us
    ppermute x1, waiting for transfers between devices, shards(): cots += [lax.ppermute(c, 'mp', mp_pairs(bit)) for c in cots]  8.9 us
    pallas_call x2, Pallas kernels, share_panels(): pl.pallas_call(kernel, grid_spec=pltpu.PrefetchScalarGridSpec(num_scalar_...  8.74 us
    all_to_all x1, waiting for transfers between devices, shards(): lax.all_to_all(share_b.reshape(tenants, rank, out_width), 'dp', split_axi...  8.19 us
  transfers between devices with their start and end apart: 27, of which 13 were waited for; matrix products, arithmetic and copies ran while one was open for 5% of the time, Pallas kernels for 22%

profile of v4, /device:TPU:0, one launch (start us, length us, event | category | flops | bytes accessed | tf_op | source)
XLA Modules:
  0.0 179.9 jit_solution(10709193985518378505)
XLA Ops:
  0.7 3.1 %collective-permute-start = (bf16[3,64,2048]{2,1,0:T(8,128)(2,1)}, bf16[3,64,2048]{2,1,0:T(8,128)(2,1)S(1)}, u32[]{:S(2)}, u32[]{:S(2)}) collective-permute-start(bf16[3,64,2048]{2,1,0:T(8,128)(2,1)} %refs_0_.3), channel_id=1, source_target_pairs={{0,8},{8,16},{16,24},{24,28},{28,20},{20,12},{12,4},{4,0},{1,9},{9... | collective-permute-start | bytes 2359304 | tf_op jit(solution)/shard_map/ppermute | solution.py:368
  3.8 2.0 %broadcast_in_dim.53 = bf16[8,3,64,256]{3,2,1,0:T(8,128)(2,1)} broadcast(bf16[3,64,256]{2,1,0:T(8,128)(2,1)} %param.13), dimensions={1,2,3} | broadcast | bytes 884736 | tf_op jit(solution)/shard_map/broadcast_in_dim | solution.py:349
  5.7 6.3 %all-to-all-start = ((bf16[8,3,64,256]{3,2,1,0:T(8,128)(2,1)}), bf16[8,3,64,256]{3,2,1,0:T(8,128)(2,1)S(1)}, u32[]{:S(2)}, u32[]{:S(2)}) async-start(bf16[8,3,64,256]{3,2,1,0:T(8,128)(2,1)} %broadcast_in_dim.53), calls=%async_computation | async-start | bytes 1572864 | tf_op jit(solution)/shard_map/all_to_all | solution.py:348
  13.3 8.9 %collective-permute-done.refs_6_ = bf16[3,64,2048]{2,1,0:T(8,128)(2,1)S(1)} collective-permute-done((bf16[3,64,2048]{2,1,0:T(8,128)(2,1)}, bf16[3,64,2048]{2,1,0:T(8,128)(2,1)S(1)}, u32[]{:S(2)}, u32[]{:S(2)}) %collective-permute-start) | collective-permute-done | bytes 786464 | tf_op jit(solution)/shard_map/ppermute | solution.py:368
  22.2 2.2 %collective-permute-done.1.refs_1_ = bf16[3,64,2048]{2,1,0:T(8,128)(2,1)S(1)} collective-permute-done((bf16[3,64,2048]{2,1,0:T(8,128)(2,1)}, bf16[3,64,2048]{2,1,0:T(8,128)(2,1)S(1)}, u32[]{:S(2)}, u32[]{:S(2)}) %collective-permute-start.1) | collective-permute-done | bytes 786464 | tf_op jit(solution)/shard_map/ppermute | solution.py:368
  25.3 7.7 %base_products.1 = (f32[1024,256]{1,0:T(8,128)S(1)}, f32[1024,256]{1,0:T(8,128)S(1)}, f32[1024,512]{1,0:T(8,128)S(1)}) custom-call(s32[1]{0:T(128)} %bitcast.3.at_ref, bf16[1024,2048]{1,0:T(8,128)(2,1)} %second_ref.1, bf16[2048,1024]{1,0:T(8,128)(2,1)} %refs_7_.1, bf16[2048,1024]{1,0:T(8,128)(2,1)} %refs_7_.1, bf16[2048,1024]{1,0:T(8,128)(2,1)} %refs_7_.1, ...), custom_call_target="tpu_custom_call" | custom-call | flops 9349999616 | bytes 28900000 | tf_op jit(solution)/shard_map/base_products/pallas_call | solution.py:243
  35.3 5.5 %all-to-all-done = bf16[8,3,64,256]{3,2,1,0:T(8,128)(2,1)S(1)} async-done(((bf16[8,3,64,256]{3,2,1,0:T(8,128)(2,1)}), bf16[8,3,64,256]{3,2,1,0:T(8,128)(2,1)S(1)}, u32[]{:S(2)}, u32[]{:S(2)}) %all-to-all-start) | async-done | bytes 786464 | tf_op jit(solution)/shard_map/all_to_all | solution.py:348
  40.8 2.0 %collective-permute-start.3 = (bf16[3,64,2048]{2,1,0:T(8,128)(2,1)}, bf16[3,64,2048]{2,1,0:T(8,128)(2,1)}, u32[]{:S(2)}, u32[]{:S(2)}) collective-permute-start(bf16[3,64,2048]{2,1,0:T(8,128)(2,1)} %copy-done.9), channel_id=1, source_target_pairs={{8,0},{16,8},{24,16},{28,24},{20,28},{12,20},{4,12},{0,4},{9,1},{1... | collective-permute-start | bytes 2359304 | tf_op jit(solution)/shard_map/ppermute | solution.py:368
  43.1 2.3 %up_products.1 = (f32[512,128]{1,0:T(8,128)S(1)}, bf16[512,256]{1,0:T(8,128)(2,1)S(1)}) custom-call(s32[8]{0:T(128)S(1)} %select_reduce_fusion.3.at_ref, bf16[24,64,256]{2,1,0:T(8,128)(2,1)S(1)} %bitcast.14, bf16[1024,256]{1,0:T(8,128)(2,1)S(1)} %copy-done, s32[1024,1]{1,0:T(8,128)S(1)} %copy.19.slot_ref.slot_a_ref.slot_b_ref), custom_call_target="tpu_custom_call" | custom-call | flops 137500000 | bytes 425000 | tf_op jit(solution)/shard_map/up_products/pallas_call | solution.py:93
  48.6 6.8 %collective-permute-done.5.b_ref = f32[512,128]{1,0:T(8,128)S(1)} collective-permute-done((f32[512,128]{1,0:T(8,128)S(1)}, f32[512,128]{1,0:T(8,128)S(1)}, u32[]{:S(2)}, u32[]{:S(2)}) %collective-permute-start.5) | collective-permute-done | bytes 262176 | tf_op jit(solution)/shard_map/ppermute | solution.py:342
  55.5 7.4 %share_panels.2 = (bf16[1536,2048]{1,0:T(8,128)(2,1)}, bf16[1024,512]{1,0:T(8,128)(2,1)S(1)}, bf16[192,1024]{1,0:T(8,128)(2,1)S(1)}, bf16[192,1024]{1,0:T(8,128)(2,1)S(1)}) custom-call(s32[8]{0:T(128)S(1)} %get-tuple-element.65.at_ref, f32[512,128]{1,0:T(8,128)S(1)} %add.45.a_ref, f32[512,128]{1,0:T(8,128)S(1)} %collective-permute-done.5.b_ref, ...), custom_call_target="tpu_custom_call" | custom-call | flops 412500000 | bytes 1275000 | tf_op jit(solution)/shard_map/share_panels/pallas_call | solution.py:193
  66.3 1.9 %collective-permute-start.8 = (bf16[3,64,2048]{2,1,0:T(8,128)(2,1)}, bf16[3,64,2048]{2,1,0:T(8,128)(2,1)S(1)}, u32[]{:S(2)}, u32[]{:S(2)}) collective-permute-start(bf16[3,64,2048]{2,1,0:T(8,128)(2,1)} %collective-permute-done.3.refs_2_), channel_id=1, source_target_pairs={{8,0},{16,8},{24,16},{28,24},{20,28},{12,20},{4,12},{0,4},{9,1},{1... | collective-permute-start | bytes 2359304 | tf_op jit(solution)/shard_map/ppermute | solution.py:368
  68.4 1.9 %collective-permute-start.10 = (bf16[192,1024]{1,0:T(8,128)(2,1)S(1)}, bf16[192,1024]{1,0:T(8,128)(2,1)S(1)}, u32[]{:S(2)}, u32[]{:S(2)}) collective-permute-start(bf16[192,1024]{1,0:T(8,128)(2,1)S(1)} %get-tuple-element.81), channel_id=1, source_target_pairs={{8,0},{16,8},{24,16},{28,24},{20,28},{12,20},{4,12},{0,4},{9,1},{1... | collective-permute-start | bytes 1179656 | tf_op jit(solution)/shard_map/ppermute | solution.py:368
  70.3 7.6 %collective-permute-done.11 = bf16[1024,256]{1,0:T(8,128)(2,1)S(1)} collective-permute-done((bf16[1024,256]{1,0:T(8,128)(2,1)S(1)}, bf16[1024,256]{1,0:T(8,128)(2,1)S(1)}, u32[]{:S(2)}, u32[]{:S(2)}) %collective-permute-start.11) | collective-permute-done | bytes 524320 | tf_op jit(solution)/shard_map/ppermute | solution.py:412
  78.0 2.4 %convert_add_fusion = f32[1024,256]{1,0:T(8,128)} fusion(bf16[1024,256]{1,0:T(8,128)(2,1)S(1)} %collective-permute-done.11, f32[1024,256]{1,0:T(8,128)S(1)} %get-tuple-element.82, f32[1024,512]{1,0:T(8,128)} %collective-permute-done.6), kind=kLoop, calls=%fused_computation.7 | loop fusion | flops 786432 | bytes 3670016 | tf_op jit(solution)/shard_map/add | solution.py:413
  80.3 13.1 %collective-permute-done.9 = bf16[192,1024]{1,0:T(8,128)(2,1)S(1)} collective-permute-done((bf16[192,1024]{1,0:T(8,128)(2,1)S(1)}, bf16[192,1024]{1,0:T(8,128)(2,1)S(1)}, u32[]{:S(2)}, u32[]{:S(2)}) %collective-permute-start.9) | collective-permute-done | bytes 393248 | tf_op jit(solution)/shard_map/ppermute | solution.py:368
  98.6 8.9 %collective-permute-done.16.refs_2_ = bf16[1024,256]{1,0:T(8,128)(2,1)} collective-permute-done((bf16[1024,256]{1,0:T(8,128)(2,1)S(1)}, bf16[1024,256]{1,0:T(8,128)(2,1)}, u32[]{:S(2)}, u32[]{:S(2)}) %collective-permute-start.16) | collective-permute-done | bytes 524320 | tf_op jit(solution)/shard_map/ppermute | solution.py:419
  107.5 12.5 %collective-permute-done.13.refs_8_ = bf16[3,64,1024]{2,1,0:T(8,128)(2,1)S(1)} collective-permute-done((bf16[3,64,1024]{2,1,0:T(8,128)(2,1)S(1)}, bf16[3,64,1024]{2,1,0:T(8,128)(2,1)S(1)}, u32[]{:S(2)}, u32[]{:S(2)}) %collective-permute-start.13) | collective-permute-done | bytes 393248 | tf_op jit(solution)/shard_map/ppermute | solution.py:368
  125.7 4.6 %down_products.1 = f32[512,128]{1,0:T(8,128)S(1)} custom-call(bf16[1024,2048]{1,0:T(8,128)(2,1)} %second_ref.1, bf16[1024,2048]{1,0:T(8,128)(2,1)} %second_ref.1, bf16[512,2048]{1,0:T(8,128)(2,1)S(1)} %bitcast.12, s32[1024,1]{1,0:T(8,128)S(1)} %copy.19.slot_ref.slot_a_ref.slot_b_ref, s32[1024,1]{1,0:T(8,128)S(1)} %copy.19.slot_ref.slot_a_ref.slot_b_ref), custom_call_target="tpu_custom_call" | custom-call | flops 253000000 | bytes 781999 | tf_op jit(solution)/shard_map/down_products/pallas_call | solution.py:120
  132.4 7.9 %collective-permute-done.20.b_ref = f32[512,128]{1,0:T(8,128)S(1)} collective-permute-done((f32[512,128]{1,0:T(8,128)S(1)}, f32[512,128]{1,0:T(8,128)S(1)}, u32[]{:S(2)}, u32[]{:S(2)}) %collective-permute-start.20) | collective-permute-done | bytes 262176 | tf_op jit(solution)/shard_map/ppermute | solution.py:342
  147.8 4.2 %all-to-all-start.1 = ((bf16[24,64,256]{2,1,0:T(8,128)(2,1)}), bf16[24,64,256]{2,1,0:T(8,128)(2,1)}, u32[]{:S(2)}, u32[]{:S(2)}) async-start(bf16[24,64,256]{2,1,0:T(8,128)(2,1)} %bitcast.15), calls=%async_computation.1 | async-start | bytes 1572864 | tf_op jit(solution)/shard_map/all_to_all | solution.py:454
  155.2 10.9 %input_gradient.1 = bf16[1024,2048]{1,0:T(8,128)(2,1)} custom-call(s32[1]{0:T(128)} %bitcast.3.at_ref, bf16[1024,512]{1,0:T(8,128)(2,1)S(1)} %copy-done.2, bf16[512,2048]{1,0:T(8,128)(2,1)S(1)} %bitcast.13, bf16[1024,256]{1,0:T(8,128)(2,1)S(1)} %copy-done, bf16[1024,256]{1,0:T(8,128)(2,1)} %collective-permute-done.21.refs_1_, ...), custom_call_target="tpu_custom_call" | custom-call | flops 605000000 | bytes 1870000 | tf_op jit(solution)/shard_map/input_gradient/pallas_call | solution.py:275
  166.1 3.7 %add_panels.1 = bf16[192,2048]{1,0:T(8,128)(2,1)} custom-call(bf16[1536,2048]{1,0:T(8,128)(2,1)} %get-tuple-element.86.refs_0_, bf16[192,2048]{1,0:T(8,128)(2,1)} %collective-permute-done.23.refs_1_, bf16[192,2048]{1,0:T(8,128)(2,1)} %collective-permute-done.24.refs_2_), custom_call_target="tpu_custom_call" | custom-call | flops 14300000256 | bytes 44200000 | tf_op jit(solution)/shard_map/add_panels/pallas_call | solution.py:220
  169.8 8.2 %all-to-all-done.1 = bf16[24,64,256]{2,1,0:T(8,128)(2,1)} async-done(((bf16[24,64,256]{2,1,0:T(8,128)(2,1)}), bf16[24,64,256]{2,1,0:T(8,128)(2,1)}, u32[]{:S(2)}, u32[]{:S(2)}) %all-to-all-start.1) | async-done | bytes 786464 | tf_op jit(solution)/shard_map/all_to_all | solution.py:454
  (97 shorter events, 36.9 us)
Async XLA Ops:
  0.7 21.6 %collective-permute-start = (bf16[3,64,2048]{2,1,0:T(8,128)(2,1)}, bf16[3,64,2048]{2,1,0:T(8,128)(2,1)S(1)}, u32[]{:S(2)}, u32[]{:S(2)}) collective-permute-start(bf16[3,64,2048]{2,1,0:T(8,128)(2,1)} %refs_0_.3), channel_id=1, source_target_pairs={{0,8},{8,16},{16,24},{24,28},{28,20},{20,12},{12,4},{4,0},{1,9},{9... | collective-permute-start | bytes 2359304 | tf_op jit(solution)/shard_map/ppermute | solution.py:368
  3.8 20.7 %collective-permute-start.1 = (bf16[3,64,2048]{2,1,0:T(8,128)(2,1)}, bf16[3,64,2048]{2,1,0:T(8,128)(2,1)S(1)}, u32[]{:S(2)}, u32[]{:S(2)}) collective-permute-start(bf16[3,64,2048]{2,1,0:T(8,128)(2,1)} %refs_0_.3), channel_id=1, source_target_pairs={{8,0},{16,8},{24,16},{28,24},{20,28},{12,20},{4,12},{0,4},{9,1},{1... | collective-permute-start | bytes 2359304 | tf_op jit(solution)/shard_map/ppermute | solution.py:368
  5.7 35.1 %all-to-all-start = ((bf16[8,3,64,256]{3,2,1,0:T(8,128)(2,1)}), bf16[8,3,64,256]{3,2,1,0:T(8,128)(2,1)S(1)}, u32[]{:S(2)}, u32[]{:S(2)}) async-start(bf16[8,3,64,256]{3,2,1,0:T(8,128)(2,1)} %broadcast_in_dim.53), calls=%async_computation | async-start | bytes 1572864 | tf_op jit(solution)/shard_map/all_to_all | solution.py:348
  40.8 22.1 %collective-permute-start.6 = (f32[1024,512]{1,0:T(8,128)}, f32[1024,512]{1,0:T(8,128)}, u32[]{:S(2)}, u32[]{:S(2)}) collective-permute-start(f32[1024,512]{1,0:T(8,128)} %copy-done.12), channel_id=1, source_target_pairs={{0,1},{1,0},{2,3},{3,2},{4,5},{5,4},{6,7},{7,6},{8,9},{9,8},{10,11... | collective-permute-start | bytes 6291464 | tf_op jit(solution)/shard_map/ppermute | solution.py:406
  40.8 22.1 %collective-permute-start.2 = (bf16[3,64,2048]{2,1,0:T(8,128)(2,1)}, bf16[3,64,2048]{2,1,0:T(8,128)(2,1)}, u32[]{:S(2)}, u32[]{:S(2)}) collective-permute-start(bf16[3,64,2048]{2,1,0:T(8,128)(2,1)} %copy-done.7), channel_id=1, source_target_pairs={{0,8},{8,16},{16,24},{24,28},{28,20},{20,12},{12,4},{4,0},{1,9},{9... | collective-permute-start | bytes 2359304 | tf_op jit(solution)/shard_map/ppermute | solution.py:368
  40.8 22.1 %collective-permute-start.3 = (bf16[3,64,2048]{2,1,0:T(8,128)(2,1)}, bf16[3,64,2048]{2,1,0:T(8,128)(2,1)}, u32[]{:S(2)}, u32[]{:S(2)}) collective-permute-start(bf16[3,64,2048]{2,1,0:T(8,128)(2,1)} %copy-done.9), channel_id=1, source_target_pairs={{8,0},{16,8},{24,16},{28,24},{20,28},{12,20},{4,12},{0,4},{9,1},{1... | collective-permute-start | bytes 2359304 | tf_op jit(solution)/shard_map/ppermute | solution.py:368
  64.7 13.3 %collective-permute-start.11 = (bf16[1024,256]{1,0:T(8,128)(2,1)S(1)}, bf16[1024,256]{1,0:T(8,128)(2,1)S(1)}, u32[]{:S(2)}, u32[]{:S(2)}) collective-permute-start(bf16[1024,256]{1,0:T(8,128)(2,1)S(1)} %add_convert_fusion.7), channel_id=1, source_target_pairs={{0,2},{1,3},{2,0},{3,1},{4,6},{5,7},{6,4},{7,5},{8,10},{9,11},{10,... | collective-permute-start | bytes 1572872 | tf_op jit(solution)/shard_map/ppermute | solution.py:412
  66.3 27.2 %collective-permute-start.7 = (bf16[3,64,2048]{2,1,0:T(8,128)(2,1)}, bf16[3,64,2048]{2,1,0:T(8,128)(2,1)S(1)}, u32[]{:S(2)}, u32[]{:S(2)}) collective-permute-start(bf16[3,64,2048]{2,1,0:T(8,128)(2,1)} %collective-permute-done.2.refs_5_), channel_id=1, source_target_pairs={{0,8},{8,16},{16,24},{24,28},{28,20},{20,12},{12,4},{4,0},{1,9},{9... | collective-permute-start | bytes 2359304 | tf_op jit(solution)/shard_map/ppermute | solution.py:368
  66.3 27.1 %collective-permute-start.8 = (bf16[3,64,2048]{2,1,0:T(8,128)(2,1)}, bf16[3,64,2048]{2,1,0:T(8,128)(2,1)S(1)}, u32[]{:S(2)}, u32[]{:S(2)}) collective-permute-start(bf16[3,64,2048]{2,1,0:T(8,128)(2,1)} %collective-permute-done.3.refs_2_), channel_id=1, source_target_pairs={{8,0},{16,8},{24,16},{28,24},{20,28},{12,20},{4,12},{0,4},{9,1},{1... | collective-permute-start | bytes 2359304 | tf_op jit(solution)/shard_map/ppermute | solution.py:368
  68.3 25.2 %collective-permute-start.9 = (bf16[192,1024]{1,0:T(8,128)(2,1)S(1)}, bf16[192,1024]{1,0:T(8,128)(2,1)S(1)}, u32[]{:S(2)}, u32[]{:S(2)}) collective-permute-start(bf16[192,1024]{1,0:T(8,128)(2,1)S(1)} %get-tuple-element.80), channel_id=1, source_target_pairs={{0,8},{8,16},{16,24},{24,28},{28,20},{20,12},{12,4},{4,0},{1,9},{9... | collective-permute-start | bytes 1179656 | tf_op jit(solution)/shard_map/ppermute | solution.py:368
  68.4 25.1 %collective-permute-start.10 = (bf16[192,1024]{1,0:T(8,128)(2,1)S(1)}, bf16[192,1024]{1,0:T(8,128)(2,1)S(1)}, u32[]{:S(2)}, u32[]{:S(2)}) collective-permute-start(bf16[192,1024]{1,0:T(8,128)(2,1)S(1)} %get-tuple-element.81), channel_id=1, source_target_pairs={{8,0},{16,8},{24,16},{28,24},{20,28},{12,20},{4,12},{0,4},{9,1},{1... | collective-permute-start | bytes 1179656 | tf_op jit(solution)/shard_map/ppermute | solution.py:368
  93.8 27.3 %collective-permute-start.15 = (bf16[192,2048]{1,0:T(8,128)(2,1)S(1)}, bf16[192,2048]{1,0:T(8,128)(2,1)S(1)}, u32[]{:S(2)}, u32[]{:S(2)}) collective-permute-start(bf16[192,2048]{1,0:T(8,128)(2,1)S(1)} %get-tuple-element.117), channel_id=1, source_target_pairs={{8,0},{16,8},{24,16},{28,24},{20,28},{12,20},{4,12},{0,4},{9,1},{1... | collective-permute-start | bytes 2359304 | tf_op jit(solution)/shard_map/ppermute | solution.py:368
  95.6 25.5 %collective-permute-start.14 = (bf16[192,2048]{1,0:T(8,128)(2,1)S(1)}, bf16[192,2048]{1,0:T(8,128)(2,1)S(1)}, u32[]{:S(2)}, u32[]{:S(2)}) collective-permute-start(bf16[192,2048]{1,0:T(8,128)(2,1)S(1)} %get-tuple-element.118), channel_id=1, source_target_pairs={{0,8},{8,16},{16,24},{24,28},{28,20},{20,12},{12,4},{4,0},{1,9},{9... | collective-permute-start | bytes 2359304 | tf_op jit(solution)/shard_map/ppermute | solution.py:368
  95.9 11.6 %collective-permute-start.16 = (bf16[1024,256]{1,0:T(8,128)(2,1)S(1)}, bf16[1024,256]{1,0:T(8,128)(2,1)}, u32[]{:S(2)}, u32[]{:S(2)}) collective-permute-start(bf16[1024,256]{1,0:T(8,128)(2,1)S(1)} %copy-done), channel_id=1, source_target_pairs={{0,2},{1,3},{2,0},{3,1},{4,6},{5,7},{6,4},{7,5},{8,10},{9,11},{10,... | collective-permute-start | bytes 1572872 | tf_op jit(solution)/shard_map/ppermute | solution.py:419
  96.5 23.4 %collective-permute-start.13 = (bf16[3,64,1024]{2,1,0:T(8,128)(2,1)S(1)}, bf16[3,64,1024]{2,1,0:T(8,128)(2,1)S(1)}, u32[]{:S(2)}, u32[]{:S(2)}) collective-permute-start(bf16[3,64,1024]{2,1,0:T(8,128)(2,1)S(1)} %slice.50), channel_id=1, source_target_pairs={{8,0},{16,8},{24,16},{28,24},{20,28},{12,20},{4,12},{0,4},{9,1},{1... | collective-permute-start | bytes 1179656 | tf_op jit(solution)/shard_map/ppermute | solution.py:368
  98.3 22.8 %collective-permute-start.12 = (bf16[3,64,1024]{2,1,0:T(8,128)(2,1)S(1)}, bf16[3,64,1024]{2,1,0:T(8,128)(2,1)S(1)}, u32[]{:S(2)}, u32[]{:S(2)}) collective-permute-start(bf16[3,64,1024]{2,1,0:T(8,128)(2,1)S(1)} %slice.49), channel_id=1, source_target_pairs={{0,8},{8,16},{16,24},{24,28},{28,20},{20,12},{12,4},{4,0},{1,9},{9... | collective-permute-start | bytes 1179656 | tf_op jit(solution)/shard_map/ppermute | solution.py:368
  121.7 18.6 %collective-permute-start.18 = (bf16[192,2048]{1,0:T(8,128)(2,1)S(1)}, bf16[192,2048]{1,0:T(8,128)(2,1)S(1)}, u32[]{:S(2)}, u32[]{:S(2)}) collective-permute-start(bf16[192,2048]{1,0:T(8,128)(2,1)S(1)} %get-tuple-element.115), channel_id=1, source_target_pairs={{8,0},{16,8},{24,16},{28,24},{20,28},{12,20},{4,12},{0,4},{9,1},{1... | collective-permute-start | bytes 2359304 | tf_op jit(solution)/shard_map/ppermute | solution.py:368
  122.2 18.1 %collective-permute-start.17 = (bf16[192,2048]{1,0:T(8,128)(2,1)S(1)}, bf16[192,2048]{1,0:T(8,128)(2,1)S(1)}, u32[]{:S(2)}, u32[]{:S(2)}) collective-permute-start(bf16[192,2048]{1,0:T(8,128)(2,1)S(1)} %get-tuple-element.116), channel_id=1, source_target_pairs={{0,8},{8,16},{16,24},{24,28},{28,20},{20,12},{12,4},{4,0},{1,9},{9... | collective-permute-start | bytes 2359304 | tf_op jit(solution)/shard_map/ppermute | solution.py:368
  131.9 8.4 %collective-permute-start.20 = (f32[512,128]{1,0:T(8,128)S(1)}, f32[512,128]{1,0:T(8,128)S(1)}, u32[]{:S(2)}, u32[]{:S(2)}) collective-permute-start(f32[512,128]{1,0:T(8,128)S(1)} %add.53.a_ref), channel_id=1, source_target_pairs={{0,2},{1,3},{2,0},{3,1},{4,6},{5,7},{6,4},{7,5},{8,10},{9,11},{10,... | collective-permute-start | bytes 786440 | tf_op jit(solution)/shard_map/ppermute | solution.py:342
  142.1 24.0 %collective-permute-start.24 = (bf16[192,2048]{1,0:T(8,128)(2,1)}, bf16[192,2048]{1,0:T(8,128)(2,1)}, u32[]{:S(2)}, u32[]{:S(2)}) collective-permute-start(bf16[192,2048]{1,0:T(8,128)(2,1)} %get-tuple-element.113), channel_id=1, source_target_pairs={{8,0},{16,8},{24,16},{28,24},{20,28},{12,20},{4,12},{0,4},{9,1},{1... | collective-permute-start | bytes 2359304 | tf_op jit(solution)/shard_map/ppermute | solution.py:368
  142.3 23.7 %collective-permute-start.23 = (bf16[192,2048]{1,0:T(8,128)(2,1)}, bf16[192,2048]{1,0:T(8,128)(2,1)}, u32[]{:S(2)}, u32[]{:S(2)}) collective-permute-start(bf16[192,2048]{1,0:T(8,128)(2,1)} %get-tuple-element.114), channel_id=1, source_target_pairs={{0,8},{8,16},{16,24},{24,28},{28,20},{20,12},{12,4},{4,0},{1,9},{9... | collective-permute-start | bytes 2359304 | tf_op jit(solution)/shard_map/ppermute | solution.py:368
  144.1 10.6 %collective-permute-start.21 = (bf16[1024,256]{1,0:T(8,128)(2,1)S(1)}, bf16[1024,256]{1,0:T(8,128)(2,1)}, u32[]{:S(2)}, u32[]{:S(2)}) collective-permute-start(bf16[1024,256]{1,0:T(8,128)(2,1)S(1)} %copy-done), channel_id=1, source_target_pairs={{0,1},{1,0},{2,3},{3,2},{4,5},{5,4},{6,7},{7,6},{8,9},{9,8},{10,11... | collective-permute-start | bytes 1572872 | tf_op jit(solution)/shard_map/ppermute | solution.py:451
  144.1 10.6 %collective-permute-start.22 = (bf16[1024,256]{1,0:T(8,128)(2,1)}, bf16[1024,256]{1,0:T(8,128)(2,1)}, u32[]{:S(2)}, u32[]{:S(2)}) collective-permute-start(bf16[1024,256]{1,0:T(8,128)(2,1)} %collective-permute-done.16.refs_2_), channel_id=1, source_target_pairs={{0,1},{1,0},{2,3},{3,2},{4,5},{5,4},{6,7},{7,6},{8,9},{9,8},{10,11... | collective-permute-start | bytes 1572872 | tf_op jit(solution)/shard_map/ppermute | solution.py:451
  147.8 30.2 %all-to-all-start.1 = ((bf16[24,64,256]{2,1,0:T(8,128)(2,1)}), bf16[24,64,256]{2,1,0:T(8,128)(2,1)}, u32[]{:S(2)}, u32[]{:S(2)}) async-start(bf16[24,64,256]{2,1,0:T(8,128)(2,1)} %bitcast.15), calls=%async_computation.1 | async-start | bytes 1572864 | tf_op jit(solution)/shard_map/all_to_all | solution.py:454
  (22 other events, 234.4 us)
